TPU v7x, 32 devices: a whole 2x2x4 slice. The times are simulated.
32 devices in a mesh: fsdp: 4 (over y, x), tensor: 8 (over z, core).
Axes of the slice: x: 2, y: 2, z: 4, core: 2. Of those that a mesh axis runs over, the one named last changes fastest.
Arguments:
- inputs: bfloat16 [16, 729, 1152], P('fsdp'), may hold values from -6 to 6
- cotangent: bfloat16 [16, 729, 1152], P('fsdp'), may hold values from -6 to 6
- qkv_proj: bfloat16 [1152, 16, 216], P('fsdp', 'tensor'), may hold values from -0.1875 to 0.1875
- qv_bias: bfloat16 [16, 144], P('tensor'), may hold values from -3 to 3
- out_proj: bfloat16 [16, 72, 1152], P('tensor', None, 'fsdp'), may hold values from -3 to 3
- out_bias: bfloat16 [1152], P('fsdp'), may hold values from -3 to 3
- gain_one: bfloat16 [1152], P('fsdp'), may hold values from 0.099609375 to 1.8984375
- shift_one: bfloat16 [1152], P('fsdp'), may hold values from -3 to 3
- gain_two: bfloat16 [1152], P('fsdp'), may hold values from 0.099609375 to 1.8984375
- shift_two: bfloat16 [1152], P('fsdp'), may hold values from -3 to 3
- up_proj: bfloat16 [1152, 4304], P('fsdp', 'tensor'), may hold values from -0.1875 to 0.1875
- up_bias: bfloat16 [4304], P('tensor'), may hold values from -3 to 3
- down_proj: bfloat16 [4304, 1152], P('tensor', 'fsdp'), may hold values from -0.09375 to 0.09375
- down_bias: bfloat16 [1152], P('fsdp'), may hold values from -3 to 3
Outputs:
- layer_out: bfloat16 [16, 729, 1152], P('fsdp', None, 'tensor')
- input_gradient: float32 [16, 729, 1152], P('fsdp', None, 'tensor')
- qkv_grad: float32 [1152, 16, 216], P('fsdp', 'tensor')
- qvbias_grad: float32 [16, 144], P('tensor')
- outproj_grad: float32 [16, 72, 1152], P('tensor', None, 'fsdp')
- outbias_grad: float32 [1152], P('fsdp')
- gainone_grad: float32 [1152], P('fsdp')
- shiftone_grad: float32 [1152], P('fsdp')
- gaintwo_grad: float32 [1152], P('fsdp')
- shifttwo_grad: float32 [1152], P('fsdp')
- upproj_grad: float32 [1152, 4304], P('fsdp', 'tensor')
- upbias_grad: float32 [4304], P('tensor')
- downproj_grad: float32 [4304, 1152], P('tensor', 'fsdp')
- downbias_grad: float32 [1152], P('fsdp')
All inputs are finite; a program needn't handle non-finite values.
Results may differ from a plain program's by a relative error of at most 0.024.
Values may be sent and summed in bfloat16 or wider, within the bound.
No kernel may reach another device: no remote copies, remote signals or barrier semaphores. Data moves between devices by JAX's collectives and lax.ppermute only.
A program may use at most 192 MiB of HBM per device.

v0:
```python
import jax
import jax.numpy as jnp
from jax import lax
from jax.sharding import PartitionSpec as P

MODEL_WIDTH = 1152
HD = 72


norm_eps = 1e-06


def row_sums(row_pair):
    return lax.psum((row_pair[0], row_pair[1]), "tensor")


def share_sum(partial_rows):
    return lax.psum_scatter(
        partial_rows.astype(jnp.bfloat16), "tensor", scatter_dimension=2, tiled=True
    ).astype(jnp.float32)


def share_gather(share_rows):
    return lax.all_gather(share_rows, "tensor", axis=2, tiled=True)


def feature_portion(full_rows):
    share_width = MODEL_WIDTH // lax.axis_size("tensor")
    return lax.dynamic_slice_in_dim(
        full_rows, lax.axis_index("tensor") * share_width, share_width, full_rows.ndim - 1
    )


def standardize_rows(row_data, spread):
    row_total_values = (
        jnp.sum(row_data, axis=-1, keepdims=True),
        jnp.sum(row_data * row_data, axis=-1, keepdims=True),
    )
    if spread:
        row_total_values = row_sums(row_total_values)
    row_mean = row_total_values[0] / MODEL_WIDTH
    row_var = row_total_values[1] / MODEL_WIDTH - row_mean * row_mean
    inverse_scale = lax.rsqrt(row_var + norm_eps)
    return ((row_data - row_mean) * inverse_scale, inverse_scale)


def norm_backward_pass(gradient_rows, centered_normed, inverse_scale, gain_vector):
    scaled_rows = gradient_rows * gain_vector
    row_total_values = (
        jnp.sum(scaled_rows, axis=-1, keepdims=True),
        jnp.sum(scaled_rows * centered_normed, axis=-1, keepdims=True),
    )
    row_total_values = row_sums(row_total_values)
    return inverse_scale * (
        scaled_rows
        - row_total_values[0] / MODEL_WIDTH
        - centered_normed * (row_total_values[1] / MODEL_WIDTH)
    )


def gelu_tanh(values_in):
    return jax.nn.gelu(values_in, approximate=True)


def score_block(queries, keys_rows):
    return jnp.einsum(
        "bqhe,bkhe->bhqk", queries, keys_rows, preferred_element_type=jnp.float32
    ) * HD ** (-0.5)


def body(
    inputs,
    cotangent,
    qkv_proj,
    qv_bias,
    out_proj,
    out_bias,
    gain_one,
    shift_one,
    gain_two,
    shift_two,
    up_proj,
    up_bias,
    down_proj,
    down_bias,
):
    (
        qkv_full,
        out_full,
        up_full,
        down_full,
        outb_full,
        first_norm_gain,
        first_norm_shift,
        second_norm_gain,
        second_norm_shift,
        downb_full,
    ) = (
        lax.all_gather(qkv_proj, "fsdp", axis=0, tiled=True),
        lax.all_gather(out_proj, "fsdp", axis=2, tiled=True),
        lax.all_gather(up_proj, "fsdp", axis=0, tiled=True),
        lax.all_gather(down_proj, "fsdp", axis=1, tiled=True),
        lax.all_gather(out_bias, "fsdp", axis=0, tiled=True),
        lax.all_gather(gain_one, "fsdp", axis=0, tiled=True),
        lax.all_gather(shift_one, "fsdp", axis=0, tiled=True),
        lax.all_gather(gain_two, "fsdp", axis=0, tiled=True),
        lax.all_gather(shift_two, "fsdp", axis=0, tiled=True),
        lax.all_gather(down_bias, "fsdp", axis=0, tiled=True),
    )
    input_floats = inputs.astype(jnp.float32)
    first_centered_normed, first_inverse_std = standardize_rows(input_floats, False)
    first_normed_rows = (first_centered_normed * first_norm_gain + first_norm_shift).astype(
        jnp.bfloat16
    )
    triple = jnp.einsum(
        "bsd,dhe->bshe", first_normed_rows, qkv_full, preferred_element_type=jnp.float32
    )
    queries = (triple[..., :HD] + qv_bias[:, :HD]).astype(jnp.bfloat16)
    keys_rows = triple[..., HD : 2 * HD].astype(jnp.bfloat16)
    value_rows = (triple[..., 2 * HD :] + qv_bias[:, HD:]).astype(jnp.bfloat16)
    scores = score_block(queries, keys_rows)
    row_max = jnp.max(scores, axis=-1, keepdims=True)
    exp_scores = jnp.exp(scores - row_max)
    exp_total = jnp.sum(exp_scores, axis=-1, keepdims=True)
    log_total = row_max + jnp.log(exp_total)
    context = jnp.einsum(
        "bhqk,bkhe->bqhe",
        (exp_scores / exp_total).astype(jnp.bfloat16),
        value_rows,
        preferred_element_type=jnp.float32,
    ).astype(jnp.bfloat16)
    attn_part = jnp.einsum("bshe,hed->bsd", context, out_full, preferred_element_type=jnp.float32)
    middle_residual = (
        feature_portion(input_floats) + share_sum(attn_part) + feature_portion(outb_full)
    )
    second_centered_normed, second_inverse_std = standardize_rows(middle_residual, True)
    normed_two = share_gather(
        (
            second_centered_normed * feature_portion(second_norm_gain)
            + feature_portion(second_norm_shift)
        ).astype(jnp.bfloat16)
    )
    pre_act = (
        jnp.einsum("bsd,df->bsf", normed_two, up_full, preferred_element_type=jnp.float32) + up_bias
    )
    hidden = gelu_tanh(pre_act).astype(jnp.bfloat16)
    mlp_part = jnp.einsum("bsf,fd->bsd", hidden, down_full, preferred_element_type=jnp.float32)
    layer_out = (middle_residual + share_sum(mlp_part) + feature_portion(downb_full)).astype(
        jnp.bfloat16
    )
    grad_out = cotangent.astype(jnp.float32)
    downbias_g = jnp.sum(grad_out, axis=(0, 1))
    downproj_g = jnp.einsum("bsf,bsd->fd", hidden, cotangent, preferred_element_type=jnp.float32)
    hidden_grad = jnp.einsum(
        "bsd,fd->bsf", cotangent, down_full, preferred_element_type=jnp.float32
    )
    unused_out, gelu_pull = jax.vjp(gelu_tanh, pre_act)
    pre_grad = gelu_pull(hidden_grad)[0].astype(jnp.bfloat16)
    upbias_g = jnp.sum(pre_grad.astype(jnp.float32), axis=(0, 1))
    upproj_g = jnp.einsum("bsd,bsf->df", normed_two, pre_grad, preferred_element_type=jnp.float32)
    normed_two_part = jnp.einsum(
        "bsf,df->bsd", pre_grad, up_full, preferred_element_type=jnp.float32
    )
    second_portion = share_sum(normed_two_part)
    second_gain_gradient = jnp.sum(second_portion * second_centered_normed, axis=(0, 1))
    shift_second_g = jnp.sum(second_portion, axis=(0, 1))
    middle_gradient = feature_portion(grad_out) + norm_backward_pass(
        second_portion,
        second_centered_normed,
        second_inverse_std,
        feature_portion(second_norm_gain),
    )
    branch_grad = share_gather(middle_gradient.astype(jnp.bfloat16))
    outbias_g = jnp.sum(middle_gradient, axis=(0, 1))
    outproj_g = jnp.einsum(
        "bshe,bsd->hed", context, branch_grad, preferred_element_type=jnp.float32
    )
    context_grad = jnp.einsum(
        "bsd,hed->bshe", branch_grad, out_full, preferred_element_type=jnp.float32
    ).astype(jnp.bfloat16)
    soft_probs = jnp.exp(score_block(queries, keys_rows) - log_total)
    value_grad = jnp.einsum(
        "bhqk,bqhe->bkhe",
        soft_probs.astype(jnp.bfloat16),
        context_grad,
        preferred_element_type=jnp.float32,
    ).astype(jnp.bfloat16)
    prob_grad = jnp.einsum(
        "bqhe,bkhe->bhqk", context_grad, value_rows, preferred_element_type=jnp.float32
    )
    score_grad = (
        soft_probs * (prob_grad - jnp.sum(prob_grad * soft_probs, axis=-1, keepdims=True))
    ).astype(jnp.bfloat16)
    query_grad = (
        jnp.einsum("bhqk,bkhe->bqhe", score_grad, keys_rows, preferred_element_type=jnp.float32)
        * HD ** (-0.5)
    ).astype(jnp.bfloat16)
    keys_grad = (
        jnp.einsum("bhqk,bqhe->bkhe", score_grad, queries, preferred_element_type=jnp.float32)
        * HD ** (-0.5)
    ).astype(jnp.bfloat16)
    triple_grad = jnp.concatenate([query_grad, keys_grad, value_grad], axis=-1)
    qvbias_g = jnp.concatenate(
        [
            jnp.sum(query_grad.astype(jnp.float32), axis=(0, 1)),
            jnp.sum(value_grad.astype(jnp.float32), axis=(0, 1)),
        ],
        axis=-1,
    )
    qkvproj_g = jnp.einsum(
        "bsd,bshe->dhe", first_normed_rows, triple_grad, preferred_element_type=jnp.float32
    )
    normed_one_part = jnp.einsum(
        "bshe,dhe->bsd", triple_grad, qkv_full, preferred_element_type=jnp.float32
    )
    first_portion = share_sum(normed_one_part)
    centered_portion = feature_portion(first_centered_normed)
    first_gain_gradient = jnp.sum(first_portion * centered_portion, axis=(0, 1))
    shift_first_g = jnp.sum(first_portion, axis=(0, 1))
    input_gradient = middle_gradient + norm_backward_pass(
        first_portion, centered_portion, first_inverse_std, feature_portion(first_norm_gain)
    )
    share_width = MODEL_WIDTH // lax.axis_size("tensor")
    share_vectors = jnp.stack(
        [first_gain_gradient, shift_first_g, second_gain_gradient, shift_second_g, outbias_g]
    )
    placed = lax.dynamic_update_slice_in_dim(
        jnp.zeros((5, MODEL_WIDTH), jnp.float32),
        share_vectors,
        lax.axis_index("tensor") * share_width,
        1,
    )
    summed_vectors = lax.psum(placed, "tensor")
    vectors = jnp.concatenate([summed_vectors, downbias_g[None, :]], axis=0)
    qkv_grad, outproj_grad, upproj_grad, downproj_grad, vector_grads = (
        lax.psum_scatter(
            qkvproj_g.astype(jnp.bfloat16), "fsdp", scatter_dimension=0, tiled=True
        ).astype(jnp.float32),
        lax.psum_scatter(
            outproj_g.astype(jnp.bfloat16), "fsdp", scatter_dimension=2, tiled=True
        ).astype(jnp.float32),
        lax.psum_scatter(
            upproj_g.astype(jnp.bfloat16), "fsdp", scatter_dimension=0, tiled=True
        ).astype(jnp.float32),
        lax.psum_scatter(
            downproj_g.astype(jnp.bfloat16), "fsdp", scatter_dimension=1, tiled=True
        ).astype(jnp.float32),
        lax.psum_scatter(
            vectors.astype(jnp.bfloat16), "fsdp", scatter_dimension=1, tiled=True
        ).astype(jnp.float32),
    )
    qvbias_grad, upbias_grad = lax.psum((qvbias_g, upbias_g), "fsdp")
    return (
        layer_out,
        input_gradient,
        qkv_grad,
        qvbias_grad,
        outproj_grad,
        vector_grads[4],
        vector_grads[0],
        vector_grads[1],
        vector_grads[2],
        vector_grads[3],
        upproj_grad,
        upbias_grad,
        downproj_grad,
        vector_grads[5],
    )


def solution(mesh):
    return jax.shard_map(
        body,
        mesh=mesh,
        in_specs=(
            P("fsdp", None, None),
            P("fsdp", None, None),
            P("fsdp", "tensor", None),
            P("tensor", None),
            P("tensor", None, "fsdp"),
            P("fsdp"),
            P("fsdp"),
            P("fsdp"),
            P("fsdp"),
            P("fsdp"),
            P("fsdp", "tensor"),
            P("tensor"),
            P("tensor", "fsdp"),
            P("fsdp"),
        ),
        out_specs=(
            P("fsdp", None, "tensor"),
            P("fsdp", None, "tensor"),
            P("fsdp", "tensor", None),
            P("tensor", None),
            P("tensor", None, "fsdp"),
            P("fsdp"),
            P("fsdp"),
            P("fsdp"),
            P("fsdp"),
            P("fsdp"),
            P("fsdp", "tensor"),
            P("tensor"),
            P("tensor", "fsdp"),
            P("fsdp"),
        ),
        check_vma=False,
    )
```

profile of v0, /device:TPU:0, one launch (start us, length us, event | category | flops | bytes accessed | tf_op | source)
XLA Modules:
  0.0 843.7 jit_solution(4436794610986860137)
XLA Ops:
  16.0 17.7 %all-reduce.10 = (bf16[1152]{0:T(1024)(128)(2,1)S(1)}, bf16[1152]{0:T(1024)(128)(2,1)S(1)}, bf16[1152]{0:T(1024)(128)(2,1)S(1)}, bf16[1152]{0:T(1024)(128)(2,1)S...) all-reduce(bf16[1152]{0:T(1024)(128)(2,1)S(1)} %dynamic-update-slic, ...), channel_id=1, replica_groups=mesh['fsdp'=4,'tensor'=8] {'fsdp'}, use_global_device_ids=true, to_apply=%add.1 | all-reduce | flops 6912 | bytes 27648
  35.8 10.7 %all_gather.39 = bf16[2,72,1152]{1,0,2:T(2,128)(2,1)S(1)} all-gather(bf16[2,72,288]{1,0,2:T(2,128)(2,1)S(1)} %copy.46), channel_id=1, replica_groups=mesh['fsdp'=4,'tensor'=8] {'fsdp'}, dimensions={2}, use_global_device_ids=true | all-gather | bytes 414720 | tf_op jit(solution)/shard_map/all_gather | solution.py:100
  47.1 12.8 %all_gather.38 = bf16[1152,2,216]{2,0,1:T(8,128)(2,1)S(1)} all-gather(bf16[288,2,216]{2,0,1:T(8,128)(2,1)S(1)} %copy.43), channel_id=1, replica_groups=mesh['fsdp'=4,'tensor'=8] {'fsdp'}, dimensions={0}, use_global_device_ids=true | all-gather | bytes 1244160 | tf_op jit(solution)/shard_map/all_gather | solution.py:99
  59.9 13.1 %copy.42 = bf16[4,729,1152]{1,2,0:T(8,128)(2,1)} copy(bf16[4,729,1152]{2,0,1:T(4,128)(2,1)} %param.14) | data formatting | bytes 13436928 | tf_op args[0]
  90.9 9.2 %fusion = f32[4,2,729]{2,1,0:T(2,128)S(1)} fusion(f32[4,2,729,729]{2,3,1,0:T(8,128)} %get-tuple-element.86, f32[4,2,729]{2,1,0:T(2,128)S(1)} %get-tuple-element.85), kind=kLoop, calls=%fused_computation.5 | loop fusion | flops 12748752 | bytes 17052768 | tf_op jit(solution)/shard_map/reduce_sum | solution.py:124
  100.1 9.0 %fusion.61 = bf16[4,729,2,72]{1,3,2,0:T(8,128)(2,1)S(1)} fusion(f32[4,2,729,729]{2,3,1,0:T(8,128)} %get-tuple-element.86, f32[4,2,729]{2,1,0:T(2,128)S(1)} %fusion, f32[4,2,729]{2,1,0:T(2,128)S(1)} %get-tuple-element.85, f32[4,729,2,216]{1,3,2,0:T(8,128)} %copy-done.2, f32[2,72]{1,0:T(2,128)S(1)} %get-tuple-element.83), kind=kOutput, calls=%fused_computation.90 | convolution fusion | flops 630485824 | bytes 20744448 | tf_op jit(solution)/shard_map/bhqk,bkhe->bqhe/dot_general | solution.py:126
  115.8 10.0 %convert_element_type.159 = f32[4,729,1152]{1,2,0:T(8,128)} convert(bf16[4,729,1152]{1,2,0:T(8,128)(2,1)} %copy.42) | non-fusion elementwise | flops 3359232 | bytes 20155392 | tf_op jit(solution)/shard_map/convert_element_type | solution.py:110
  125.9 66.9 %reduce-scatter.14.cloned.1.call-done = bf16[4,729,144]{1,2,0:T(8,128)(2,1)} async-done(((bf16[4,729,1152]{1,2,0:T(8,128)(2,1)}), bf16[4,729,144]{1,2,0:T(8,128)(2,1)}) %reduce-scatter.14.cloned.1.call-update) | async-done | bytes 839824 | tf_op jit(solution)/shard_map/reduce_scatter | solution.py:18
  195.0 26.0 %all-reduce.8 = (f32[4,729,1]{1,0,2:T(4,128)S(1)}, f32[4,729,1]{1,0,2:T(4,128)S(1)}) all-reduce(f32[4,729,1]{1,0,2:T(4,128)S(1)} %bitcast.137, f32[4,729,1]{1,0,2:T(4,128)S(1)} %bitcast.136), channel_id=1, replica_groups=mesh['fsdp'=4,'tensor'=8] {'tensor'}, use_global_device_ids=true, to_apply=%region_8.0 | all-reduce | flops 5832 | bytes 46656 | tf_op jit(solution)/shard_map/psum | solution.py:14
  223.0 13.2 %copy.48 = bf16[4,729,1152]{1,2,0:T(8,128)(2,1)} copy(bf16[4,729,1152]{2,0,1:T(4,128)(2,1)} %param.15) | data formatting | bytes 13436928 | tf_op args[1]
  236.3 55.4 %all-gather.5.cloned.1.call-done = bf16[4,729,1152]{1,2,0:T(8,128)(2,1)} async-done(((bf16[4,729,144]{1,2,0:T(8,128)(2,1)}), bf16[4,729,1152]{1,2,0:T(8,128)(2,1)}) %all-gather.5.cloned.1.call-update) | async-done | bytes 6718480 | tf_op jit(solution)/shard_map/all_gather | solution.py:24
  291.7 10.8 %fusion.52 = f32[4,729,538]{1,2,0:T(8,128)} fusion(bf16[4,729,1152]{1,2,0:T(8,128)(2,1)} %all-gather.5.cloned.1.call-done, bf16[1152,538]{1,0:T(8,128)(2,1)} %all-gather.7.cloned.1.call-done), kind=kOutput, calls=%fused_computation.85 | convolution fusion | flops 3614533632 | bytes 14233248 | tf_op jit(solution)/shard_map/bsd,df->bsf/dot_general | solution.py:144
  302.5 19.5 %all-gather.9.cloned.1.call-done = bf16[538,1152]{0,1:T(8,128)(2,1)} async-done(((bf16[538,288]{0,1:T(8,128)(2,1)}), bf16[538,1152]{0,1:T(8,128)(2,1)}) %all-gather.9.cloned.1.call-update) | async-done | bytes 1239568 | tf_op jit(solution)/shard_map/all_gather | solution.py:102
  322.0 13.5 %convert_reduce_fusion.1 = (f32[538]{0:T(1024)}, bf16[4,729,538]{1,2,0:T(8,128)(2,1)S(1)}) fusion(f32[4,729,538]{1,2,0:T(8,128)} %fusion.52, f32[538]{0:T(1024)S(1)} %convert_element_type.176, bf16[4,729,1152]{1,2,0:T(8,128)(2,1)} %copy.48, bf16[538,1152]{0,1:T(8,128)(2,1)} %all-gather.9.cloned.1.call-done), kind=kOutput, calls=%fused_computation.34 | convolution fusion | flops 3650614784 | bytes 17375168 | tf_op jit(solution)/shard_map/bsd,fd->bsf/dot_general | solution.py:154
  345.3 11.1 %convolution_convert_fusion.1 = bf16[4,729,1152]{1,2,0:T(8,128)(2,1)} fusion(bf16[538,1152]{0,1:T(8,128)(2,1)} %all-gather.9.cloned.1.call-done, f32[4,729,538]{1,2,0:T(8,128)} %fusion.52, f32[538]{0:T(1024)S(1)} %convert_element_type.176), kind=kOutput, calls=%fused_computation.26 | convolution fusion | flops 3633581056 | bytes 14235400 | tf_op jit(solution)/shard_map/bsf,fd->bsd/dot_general | solution.py:147
  357.1 65.5 %reduce-scatter.18.cloned.1.call-done = bf16[4,729,144]{1,2,0:T(8,128)(2,1)} async-done(((bf16[4,729,1152]{1,2,0:T(8,128)(2,1)}), bf16[4,729,144]{1,2,0:T(8,128)(2,1)}) %reduce-scatter.18.cloned.1.call-update) | async-done | bytes 839824 | tf_op jit(solution)/shard_map/reduce_scatter | solution.py:18
  425.6 27.2 %all-reduce.7 = (f32[4,729,1]{1,0,2:T(4,128)S(1)}, f32[4,729,1]{1,0,2:T(4,128)S(1)}) all-reduce(f32[4,729,1]{1,0,2:T(4,128)S(1)} %bitcast.132, f32[4,729,1]{1,0,2:T(4,128)S(1)} %bitcast.133), channel_id=1, replica_groups=mesh['fsdp'=4,'tensor'=8] {'tensor'}, use_global_device_ids=true, to_apply=%region_14.0 | all-reduce | flops 5832 | bytes 46656 | tf_op jit(solution)/shard_map/psum | solution.py:14
  454.1 47.0 %reduce-scatter.16.cloned.1.call-done = bf16[4,729,144]{1,2,0:T(8,128)(2,1)} async-done(((bf16[4,729,1152]{1,2,0:T(8,128)(2,1)}), bf16[4,729,144]{1,2,0:T(8,128)(2,1)}) %reduce-scatter.16.cloned.1.call-update) | async-done | bytes 839824 | tf_op jit(solution)/shard_map/reduce_scatter | solution.py:18
  506.5 11.7 %fusion.20 = bf16[538,1152]{0,1:T(8,128)(2,1)} fusion(bf16[4,729,1152]{1,2,0:T(8,128)(2,1)} %copy.48, f32[4,729,538]{1,2,0:T(8,128)} %fusion.52, f32[538]{0:T(1024)} %copy-done.31), kind=kOutput, calls=%fused_computation.40 | convolution fusion | flops 3630841600 | bytes 14235400 | tf_op jit(solution)/shard_map/bsf,bsd->fd/dot_general | solution.py:153
  518.4 9.9 %fusion.19 = bf16[1152,538]{1,0:T(8,128)(2,1)} fusion(bf16[4,729,1152]{1,2,0:T(8,128)(2,1)} %all-gather.5.cloned.1.call-done, bf16[4,729,538]{1,2,0:T(8,128)(2,1)} %copy-done.34), kind=kOutput, calls=%fused_computation.39 | convolution fusion | flops 3615153408 | bytes 11095632 | tf_op jit(solution)/shard_map/bsd,bsf->df/dot_general | solution.py:160
  528.3 47.5 %all-gather.11.cloned.1.call-done = bf16[4,729,1152]{1,2,0:T(8,128)(2,1)} async-done(((bf16[4,729,144]{1,2,0:T(8,128)(2,1)}), bf16[4,729,1152]{1,2,0:T(8,128)(2,1)}) %all-gather.11.cloned.1.call-update) | async-done | bytes 6718480 | tf_op jit(solution)/shard_map/all_gather | solution.py:24
  580.2 13.4 %multiply_reduce_fusion = (f32[4,2,729]{2,1,0:T(2,128)S(1)}, f32[4,2,729,729]{2,3,1,0:T(8,128)}) fusion(f32[4,2,729,729]{2,3,1,0:T(8,128)} %get-tuple-element.86, f32[4,2,729]{2,1,0:T(2,128)S(1)} %bitcast.126, bf16[4,729,2,72]{1,3,2,0:T(8,128)(2,1)S(1)} %fusion.58, f32[4,729,2,216]{1,3,2,0:T(8,128)} %copy-done.2, f32[2,72]{1,0:T(2,128)S(1)} %get-tuple-element.83), kind=kOutput, calls=%fused_computation.1 | convolution fusion | flops 630060096 | bytes 37750560 | tf_op jit(solution)/shard_map/bqhe,bkhe->bhqk/dot_general | solution.py:188
  593.7 17.1 %multiply_convert_fusion = bf16[4,2,729,729]{2,3,1,0:T(8,128)(2,1)} fusion(f32[4,2,729,729]{2,3,1,0:T(8,128)} %get-tuple-element.88, f32[4,2,729,729]{2,3,1,0:T(8,128)} %get-tuple-element.86, f32[4,2,729]{2,1,0:T(2,128)S(1)} %get-tuple-element.87, f32[4,2,729]{2,1,0:T(2,128)S(1)} %bitcast.127), kind=kLoop, calls=%fused_computation | loop fusion | flops 21257640 | bytes 42561936 | tf_op jit(solution)/shard_map/convert_element_type | solution.py:193
  628.2 9.6 %convert_reduce_fusion.4 = (f32[2,72]{1,0:T(2,128)}, bf16[4,729,2,72]{1,3,2,0:T(8,128)(2,1)}) fusion(bf16[4,729,2,72]{1,3,2,0:T(8,128)(2,1)S(1)} %fusion.58, f32[4,2,729,729]{2,3,1,0:T(8,128)} %get-tuple-element.86, f32[4,2,729]{2,1,0:T(2,128)S(1)} %bitcast.128), kind=kOutput, calls=%fused_computation.73 | convolution fusion | flops 626234176 | bytes 18709632 | tf_op jit(solution)/shard_map/bhqk,bqhe->bkhe/dot_general | solution.py:182
  638.4 8.6 %fusion.21 = bf16[1152,2,216]{2,0,1:T(8,128)(2,1)} fusion(f32[1152]{0:T(1024)} %copy-done.24, f32[1152]{0:T(1024)} %copy-done.23, f32[4,729]{1,0:T(4,128)S(1)} %copy-done.15, f32[4,729]{1,0:T(4,128)} %copy-done.18, bf16[4,729,1152]{1,2,0:T(8,128)(2,1)} %copy.42, bf16[4,729,2,72]{1,3,2,0:T(8,128)(2,1)} %get-tuple-element.90, ...), kind=kOutput, calls=%fused_computation.41 | convolution fusion | flops 2930587648 | bytes 10265760 | tf_op jit(solution)/shard_map/bsd,bshe->dhe/dot_general | solution.py:210
  647.1 8.2 bitcast_convert_fusion
  662.0 9.6 %subtract_multiply_fusion = f32[4,729,1152]{1,2,0:T(8,128)} fusion(bf16[4,729,1152]{1,2,0:T(8,128)(2,1)} %copy.42, f32[4,729]{1,0:T(4,128)S(1)} %copy-done.15, f32[4,729]{1,0:T(4,128)S(1)} %copy-done.19), kind=kLoop, calls=%fused_computation.11 | loop fusion | flops 10077696 | bytes 20178720 | tf_op jit(solution)/shard_map/mul | solution.py:44
  675.5 10.7 %all-reduce.9 = (f32[2,144]{1,0:T(2,128)}, f32[538]{0:T(1024)}) all-reduce(f32[2,144]{1,0:T(2,128)S(1)} %pad_maximum_fusion.4, f32[538]{0:T(1024)S(1)} %copy-done.30), channel_id=1, replica_groups=mesh['fsdp'=4,'tensor'=8] {'fsdp'}, use_global_device_ids=true, to_apply=%region_24.0 | all-reduce | flops 826 | bytes 6608 | tf_op jit(solution)/shard_map/psum | solution.py:252
  688.1 13.9 %reduce-scatter.22.cloned.1.call-done = bf16[288,2,216]{2,0,1:T(8,128)(2,1)} async-done(((bf16[1152,2,216]{2,0,1:T(8,128)(2,1)}), bf16[288,2,216]{2,0,1:T(8,128)(2,1)}) %reduce-scatter.22.cloned.1.call-update) | async-done | bytes 248848 | tf_op jit(solution)/shard_map/reduce_scatter | solution.py:236
  704.1 77.3 %reduce-scatter.20.cloned.1.call-done = bf16[4,729,144]{1,2,0:T(8,128)(2,1)} async-done(((bf16[4,729,1152]{1,2,0:T(8,128)(2,1)}), bf16[4,729,144]{1,2,0:T(8,128)(2,1)}) %reduce-scatter.20.cloned.1.call-update) | async-done | bytes 839824 | tf_op jit(solution)/shard_map/reduce_scatter | solution.py:18
  784.7 26.4 %all-reduce.6 = (f32[4,729,1]{1,0,2:T(4,128)S(1)}, f32[4,729,1]{1,0,2:T(4,128)S(1)}, bf16[5,1152]{1,0:T(8,128)(2,1)S(1)}) all-reduce(f32[4,729,1]{1,0,2:T(4,128)S(1)} %bitcast.134, f32[4,729,1]{1,0,2:T(4,128)S(1)} %bitcast.135, f32[5,1152]{1,0:T(8,128)S(1)} %dynamic_update_slice.3), channel_id=1, replica_groups=mesh['fsdp'=4,'tensor'=8] {'tensor'}, use_global_device_ids=true, to_apply=%region_20.0 | all-reduce | flops 11592 | bytes 81216 | tf_op jit(solution)/shard_map/psum | solution.py:14
  815.5 19.3 %reduce-scatter.30.cloned.1.call-done = bf16[288,6]{1,0:T(8,128)(2,1)} async-done(((bf16[1152,6]{1,0:T(8,128)(2,1)}), bf16[288,6]{1,0:T(8,128)(2,1)}) %reduce-scatter.30.cloned.1.call-update) | async-done | bytes 3472
  (171 shorter events, 104.9 us)
Async XLA Ops:
  8.0 184.8 %reduce-scatter.14.cloned.1.call-start = ((), (), s32[]{:S(2)}) async-start(), calls=%async_computation.9 | async-start | bytes 7962624 | tf_op jit(solution)/shard_map/reduce_scatter | solution.py:18
  8.9 74.2 %copy-start.20 = (f32[2,72]{1,0:T(2,128)}, f32[2,72]{1,0:T(2,128)S(1)}, u32[]{:S(2)}) copy-start(f32[2,72]{1,0:T(2,128)S(1)} %get-tuple-element.84) | copy-start | bytes 1732
  33.7 39.3 %copy-start.25 = (bf16[1152]{0:T(1024)(128)(2,1)}, bf16[1152]{0:T(1024)(128)(2,1)S(1)}, u32[]{:S(2)}) copy-start(bf16[1152]{0:T(1024)(128)(2,1)S(1)} %get-tuple-element.70) | copy-start | bytes 6916
  33.7 44.6 %copy-start.23 = (f32[1152]{0:T(1024)}, f32[1152]{0:T(1024)S(1)}, u32[]{:S(2)}) copy-start(f32[1152]{0:T(1024)S(1)} %convert_element_type.160) | copy-start | bytes 13828
  33.7 44.5 %copy-start.24 = (f32[1152]{0:T(1024)}, f32[1152]{0:T(1024)S(1)}, u32[]{:S(2)}) copy-start(f32[1152]{0:T(1024)S(1)} %convert_element_type.161) | copy-start | bytes 13828
  47.1 62.0 %copy-start.5 = (bf16[2,72,1152]{2,1,0:T(8,128)(2,1)}, bf16[2,72,1152]{2,1,0:T(8,128)(2,1)S(1)}, u32[]{:S(2)}) copy-start(bf16[2,72,1152]{2,1,0:T(8,128)(2,1)S(1)} %copy.47) | copy-start | bytes 995332
  59.9 18.4 %copy-start.7 = (bf16[1152,2,216]{2,0,1:T(8,128)(2,1)}, bf16[1152,2,216]{2,0,1:T(8,128)(2,1)S(1)}, u32[]{:S(2)}) copy-start(bf16[1152,2,216]{2,0,1:T(8,128)(2,1)S(1)} %all_gather.38) | copy-start | bytes 2985988
  115.2 121.1 %all-gather.7.cloned.1.call-start = ((), (), s32[]{:S(2)}) async-start(), calls=%async_computation.11 | async-start | bytes 1843200 | tf_op jit(solution)/shard_map/all_gather | solution.py:101
  115.7 175.9 %all-gather.5.cloned.1.call-start = ((), (), s32[]{:S(2)}) async-start(), calls=%async_computation.10 | async-start | bytes 7962624 | tf_op jit(solution)/shard_map/all_gather | solution.py:24
  125.8 97.2 %copy-start.32 = (bf16[538]{0:T(1024)(128)(2,1)S(1)}, bf16[538]{0:T(1024)(128)(2,1)}, u32[]{:S(2)}) copy-start(bf16[538]{0:T(1024)(128)(2,1)} %param.25) | copy-start | bytes 3232
  125.8 296.8 %copy-start.22 = (f32[144]{0:T(256)}, f32[144]{0:T(256)S(1)}, u32[]{:S(2)}) copy-start(f32[144]{0:T(256)S(1)} %dynamic-slice_convert_fusion.3) | copy-start | bytes 1732
  221.0 201.6 %copy-start.13 = (f32[4,729]{1,0:T(4,128)}, f32[4,729]{1,0:T(4,128)S(1)}, u32[]{:S(2)}) copy-start(f32[4,729]{1,0:T(4,128)S(1)} %get-tuple-element.80) | copy-start | bytes 34996
  222.4 99.7 %all-gather.9.cloned.1.call-start = ((), (), s32[]{:S(2)}) async-start(), calls=%async_computation.12 | async-start | bytes 1843200 | tf_op jit(solution)/shard_map/all_gather | solution.py:102
  222.9 199.7 %reduce-scatter.18.cloned.1.call-start = ((), (), s32[]{:S(2)}) async-start(), calls=%async_computation.14 | async-start | bytes 7962624 | tf_op jit(solution)/shard_map/reduce_scatter | solution.py:18
  223.0 122.3 %copy-start.31 = (f32[538]{0:T(1024)}, f32[538]{0:T(1024)S(1)}, u32[]{:S(2)}) copy-start(f32[538]{0:T(1024)S(1)} %convert_element_type.176) | copy-start | bytes 6460
  322.0 15.3 %copy-start.33 = (bf16[1152,538]{1,0:T(8,128)(2,1)S(1)}, bf16[1152,538]{1,0:T(8,128)(2,1)}, u32[]{:S(2)}) copy-start(bf16[1152,538]{1,0:T(8,128)(2,1)} %all-gather.7.cloned.1.call-done) | copy-start | bytes 3718660
  345.2 155.8 %reduce-scatter.16.cloned.1.call-start = ((), (), s32[]{:S(2)}) async-start(), calls=%async_computation.13 | async-start | bytes 7962624 | tf_op jit(solution)/shard_map/reduce_scatter | solution.py:18
  356.4 219.4 %all-gather.11.cloned.1.call-start = ((), (), s32[]{:S(2)}) async-start(), calls=%async_computation.15 | async-start | bytes 7962624 | tf_op jit(solution)/shard_map/all_gather | solution.py:24
  506.4 165.2 %reduce-scatter.26.cloned.1.call-start = ((), (), s32[]{:S(2)}) async-start(), calls=%async_computation.19 | async-start | bytes 1843200 | tf_op jit(solution)/shard_map/reduce_scatter | solution.py:245
  518.2 155.3 %reduce-scatter.24.cloned.1.call-start = ((), (), s32[]{:S(2)}) async-start(), calls=%async_computation.18 | async-start | bytes 1843200 | tf_op jit(solution)/shard_map/reduce_scatter | solution.py:242
  518.3 75.3 %copy-start.9 = (f32[1,8,729]{2,1,0:T(8,128)}, f32[1,8,729]{2,1,0:T(8,128)S(1)}, u32[]{:S(2)}) copy-start(f32[1,8,729]{2,1,0:T(8,128)S(1)} %log_add_fusion) | copy-start | bytes 69988
  518.3 57.5 %copy-start.6 = (bf16[2,72,1152]{2,1,0:T(8,128)(2,1)S(1)}, bf16[2,72,1152]{2,1,0:T(8,128)(2,1)}, u32[]{:S(2)}) copy-start(bf16[2,72,1152]{2,1,0:T(8,128)(2,1)} %copy-done.5) | copy-start | bytes 995332
  528.3 157.9 %reduce-scatter.28.cloned.1.call-start = ((), (), s32[]{:S(2)}) async-start(), calls=%async_computation.20 | async-start | bytes 737280
  580.2 30.6 %slice-start = ((s8[7077888]{0:T(1024)(128)(4,1)}), s8[2883584]{0:T(1024)(128)(4,1)S(1)}, s32[]{:S(2)}) async-start(s8[7077888]{0:T(1024)(128)(4,1)} %bitcast.121), calls=%async_computation.22 | async-start | bytes 5767168
  593.7 17.2 %slice-start.1 = ((s8[7077888]{0:T(1024)(128)(4,1)}), s8[4194304]{0:T(1024)(128)(4,1)S(1)}, s32[]{:S(2)}) async-start(s8[7077888]{0:T(1024)(128)(4,1)} %bitcast.121), calls=%async_computation.23 | async-start | bytes 8388608
  593.7 17.1 %copy-start.4 = (bf16[4,729,2,72]{1,3,2,0:T(8,128)(2,1)S(1)}, bf16[4,729,2,72]{1,3,2,0:T(8,128)(2,1)}, u32[]{:S(2)}) copy-start(bf16[4,729,2,72]{1,3,2,0:T(8,128)(2,1)} %copy-done.3) | copy-start | bytes 2519428
  637.8 64.2 %reduce-scatter.22.cloned.1.call-start = ((), (), s32[]{:S(2)}) async-start(), calls=%async_computation.17 | async-start | bytes 1474560 | tf_op jit(solution)/shard_map/reduce_scatter | solution.py:236
  647.0 134.4 %reduce-scatter.20.cloned.1.call-start = ((), (), s32[]{:S(2)}) async-start(), calls=%async_computation.16 | async-start | bytes 7962624 | tf_op jit(solution)/shard_map/reduce_scatter | solution.py:18
  655.3 179.4 %reduce-scatter.30.cloned.1.call-start = ((), (), s32[]{:S(2)}) async-start(), calls=%async_computation.21 | async-start | bytes 368640
  671.6 112.7 %copy-start.27 = (f32[144]{0:T(256)S(1)}, f32[144]{0:T(256)}, u32[]{:S(2)}) copy-start(f32[144]{0:T(256)} %get-tuple-element.46) | copy-start | bytes 1732
  671.6 112.7 %copy-start.28 = (f32[144]{0:T(256)S(1)}, f32[144]{0:T(256)}, u32[]{:S(2)}) copy-start(f32[144]{0:T(256)} %get-tuple-element.52) | copy-start | bytes 1732
  671.6 112.7 %copy-start.29 = (f32[144]{0:T(256)S(1)}, f32[144]{0:T(256)}, u32[]{:S(2)}) copy-start(f32[144]{0:T(256)} %get-tuple-element.75) | copy-start | bytes 1732
  (18 other events, 141.3 us)
Sparse Core Ops, SparseCore 0:
  115.3 77.5 reduce-scatter.13
  345.4 77.2 reduce-scatter.17
  424.9 76.0 reduce-scatter.15
Sparse Core Ops, SparseCore 1:
  117.5 30.2 all-gather.6
  222.5 69.2 all-gather.4
  293.4 28.6 all-gather.8
  506.5 69.3 all-gather.10
  578.9 28.9 reduce-scatter.25
  611.7 30.2 reduce-scatter.23
  645.3 25.1 reduce-scatter.27
  673.5 28.5 reduce-scatter.21
  704.3 77.0 reduce-scatter.19
  812.1 22.6 reduce-scatter.29
where the time goes:
time: 848 us; the launch traced here: 844 us
  waiting for transfers between devices  414 us (49%)
  matrix products  150 us (18%)
  blocking collectives  131 us (15%)
  other arithmetic  83.1 us (10%)
  local copies, waits for them, and re-layouts  47.1 us (6%)
  between operations  16.8 us (2%)
    reduce_scatter x4, waiting for transfers between devices, share_sum(): lax.psum_scatter(partial_rows.astype(jnp.bfloat16), 'tensor', scatter_dim...  257 us
    all_gather x2, waiting for transfers between devices, share_gather(): return lax.all_gather(share_rows, 'tensor', axis=2, tiled=True)  103 us
    psum x3, blocking collectives, row_sums(): return lax.psum((row_pair[0], row_pair[1]), 'tensor')  79.6 us
    unnamed x98, local copies, waits for them, and re-layouts  45.5 us
    unnamed x15, waiting for transfers between devices  20.5 us
    all_gather x1, waiting for transfers between devices, body(): lax.all_gather(down_proj, 'fsdp', axis=1, tiled=True)  19.5 us
    unnamed x1, blocking collectives  17.7 us
    convert_element_type x1, other arithmetic, body(): score_grad = (soft_probs * (prob_grad - jnp.sum(prob_grad * soft_probs, a...  17.1 us
  transfers between devices with their start and end apart: 13, of which 9 were waited for; matrix products, arithmetic and copies ran while one was open for 21% of the time, Pallas kernels for 0%

commit v1 on v0

v1 whole, which is shorter than its diff:
```python
import functools

import jax
import jax.numpy as jnp
from jax import lax
from jax.experimental import pallas as pl
from jax.experimental.pallas import tpu as pltpu
from jax.sharding import PartitionSpec as P

HD = 72
norm_eps = 1e-06
LOG2E = 1.4426950408889634
bf16 = jnp.bfloat16
f32 = jnp.float32


def round_up(value, unit):
    return -(-value // unit) * unit


def nn(a, b):
    return lax.dot_general(a, b, (((1,), (0,)), ((), ())), preferred_element_type=f32)


def nt(a, b):
    return lax.dot_general(a, b, (((1,), (1,)), ((), ())), preferred_element_type=f32)


def fsdp_swap(x, bit):
    size = lax.axis_size("fsdp")
    return lax.ppermute(x, "fsdp", [(i, i ^ bit) for i in range(size)])


def tensor_swap(x, bit):
    size = lax.axis_size("tensor")
    return lax.ppermute(x, "tensor", [(i, i ^ bit) for i in range(size)])


def fsdp_bits(part):
    bits = []
    bit = 1
    while bit < lax.axis_size("fsdp"):
        bits.append(bit)
        bit *= 2
    return bits if part == 0 else bits[::-1]


def gather_rows(own):
    half = own.shape[1] // 2
    cut = lambda x, part: x[:, part * half : (part + 1) * half]
    first = {bit: fsdp_swap(own, bit) for bit in fsdp_bits(0)}
    pieces = []
    for part in (0, 1):
        have = {0: cut(own, part)}
        for bit in fsdp_bits(part):
            new = {}
            for offset, block in have.items():
                new[offset ^ bit] = cut(first[bit], part) if offset == 0 else fsdp_swap(block, bit)
            have.update(new)
        pieces += [have[o] for o in range(len(have))]
        used = half * len(have)
        spare = round_up(used, 128) - used
        if spare:
            pieces.append(jnp.zeros((own.shape[0], spare, own.shape[2]), own.dtype))
    return jnp.concatenate(pieces, axis=1)


def add_low(a, b):
    return (a.astype(f32) + b.astype(f32)).astype(bf16)


def split_blocks(x, axis, start, size):
    count = min(lax.axis_size("fsdp"), (x.shape[axis] - start) // size)
    return {n: lax.slice_in_dim(x, start + n * size, start + (n + 1) * size, axis=axis) for n in range(count)}


def scatter_rows(grads, rows):
    half_pad = grads.shape[1] // 2
    done = []
    for part in (0, 1):
        held = split_blocks(grads, 1, part * half_pad, rows // 2)
        for bit in fsdp_bits(part):
            leave = [o for o in held if o & bit]
            got = fsdp_swap(jnp.concatenate([held.pop(o) for o in leave], axis=1), bit)
            got = split_blocks(got, 1, 0, rows // 2)
            for n, o in enumerate(leave):
                held[o ^ bit] = add_low(held[o ^ bit], got[n])
        done.append(held[0])
    return jnp.concatenate(done, axis=1)


def attend_kernel(seq, heads, xn_ref, w_ref, bias_ref, qkv_ref, ctx_ref, lse_ref, part_ref, total):
    unit = pl.program_id(0)
    rows = xn_ref.shape[0]
    wide = heads * 3 * HD
    qkv = nn(xn_ref[...], w_ref[0, :, :wide]) + bias_ref[0]
    qkv_t = qkv.T
    qkv_ref[0] = qkv_t.astype(bf16)
    live = lax.broadcasted_iota(jnp.int32, (rows, 1), 0) < seq
    contexts = []
    for h in range(heads):
        at = h * 3 * HD
        q_t = qkv_t[at : at + HD].astype(bf16)
        k_n = qkv[:, at + HD : at + 2 * HD].astype(bf16)
        v_t = qkv_t[at + 2 * HD : at + 3 * HD].astype(bf16)
        scores = nn(k_n, q_t) * (HD**-0.5 * LOG2E)
        scores = jnp.where(live, scores, -1e30)
        top = jnp.max(scores, axis=0, keepdims=True)
        weight = jnp.exp2(scores - top)
        total_weight = jnp.sum(weight, axis=0, keepdims=True)
        lse_ref[0, h : h + 1, :] = top + jnp.log2(total_weight)
        contexts.append(nn(v_t, weight.astype(bf16)) / total_weight)
    ctx_t = jnp.concatenate(contexts, axis=0)
    ctx = ctx_t.T.astype(bf16)
    ctx_ref[0] = ctx
    add = nt(ctx, w_ref[0, :, wide : wide + heads * HD])

    @pl.when(unit == 0)
    def _():
        total[...] = add

    @pl.when(unit > 0)
    def _():
        total[...] += add

    @pl.when(unit == pl.num_programs(0) - 1)
    def _():
        half = total.shape[1] // 2
        part_ref[0] = total[:, :half].astype(bf16)
        part_ref[1] = total[:, half:].astype(bf16)


def attend(xn, weights, bias, seq, heads):
    units, feats, cols = weights.shape
    rows = xn.shape[0]
    wide = heads * 3 * HD
    return pl.pallas_call(
        functools.partial(attend_kernel, seq, heads),
        grid=(units,),
        in_specs=[
            pl.BlockSpec((rows, feats), lambda u: (0, 0)),
            pl.BlockSpec((1, feats, cols), lambda u: (u, 0, 0)),
            pl.BlockSpec((1, 1, wide), lambda u: (u, 0, 0)),
        ],
        out_specs=[
            pl.BlockSpec((1, wide, rows), lambda u: (u, 0, 0)),
            pl.BlockSpec((1, rows, heads * HD), lambda u: (u, 0, 0)),
            pl.BlockSpec((1, heads, rows), lambda u: (u, 0, 0)),
            pl.BlockSpec((2, rows, feats // 2), lambda u: (0, 0, 0)),
        ],
        out_shape=[
            jax.ShapeDtypeStruct((units, wide, rows), bf16),
            jax.ShapeDtypeStruct((units, rows, heads * HD), bf16),
            jax.ShapeDtypeStruct((units, heads, rows), f32),
            jax.ShapeDtypeStruct((2, rows, feats // 2), bf16),
        ],
        scratch_shapes=[pltpu.VMEM((rows, feats), f32)],
        compiler_params=pltpu.CompilerParams(vmem_limit_bytes=56 * 1024 * 1024),
        cost_estimate=pl.CostEstimate(
            flops=units * 2 * rows * (feats * cols + heads * 2 * rows * 256),
            bytes_accessed=2 * (units * feats * cols + 4 * rows * feats),
            transcendentals=units * heads * rows * rows,
        ),
    )(xn, weights, bias)


def attend_back_kernel(
    seq, heads, xnt_ref, bg_ref, bgt_ref, w_ref, qkv_ref, ctx_ref, lse_ref,
    dw_ref, db_ref, part_ref, total,
):
    unit = pl.program_id(0)
    rows = bg_ref.shape[0]
    wide = heads * 3 * HD
    d_ctx_t = nn(bg_ref[...], w_ref[0, :, wide : wide + heads * HD]).T
    qkv_t = qkv_ref[0].astype(f32)
    qkv = qkv_t.T
    live = lax.broadcasted_iota(jnp.int32, (rows, 1), 0) < seq
    scale = HD**-0.5
    pieces = []
    for h in range(heads):
        at = h * 3 * HD
        q_t = qkv_t[at : at + HD].astype(bf16)
        k_t = qkv_t[at + HD : at + 2 * HD].astype(bf16)
        k_n = qkv[:, at + HD : at + 2 * HD].astype(bf16)
        v_n = qkv[:, at + 2 * HD : at + 3 * HD].astype(bf16)
        d_o = d_ctx_t[h * HD : (h + 1) * HD].astype(bf16)
        scores = nn(k_n, q_t) * (scale * LOG2E)
        probs = jnp.where(live, jnp.exp2(scores - lse_ref[0, h : h + 1, :]), 0.0)
        d_probs = nn(v_n, d_o)
        delta = jnp.sum(d_probs * probs, axis=0, keepdims=True)
        d_scores = (probs * (d_probs - delta)).astype(bf16)
        d_v = nt(probs.astype(bf16), d_o)
        d_k = nt(d_scores, q_t) * scale
        d_q = nn(k_t, d_scores) * scale
        pieces += [d_q.T, d_k, d_v]
    d_qkv = jnp.concatenate(pieces, axis=1).astype(bf16)
    db_ref[0] = jnp.sum(d_qkv.astype(f32), axis=0, keepdims=True)
    dw_ref[0, :, :wide] = nn(xnt_ref[...], d_qkv).astype(bf16)
    dw_ref[0, :, wide : wide + heads * HD] = nn(bgt_ref[...], ctx_ref[0]).astype(bf16)
    add = nt(d_qkv, w_ref[0, :, :wide])

    @pl.when(unit == 0)
    def _():
        total[...] = add

    @pl.when(unit > 0)
    def _():
        total[...] += add

    @pl.when(unit == pl.num_programs(0) - 1)
    def _():
        half = total.shape[1] // 2
        part_ref[0] = total[:, :half].astype(bf16)
        part_ref[1] = total[:, half:].astype(bf16)


def attend_back(xnt, bg, bgt, weights, qkv_t, ctx, lse, seq, heads):
    units, feats, cols = weights.shape
    rows = bg.shape[0]
    wide = heads * 3 * HD
    by_unit = lambda *shape: pl.BlockSpec((1,) + shape, lambda u: (u, 0, 0))
    return pl.pallas_call(
        functools.partial(attend_back_kernel, seq, heads),
        grid=(units,),
        in_specs=[
            pl.BlockSpec((feats, rows), lambda u: (0, 0)),
            pl.BlockSpec((rows, feats), lambda u: (0, 0)),
            pl.BlockSpec((feats, rows), lambda u: (0, 0)),
            by_unit(feats, cols),
            by_unit(wide, rows),
            by_unit(rows, heads * HD),
            by_unit(heads, rows),
        ],
        out_specs=[
            by_unit(feats, cols),
            by_unit(1, wide),
            pl.BlockSpec((2, rows, feats // 2), lambda u: (0, 0, 0)),
        ],
        out_shape=[
            jax.ShapeDtypeStruct((units, feats, cols), bf16),
            jax.ShapeDtypeStruct((units, 1, wide), f32),
            jax.ShapeDtypeStruct((2, rows, feats // 2), bf16),
        ],
        scratch_shapes=[pltpu.VMEM((rows, feats), f32)],
        compiler_params=pltpu.CompilerParams(vmem_limit_bytes=56 * 1024 * 1024),
        cost_estimate=pl.CostEstimate(
            flops=units * 2 * rows * (2 * feats * cols + heads * 5 * rows * 256),
            bytes_accessed=2 * (2 * units * feats * cols + 6 * rows * feats),
            transcendentals=units * heads * rows * rows,
        ),
    )(xnt, bg, bgt, weights, qkv_t, ctx, lse)


def standardize(rows, width):
    mean = jnp.sum(rows, axis=-1, keepdims=True) / width
    var = jnp.sum(rows * rows, axis=-1, keepdims=True) / width - mean * mean
    rstd = lax.rsqrt(var + norm_eps)
    return (rows - mean) * rstd, rstd


def norm_back(grad, xhat, rstd, gain, width):
    a = grad * gain
    mean_a = jnp.sum(a, axis=-1, keepdims=True) / width
    mean_ax = jnp.sum(a * xhat, axis=-1, keepdims=True) / width
    return rstd * (a - mean_a - xhat * mean_ax)


def gelu_tanh(values_in):
    return jax.nn.gelu(values_in, approximate=True)


def body(
    inputs, cotangent, qkv_proj, qv_bias, out_proj, out_bias, gain_one, shift_one, gain_two,
    shift_two, up_proj, up_bias, down_proj, down_bias,
):
    fsdp, tensor = lax.axis_size("fsdp"), lax.axis_size("tensor")
    images, seq, width = inputs.shape
    groups = images
    sub = tensor // groups
    heads = qkv_proj.shape[1]
    units = up_proj.shape[1]
    shard = qkv_proj.shape[0]
    share = width // tensor
    half = shard // 2
    used = half * fsdp
    half_pad = round_up(used, 128)
    feats = 2 * half_pad
    rows = round_up(seq, 128)
    wide = heads * 3 * HD
    fi, ti = lax.axis_index("fsdp"), lax.axis_index("tensor")
    gi, ci = ti // sub, ti % 2
    group_bits = []
    bit = 1
    while bit < groups:
        group_bits.append(bit * sub)
        bit *= 2
    pair_bit, far_bits = group_bits[0], group_bits[1:][::-1]
    core_bits = []
    bit = 1
    while bit < sub:
        core_bits.append(bit)
        bit *= 2

    def gather_units(x, bits):
        for bit in bits:
            x = jnp.concatenate([x, tensor_swap(x, bit)], axis=0)
        return x

    def scatter_units(x, bits):
        for bit in bits[::-1]:
            keep = x.shape[0] // 2
            x = add_low(x[:keep], tensor_swap(x[keep:], bit))
        return x

    def swap_halves(x, axis):
        low = lax.slice_in_dim(x, 0, half, axis=axis)
        high = lax.slice_in_dim(x, half, 2 * half, axis=axis)
        a = jnp.where(ci == 0, low, high)
        b = jnp.where(ci == 0, high, low)
        return jnp.concatenate([a, b], axis=axis)

    feature_vectors = swap_halves(
        jnp.stack([out_bias, gain_one, shift_one, gain_two, shift_two, down_bias]), 1
    )
    unit_vectors = jnp.concatenate([qv_bias.reshape(-1), up_bias])[None]
    unit_vectors = gather_units(unit_vectors, far_bits + [pair_bit])
    vectors = gather_rows(feature_vectors[:, :, None])[:, :, 0].astype(f32)
    outb, gain1, shift1, gain2, shift2, downb = [vectors[i : i + 1] for i in range(6)]

    wire_a = jnp.concatenate(
        [qkv_proj.reshape(shard, wide), out_proj.reshape(heads * HD, shard).T], axis=1
    )
    wire_a = gather_units(swap_halves(wire_a, 0)[None], far_bits + [pair_bit])
    full_a = gather_rows(wire_a)
    wire_b = jnp.concatenate([up_proj, down_proj.T], axis=1)
    wire_b = gather_units(swap_halves(wire_b, 0)[None], far_bits)
    full_b = gather_rows(wire_b)
    unit_count = full_b.shape[0]
    bias_a = unit_vectors[:, : heads * 2 * HD].astype(f32).reshape(groups, heads, 2, HD)
    bias_a = jnp.concatenate(
        [bias_a[:, :, :1], jnp.zeros_like(bias_a[:, :, :1]), bias_a[:, :, 1:]], axis=2
    ).reshape(groups, 1, wide)
    bias_b = unit_vectors[:unit_count, heads * 2 * HD :].astype(f32)

    lane = jnp.arange(feats, dtype=jnp.int32)
    part, at = lane // half_pad, lane % half_pad
    block = jnp.minimum(at // half, fsdp - 1) ^ fi
    source = jnp.where(at < used, block * shard + (part ^ ci) * half + at % half, -1)
    place = (jnp.arange(width, dtype=jnp.int32)[:, None] == source[None, :]).astype(bf16)

    def arrange(x):
        x = jnp.pad(x, ((0, 0), (0, rows - seq), (0, 0)))
        return jnp.einsum("brd,de->bre", x, place, preferred_element_type=f32).astype(bf16)

    mine = lax.dynamic_slice_in_dim(inputs, gi, 1, 0)
    x = arrange(mine)[0].astype(f32)
    cot = arrange(
        jnp.concatenate(
            [
                lax.dynamic_slice_in_dim(cotangent, gi, 1, 0),
                lax.dynamic_slice_in_dim(cotangent, gi ^ 1, 1, 0),
            ]
        )
    )

    def sum_cores(parts):
        low, high = parts[0].astype(f32), parts[1].astype(f32)
        for bit in core_bits:
            other = tensor_swap(jnp.stack([low, high]).astype(bf16), bit).astype(f32)
            low, high = (low + other[1], high + other[0]) if bit == 1 else (low + other[0], high + other[1])
        return jnp.concatenate([low, high], axis=-1)

    def sum_pair(parts):
        low = parts.astype(bf16)
        low = add_low(low[..., :half_pad], tensor_swap(low[..., half_pad:], 1))
        for bit in core_bits[1:]:
            low = add_low(low, tensor_swap(low, bit))
        return low[0].astype(f32) + tensor_swap(low[1, :seq_pad], pair_bit).astype(f32)

    seq_pad = rows

    xhat1, rstd1 = standardize(x, width)
    xn = (xhat1 * gain1 + shift1).astype(bf16)
    qkv_t, ctx, lse, attn = attend(xn, full_a, bias_a, seq, heads)
    middle = x + sum_cores(attn) + outb
    xhat2, rstd2 = standardize(middle, width)
    n2 = (xhat2 * gain2 + shift2).astype(bf16)
    far_low = tensor_swap(n2[:, :half_pad], pair_bit)
    far_high = tensor_swap(far_low, 1)
    n2 = jnp.stack([n2, jnp.concatenate([far_low, far_high], axis=1)])
    up, down_t = full_b[:, :, :units], full_b[:, :, units:]
    pre_act = (
        jnp.einsum("brd,udf->burf", n2, up, preferred_element_type=f32) + bias_b[None, :, None]
    )
    hidden, pull = jax.vjp(gelu_tanh, pre_act)
    hidden = hidden.astype(bf16)
    mlp = jnp.einsum("burf,udf->brd", hidden, down_t, preferred_element_type=f32)
    out_half = middle[:, :half_pad] + sum_pair(mlp) + downb[:, :half_pad]

    cot_f = cot[0].astype(f32)
    downb_g = jnp.sum(cot_f, axis=0)
    hidden_grad = jnp.einsum("brd,udf->burf", cot, down_t, preferred_element_type=f32)
    pre_grad = pull(hidden_grad)[0].astype(bf16)
    up_bias_g = jnp.sum(pre_grad.astype(f32), axis=(0, 2))
    up_g = jnp.einsum("brd,burf->udf", n2, pre_grad, preferred_element_type=f32).astype(bf16)
    down_g = jnp.einsum("brd,burf->udf", cot, hidden, preferred_element_type=f32).astype(bf16)
    grad_b = scatter_rows(jnp.concatenate([up_g, down_g], axis=2), shard)
    grad_b = scatter_units(grad_b, far_bits)[0]
    n2_part = jnp.einsum("burf,udf->brd", pre_grad, up, preferred_element_type=f32)
    n2_low = sum_pair(n2_part)
    n2_high = tensor_swap(n2_low.astype(bf16), 1).astype(f32)
    n2_grad = jnp.concatenate([n2_low, n2_high], axis=1)
    gain2_g = jnp.sum(n2_grad * xhat2, axis=0)
    shift2_g = jnp.sum(n2_grad, axis=0)
    middle_grad = cot_f + norm_back(n2_grad, xhat2, rstd2, gain2, width)
    outb_g = jnp.sum(middle_grad, axis=0)
    branch_grad = middle_grad.astype(bf16)

    grad_a, bias_a_g, n1 = attend_back(
        xn.T, branch_grad, branch_grad.T, full_a, qkv_t, ctx, lse, seq, heads
    )
    grad_a = scatter_rows(grad_a, shard)
    grad_a = scatter_units(grad_a, far_bits + [pair_bit])[0]
    n1_grad = sum_cores(n1)
    gain1_g = jnp.sum(n1_grad * xhat1, axis=0)
    shift1_g = jnp.sum(n1_grad, axis=0)
    in_half = (middle_grad + norm_back(n1_grad, xhat1, rstd1, gain1, width))[:, :half_pad]

    def spread(y):
        y = y.astype(bf16)
        got = []
        for i in range(groups):
            first = ((gi ^ i) * sub + ti % sub) * share
            pick = (source[:half_pad, None] == first + jnp.arange(share, dtype=jnp.int32)[None]).astype(bf16)
            block = lax.dot_general(pick, y, (((0,), (1,)), ((), ())), preferred_element_type=f32).astype(bf16)
            got.append(tensor_swap(block, i * sub) if i else block)
        got = jnp.stack(got)
        for i, bit in enumerate(group_bits):
            paired = got.reshape((-1, 2, 1 << i) + got.shape[1:])
            paired = jnp.where((gi >> i) & 1 == 1, paired[:, ::-1], paired)
            got = paired.reshape(got.shape)
        return got.transpose(0, 2, 1)[:, :seq]

    layer_out = spread(out_half)
    input_grad = spread(in_half).astype(f32)

    vector_g = jnp.stack([outb_g, gain1_g, shift1_g, gain2_g, shift2_g, downb_g])
    for bit in group_bits:
        vector_g = vector_g + tensor_swap(vector_g, bit)
    vector_g = scatter_rows_exact(vector_g, shard)
    vector_g = swap_halves(vector_g, 1)
    qv_g = bias_a_g.reshape(groups, heads, 3, HD)[:, :, ::2].reshape(groups, heads * 2 * HD)
    for bit in (far_bits + [pair_bit])[::-1]:
        keep = qv_g.shape[0] // 2
        qv_g = qv_g[:keep] + tensor_swap(qv_g[keep:], bit)
    for bit in far_bits[::-1]:
        keep = up_bias_g.shape[0] // 2
        up_bias_g = up_bias_g[:keep] + tensor_swap(up_bias_g[keep:], bit)
    unit_g = jnp.concatenate([qv_g[0], up_bias_g[0]])[None]
    for bit in fsdp_bits(0):
        unit_g = unit_g + fsdp_swap(unit_g, bit)
    qvbias_g = unit_g[0, : heads * 2 * HD].reshape(heads, 2 * HD)
    upbias_g = unit_g[0, heads * 2 * HD :]

    grad_a = swap_halves(grad_a.astype(f32), 0)
    grad_b = swap_halves(grad_b.astype(f32), 0)
    return (
        layer_out,
        input_grad,
        grad_a[:, :wide].reshape(shard, heads, 3 * HD),
        qvbias_g,
        grad_a[:, wide:].T.reshape(heads, HD, shard),
        vector_g[0],
        vector_g[1],
        vector_g[2],
        vector_g[3],
        vector_g[4],
        grad_b[:, :units],
        upbias_g,
        grad_b[:, units:].T,
        vector_g[5],
    )


def scatter_rows_exact(vectors, rows):
    half_pad = vectors.shape[1] // 2
    done = []
    for part in (0, 1):
        held = split_blocks(vectors, 1, part * half_pad, rows // 2)
        for bit in fsdp_bits(part):
            leave = [o for o in held if o & bit]
            got = fsdp_swap(jnp.concatenate([held.pop(o) for o in leave], axis=1), bit)
            got = split_blocks(got, 1, 0, rows // 2)
            for n, o in enumerate(leave):
                held[o ^ bit] = held[o ^ bit] + got[n]
        done.append(held[0])
    return jnp.concatenate(done, axis=1)


def solution(mesh):
    return jax.shard_map(
        body,
        mesh=mesh,
        in_specs=(
            P("fsdp", None, None),
            P("fsdp", None, None),
            P("fsdp", "tensor", None),
            P("tensor", None),
            P("tensor", None, "fsdp"),
            P("fsdp"),
            P("fsdp"),
            P("fsdp"),
            P("fsdp"),
            P("fsdp"),
            P("fsdp", "tensor"),
            P("tensor"),
            P("tensor", "fsdp"),
            P("fsdp"),
        ),
        out_specs=(
            P("fsdp", None, "tensor"),
            P("fsdp", None, "tensor"),
            P("fsdp", "tensor", None),
            P("tensor", None),
            P("tensor", None, "fsdp"),
            P("fsdp"),
            P("fsdp"),
            P("fsdp"),
            P("fsdp"),
            P("fsdp"),
            P("fsdp", "tensor"),
            P("tensor"),
            P("tensor", "fsdp"),
            P("fsdp"),
        ),
        check_vma=False,
    )
```

time: 848 us -> 667 us (0.79)
  waiting for transfers between devices: 414 us -> 264 us
  blocking collectives: 131 us -> 0 us
  local copies, waits for them, and re-layouts: 47.1 us -> 147 us
  matrix products: 150 us -> 59.5 us
  starting transfers between devices: 1.2 us -> 56.7 us
  Pallas kernels: 0 us -> 55.2 us
  between operations: 16.8 us -> 2.08 us
    reduce_scatter x7 -> x0, waiting for transfers between devices: 271 us -> none  [the longest x4 257 us: share_sum(): lax.psum_scatter(partial_rows.astype(jnp.bfloat16), 'tensor', scatter_dim...]
    ppermute x0 -> x54, waiting for transfers between devices: none -> 264 us  [the longest x26 147 us: fsdp_swap(): return lax.ppermute(x, 'fsdp', [(i, i ^ bit) for i in range(size)])]
    all_gather x4 -> x0, waiting for transfers between devices: 122 us -> none  [the longest x2 103 us: share_gather(): return lax.all_gather(share_rows, 'tensor', axis=2, tiled=True)]
    dot_general x18 -> x16, matrix products: 150 us -> 59.5 us  [the longest x2 10.7 us: arrange(): jnp.einsum('brd,de->bre', x, place, preferred_element_type=f32).astype(bf16)]
    psum x4 -> x0, blocking collectives: 90.3 us -> none  [the longest x3 79.6 us: row_sums(): return lax.psum((row_pair[0], row_pair[1]), 'tensor')]
    ppermute x0 -> x54, starting transfers between devices: none -> 56.7 us  [the longest x26 28.8 us: fsdp_swap(): return lax.ppermute(x, 'fsdp', [(i, i ^ bit) for i in range(size)])]
    pallas_call x0 -> x2, Pallas kernels: none -> 55.2 us  [the longest x1 35.3 us: attend_back(): pl.pallas_call(functools.partial(attend_back_kernel, seq, heads), grid=(u...]
    concatenate x0 -> x9, local copies, waits for them, and re-layouts: none -> 25 us  [the longest x3 14.1 us: gather_rows(): return jnp.concatenate(pieces, axis=1)]
  transfers between devices with their start and end apart: 13 -> 54, of which waited for: 9 -> 22; matrix products, arithmetic and copies ran while one was open for 21% -> 35% of each run, Pallas kernels for 0% -> 8%
where the time goes in v1:
time: 667 us; the launch traced here: 662 us
  waiting for transfers between devices  264 us (40%)
  local copies, waits for them, and re-layouts  147 us (22%)
  other arithmetic  77.2 us (12%)
  matrix products  59.5 us (9%)
  starting transfers between devices  56.7 us (9%)
  Pallas kernels  55.2 us (8%)
    ppermute x26, waiting for transfers between devices, fsdp_swap(): return lax.ppermute(x, 'fsdp', [(i, i ^ bit) for i in range(size)])  147 us
    ppermute x28, waiting for transfers between devices, tensor_swap(): return lax.ppermute(x, 'tensor', [(i, i ^ bit) for i in range(size)])  117 us
    unnamed x120, local copies, waits for them, and re-layouts  40.7 us
    pallas_call x1, Pallas kernels, attend_back(): pl.pallas_call(functools.partial(attend_back_kernel, seq, heads), grid=(u...  35.3 us
    ppermute x26, starting transfers between devices, fsdp_swap(): return lax.ppermute(x, 'fsdp', [(i, i ^ bit) for i in range(size)])  28.8 us
    ppermute x28, starting transfers between devices, tensor_swap(): return lax.ppermute(x, 'tensor', [(i, i ^ bit) for i in range(size)])  27.9 us
    pallas_call x1, Pallas kernels, attend(): pl.pallas_call(functools.partial(attend_kernel, seq, heads), grid=(units,...  19.9 us
    convert_element_type x8, other arithmetic, add_low(): return (a.astype(f32) + b.astype(f32)).astype(bf16)  19.6 us
  transfers between devices with their start and end apart: 54, of which 22 were waited for; matrix products, arithmetic and copies ran while one was open for 35% of the time, Pallas kernels for 8%

profile of v1, /device:TPU:0, one launch (start us, length us, event | category | flops | bytes accessed | tf_op | source)
XLA Modules:
  0.0 661.8 jit_solution(5610580340380319397)
XLA Ops:
  21.5 14.8 %constant_dynamic-slice_fusion.1 = (bf16[1,729,1152]{2,0,1:T(2,128)(2,1)S(1)}, bf16[1,729,1152]{2,0,1:T(2,128)(2,1)S(1)}, bf16[1,729,1152]{2,0,1:T(2,128)(2,1)S(1)}) fusion(bf16[4,729,1152]{2,0,1:T(4,128)(2,1)} %param.15, s32[]{:T(128)S(6)} %select_n.195, s32[]{:T(128)S(6)} %select_n.207, bf16[4,729,1152]{2,0,1:T(4,128)(2,1)} %param.14), kind=kLoop, calls=%fused_computation.313 | loop fusion | bytes 10077704 | tf_op jit(solution)/shard_map/dynamic_slice | solution.py:360
  41.3 8.5 %collective-permute-done.4 = bf16[1,288,576]{2,1,0:T(8,128)(2,1)S(1)} collective-permute-done((bf16[1,288,576]{2,1,0:T(8,128)(2,1)S(1)}, bf16[1,288,576]{2,1,0:T(8,128)(2,1)S(1)}, u32[]{:S(2)}, u32[]{:S(2)}) %collective-permute-start.4) | collective-permute-done | bytes 331808 | tf_op jit(solution)/shard_map/ppermute | solution.py:36
  53.7 24.9 %collective-permute-done.5 = bf16[2,288,576]{2,1,0:T(8,128)(2,1)S(1)} collective-permute-done((bf16[2,288,576]{2,1,0:T(8,128)(2,1)S(1)}, bf16[2,288,576]{2,1,0:T(8,128)(2,1)S(1)}, u32[]{:S(2)}, u32[]{:S(2)}) %collective-permute-start.5) | collective-permute-done | bytes 663584 | tf_op jit(solution)/shard_map/ppermute | solution.py:36
  87.4 27.2 %collective-permute-done.3 = bf16[6,144,1]{1,0,2:T(8,128)(2,1)S(1)} collective-permute-done((bf16[6,144,1]{1,0,2:T(8,128)(2,1)S(1)}, bf16[6,144,1]{1,0,2:T(8,128)(2,1)S(1)}, u32[]{:S(2)}, u32[]{:S(2)}) %collective-permute-start.3) | collective-permute-done | bytes 1760 | tf_op jit(solution)/shard_map/ppermute | solution.py:31
  120.9 14.6 %collective-permute-done.8 = bf16[4,144,576]{2,1,0:T(8,128)(2,1)S(1)} collective-permute-done((bf16[4,144,576]{2,1,0:T(8,128)(2,1)S(1)}, bf16[4,144,576]{2,1,0:T(8,128)(2,1)S(1)}, u32[]{:S(2)}, u32[]{:S(2)}) %collective-permute-start.8) | collective-permute-done | bytes 663584 | tf_op jit(solution)/shard_map/ppermute | solution.py:31
  144.2 4.0 copy.85.xn_ref
  159.2 19.9 %shard_map.245 = (bf16[4,432,768]{2,1,0:T(8,128)(2,1)}, bf16[4,768,144]{2,1,0:T(8,128)(2,1)}, f32[4,2,768]{2,1,0:T(2,128)}, bf16[2,768,640]{2,1,0:T(8,128)(2,1)}) custom-call(bf16[768,1280]{1,0:T(8,128)(2,1)} %copy.85.xn_ref, bf16[4,1280,576]{2,1,0:T(8,128)(2,1)} %broadcast_dynamic-update-slice_fusion.1.w_ref, f32[4,1,432]{2,1,0:T(1,128)} %reshape.299.bias_ref), custom_call_target="tpu_custom_call" | custom-call | flops 9361686528 | bytes 13762560 | tf_op jit(solution)/shard_map/pallas_call | solution.py:137
  179.1 4.1 copy.87
  183.3 7.6 %fusion.17 = bf16[2,768,1280]{1,2,0:T(8,128)(2,1)S(1)} fusion(bf16[1,729,1152]{2,1,0:T(8,128)(2,1)} %copy.156, bf16[1,729,1152]{2,1,0:T(8,128)(2,1)} %copy.155, s32[1280]{0:T(1024)S(1)} %copy-done.45), kind=kOutput, calls=%fused_computation.46 | convolution fusion | flops 4545675264 | bytes 7296512 | tf_op jit(solution)/shard_map/brd,de->bre/dot_general | solution.py:353
  201.9 22.4 %collective-permute-done.14 = bf16[2,288,1076]{2,1,0:T(8,128)(2,1)S(1)} collective-permute-done((bf16[2,288,1076]{2,1,0:T(8,128)(2,1)S(1)}, bf16[2,288,1076]{2,1,0:T(8,128)(2,1)S(1)}, u32[]{:S(2)}, u32[]{:S(2)}) %collective-permute-start.14) | collective-permute-done | bytes 1239584 | tf_op jit(solution)/shard_map/ppermute | solution.py:31
  243.9 12.5 %concatenate.118 = bf16[2,1280,1076]{1,2,0:T(8,128)(2,1)} concatenate(bf16[2,144,1076]{1,2,0:T(8,128)(2,1)S(1)} %get-tuple-element.124, bf16[2,144,1076]{1,2,0:T(8,128)(2,1)} %copy.151, bf16[2,144,1076]{1,2,0:T(8,128)(2,1)} %copy.152, bf16[2,144,1076]{1,2,0:T(8,128)(2,1)} %copy.102, bf16[2,64,1076]{1,2,0:T(8,128)(2,1)S(1)} %broadcast.256, ...), dimensions={1} | concatenate | bytes 11018240 | tf_op jit(solution)/shard_map/concatenate | solution.py:65
  261.0 4.5 fusion.41
  265.5 6.3 fusion.34
  271.9 7.9 %convert_reduce_fusion.1 = (f32[2,538]{1,0:T(2,128)S(1)}, bf16[2,2,768,538]{2,3,0,1:T(8,128)(2,1)S(1)}) fusion(f32[2,538,2,768]{3,1,2,0:T(8,128)S(1)} %fusion.41, f32[2,538]{1,0:T(2,128)S(1)} %maximum_convert_fusion, bf16[2,768,1280]{1,2,0:T(8,128)(2,1)S(1)} %copy-done.17, bf16[2,1280,1076]{1,2,0:T(8,128)(2,1)S(1)} %copy-done.15), kind=kOutput, calls=%fused_computation.37 | convolution fusion | flops 4269016064 | bytes 16717008 | tf_op jit(solution)/shard_map/brd,udf->burf/dot_general | solution.py:402
  279.8 5.2 fusion.33
  300.1 9.9 %bitcast_convert_fusion.1 = bf16[2,768,1280]{1,2,0:T(8,128)(2,1)S(1)} fusion(bf16[2,1280,1076]{1,2,0:T(8,128)(2,1)} %concatenate.118, f32[2,538,2,768]{3,1,2,0:T(8,128)} %copy-done.47, f32[2,538]{1,0:T(2,128)S(1)} %maximum_convert_fusion), kind=kOutput, calls=%fused_computation.15 | convolution fusion | flops 4249497600 | bytes 13406416 | tf_op jit(solution)/shard_map/burf,udf->brd/dot_general | solution.py:397
  311.6 10.8 %collective-permute-done.51 = bf16[2,288,1076]{2,1,0:T(8,128)(2,1)} collective-permute-done((bf16[2,288,1076]{2,1,0:T(8,128)(2,1)}, bf16[2,288,1076]{2,1,0:T(8,128)(2,1)}, u32[]{:S(2)}, u32[]{:S(2)}) %collective-permute-start.51) | collective-permute-done | bytes 1239584 | tf_op jit(solution)/shard_map/ppermute | solution.py:31
  333.6 4.8 add_convert_fusion.8
  344.5 8.1 %bitcast_convert_fusion = bf16[2,768,1280]{1,2,0:T(8,128)(2,1)S(1)} fusion(bf16[2,2,768,538]{2,3,0,1:T(8,128)(2,1)} %copy-done.48, bf16[2,1280,1076]{1,2,0:T(8,128)(2,1)} %concatenate.118), kind=kOutput, calls=%fused_computation.14 | convolution fusion | flops 4232970240 | bytes 10059776 | tf_op jit(solution)/shard_map/burf,udf->brd/dot_general | solution.py:409
  365.2 3.5 add_convert_fusion.7
  382.0 21.0 %collective-permute-done.53 = bf16[1,288,1076]{2,1,0:T(8,128)(2,1)} collective-permute-done((bf16[1,288,1076]{2,1,0:T(8,128)(2,1)S(1)}, bf16[1,288,1076]{2,1,0:T(8,128)(2,1)}, u32[]{:S(2)}, u32[]{:S(2)}) %collective-permute-start.53) | collective-permute-done | bytes 619808 | tf_op jit(solution)/shard_map/ppermute | solution.py:36
  410.0 25.0 %collective-permute-done.26 = bf16[768,640]{0,1:T(8,128)(2,1)} collective-permute-done((bf16[768,640]{0,1:T(8,128)(2,1)}, bf16[768,640]{0,1:T(8,128)(2,1)}, u32[]{:S(2)}, u32[]{:S(2)}) %collective-permute-start.26) | collective-permute-done | bytes 983072 | tf_op jit(solution)/shard_map/ppermute | solution.py:36
  458.0 35.3 %shard_map.246 = (bf16[4,1280,576]{2,1,0:T(8,128)(2,1)}, f32[4,1,432]{2,1,0:T(1,128)}, bf16[2,768,640]{2,1,0:T(8,128)(2,1)}) custom-call(bf16[1280,768]{1,0:T(8,128)(2,1)} %fusion.164.xnt_ref, bf16[768,1280]{1,0:T(8,128)(2,1)} %copy.111.bg_ref, bf16[1280,768]{1,0:T(8,128)(2,1)} %convert_bitcast_fusion.2.bgt_ref, ...), custom_call_target="tpu_custom_call" | custom-call | flops 21139292160 | bytes 23592960 | tf_op jit(solution)/shard_map/pallas_call | solution.py:222
  507.0 27.5 %collective-permute-done.41 = f32[1,826]{1,0:T(1,128)S(1)} collective-permute-done((f32[1,826]{1,0:T(1,128)S(1)}, f32[1,826]{1,0:T(1,128)S(1)}, u32[]{:S(2)}, u32[]{:S(2)}) %collective-permute-start.41) | collective-permute-done | bytes 3336 | tf_op jit(solution)/shard_map/ppermute | solution.py:31
  547.8 4.7 fusion.39
  558.8 15.5 %collective-permute-done.34 = bf16[4,288,576]{2,1,0:T(8,128)(2,1)} collective-permute-done((bf16[4,288,576]{2,1,0:T(8,128)(2,1)}, bf16[4,288,576]{2,1,0:T(8,128)(2,1)}, u32[]{:S(2)}, u32[]{:S(2)}) %collective-permute-start.34) | collective-permute-done | bytes 1327136 | tf_op jit(solution)/shard_map/ppermute | solution.py:31
  574.4 13.5 %collective-permute-done.33 = bf16[4,144,576]{2,1,0:T(8,128)(2,1)} collective-permute-done((bf16[4,144,576]{2,1,0:T(8,128)(2,1)}, bf16[4,144,576]{2,1,0:T(8,128)(2,1)}, u32[]{:S(2)}, u32[]{:S(2)}) %collective-permute-start.33) | collective-permute-done | bytes 663584 | tf_op jit(solution)/shard_map/ppermute | solution.py:31
  594.4 12.3 %collective-permute-done.45 = f32[6,288]{1,0:T(8,128)S(1)} collective-permute-done((f32[6,288]{1,0:T(8,128)S(1)}, f32[6,288]{1,0:T(8,128)S(1)}, u32[]{:S(2)}, u32[]{:S(2)}) %collective-permute-start.45) | collective-permute-done | bytes 6944 | tf_op jit(solution)/shard_map/ppermute | solution.py:31
  616.1 3.7 collective-permute-start.30
  620.5 17.2 %collective-permute-done.31 = bf16[144,768]{1,0:T(8,128)(2,1)S(1)} collective-permute-done((bf16[144,768]{1,0:T(8,128)(2,1)S(1)}, bf16[144,768]{1,0:T(8,128)(2,1)S(1)}, u32[]{:S(2)}, u32[]{:S(2)}) %collective-permute-start.31) | collective-permute-done | bytes 221216 | tf_op jit(solution)/shard_map/ppermute | solution.py:36
  637.7 5.0 collective-permute-done.29
  647.7 11.3 %collective-permute-done.37 = bf16[1,288,576]{2,1,0:T(8,128)(2,1)S(1)} collective-permute-done((bf16[1,288,576]{2,1,0:T(8,128)(2,1)S(1)}, bf16[1,288,576]{2,1,0:T(8,128)(2,1)S(1)}, u32[]{:S(2)}, u32[]{:S(2)}) %collective-permute-start.37) | collective-permute-done | bytes 331808 | tf_op jit(solution)/shard_map/ppermute | solution.py:36
  (382 shorter events, 246.3 us)
Async XLA Ops:
  5.0 75.6 %collective-permute-start.1 = (bf16[6,288,1]{1,0,2:T(8,128)(2,1)S(1)}, bf16[6,288,1]{1,0,2:T(8,128)(2,1)}, u32[]{:S(2)}, u32[]{:S(2)}) collective-permute-start(bf16[6,288,1]{1,0,2:T(8,128)(2,1)S(1)} %maximum_bitcast_fusion.6), channel_id=1, source_target_pairs={{0,16},{8,24},{16,0},{24,8},{1,17},{9,25},{17,1},{25,9},{2,18},{10... | collective-permute-start | bytes 10376 | tf_op jit(solution)/shard_map/ppermute | solution.py:31
  8.0 75.0 %collective-permute-start = (bf16[6,288,1]{1,0,2:T(8,128)(2,1)S(1)}, bf16[6,288,1]{1,0,2:T(8,128)(2,1)}, u32[]{:S(2)}, u32[]{:S(2)}) collective-permute-start(bf16[6,288,1]{1,0,2:T(8,128)(2,1)S(1)} %maximum_bitcast_fusion.6), channel_id=1, source_target_pairs={{0,8},{8,0},{16,24},{24,16},{1,9},{9,1},{17,25},{25,17},{2,10},{10... | collective-permute-start | bytes 10376 | tf_op jit(solution)/shard_map/ppermute | solution.py:31
  11.0 69.5 %collective-permute-start.10 = (bf16[1,826]{1,0:T(2,128)(2,1)S(1)}, bf16[1,826]{1,0:T(2,128)(2,1)S(1)}, u32[]{:S(2)}, u32[]{:S(2)}) collective-permute-start(bf16[1,826]{1,0:T(2,128)(2,1)S(1)} %broadcast_in_dim.16), channel_id=1, source_target_pairs={{0,4},{1,5},{2,6},{3,7},{4,0},{5,1},{6,2},{7,3},{8,12},{9,13},{10,... | collective-permute-start | bytes 4964 | tf_op jit(solution)/shard_map/ppermute | solution.py:36
  16.1 33.7 %collective-permute-start.4 = (bf16[1,288,576]{2,1,0:T(8,128)(2,1)S(1)}, bf16[1,288,576]{2,1,0:T(8,128)(2,1)S(1)}, u32[]{:S(2)}, u32[]{:S(2)}) collective-permute-start(bf16[1,288,576]{2,1,0:T(8,128)(2,1)S(1)} %maximum_bitcast_fusion.5), channel_id=1, source_target_pairs={{0,4},{1,5},{2,6},{3,7},{4,0},{5,1},{6,2},{7,3},{8,12},{9,13},{10,... | collective-permute-start | bytes 995336 | tf_op jit(solution)/shard_map/ppermute | solution.py:36
  18.9 129.3 %collective-permute-start.13 = (bf16[1,288,1076]{2,1,0:T(8,128)(2,1)}, bf16[1,288,1076]{2,1,0:T(8,128)(2,1)}, u32[]{:S(2)}, u32[]{:S(2)}) collective-permute-start(bf16[1,288,1076]{2,1,0:T(8,128)(2,1)} %copy.92), channel_id=1, source_target_pairs={{0,4},{1,5},{2,6},{3,7},{4,0},{5,1},{6,2},{7,3},{8,12},{9,13},{10,... | collective-permute-start | bytes 1859336 | tf_op jit(solution)/shard_map/ppermute | solution.py:36
  49.9 28.7 %collective-permute-start.5 = (bf16[2,288,576]{2,1,0:T(8,128)(2,1)S(1)}, bf16[2,288,576]{2,1,0:T(8,128)(2,1)S(1)}, u32[]{:S(2)}, u32[]{:S(2)}) collective-permute-start(bf16[2,288,576]{2,1,0:T(8,128)(2,1)S(1)} %pad_maximum_fusion.12), channel_id=1, source_target_pairs={{0,2},{1,3},{2,0},{3,1},{4,6},{5,7},{6,4},{7,5},{8,10},{9,11},{10,... | collective-permute-start | bytes 1990664 | tf_op jit(solution)/shard_map/ppermute | solution.py:36
  80.0 36.6 %collective-permute-start.6 = (bf16[4,288,576]{2,1,0:T(8,128)(2,1)}, bf16[4,288,576]{2,1,0:T(8,128)(2,1)}, u32[]{:S(2)}, u32[]{:S(2)}) collective-permute-start(bf16[4,288,576]{2,1,0:T(8,128)(2,1)} %pad_maximum_fusion.4), channel_id=1, source_target_pairs={{0,8},{8,0},{16,24},{24,16},{1,9},{9,1},{17,25},{25,17},{2,10},{10... | collective-permute-start | bytes 3981320 | tf_op jit(solution)/shard_map/ppermute | solution.py:31
  81.5 33.1 %collective-permute-start.3 = (bf16[6,144,1]{1,0,2:T(8,128)(2,1)S(1)}, bf16[6,144,1]{1,0,2:T(8,128)(2,1)S(1)}, u32[]{:S(2)}, u32[]{:S(2)}) collective-permute-start(bf16[6,144,1]{1,0,2:T(8,128)(2,1)S(1)} %get-tuple-element.155), channel_id=1, source_target_pairs={{0,8},{8,0},{16,24},{24,16},{1,9},{9,1},{17,25},{25,17},{2,10},{10... | collective-permute-start | bytes 5192 | tf_op jit(solution)/shard_map/ppermute | solution.py:31
  83.8 30.8 %collective-permute-start.2 = (bf16[6,144,1]{1,0,2:T(8,128)(2,1)S(1)}, bf16[6,144,1]{1,0,2:T(8,128)(2,1)S(1)}, u32[]{:S(2)}, u32[]{:S(2)}) collective-permute-start(bf16[6,144,1]{1,0,2:T(8,128)(2,1)S(1)} %get-tuple-element.158), channel_id=1, source_target_pairs={{0,16},{8,24},{16,0},{24,8},{1,17},{9,25},{17,1},{25,9},{2,18},{10... | collective-permute-start | bytes 5192 | tf_op jit(solution)/shard_map/ppermute | solution.py:31
  84.4 35.3 %collective-permute-start.7 = (bf16[4,288,576]{2,1,0:T(8,128)(2,1)}, bf16[4,288,576]{2,1,0:T(8,128)(2,1)}, u32[]{:S(2)}, u32[]{:S(2)}) collective-permute-start(bf16[4,288,576]{2,1,0:T(8,128)(2,1)} %pad_maximum_fusion.4), channel_id=1, source_target_pairs={{0,16},{8,24},{16,0},{24,8},{1,17},{9,25},{17,1},{25,9},{2,18},{10... | collective-permute-start | bytes 3981320 | tf_op jit(solution)/shard_map/ppermute | solution.py:31
  155.7 37.1 %collective-permute-start.15 = (bf16[2,288,1076]{2,1,0:T(8,128)(2,1)}, bf16[2,288,1076]{2,1,0:T(8,128)(2,1)}, u32[]{:S(2)}, u32[]{:S(2)}) collective-permute-start(bf16[2,288,1076]{2,1,0:T(8,128)(2,1)} %copy.94), channel_id=1, source_target_pairs={{0,16},{8,24},{16,0},{24,8},{1,17},{9,25},{17,1},{25,9},{2,18},{10... | collective-permute-start | bytes 3718664 | tf_op jit(solution)/shard_map/ppermute | solution.py:31
  192.2 32.0 %collective-permute-start.14 = (bf16[2,288,1076]{2,1,0:T(8,128)(2,1)S(1)}, bf16[2,288,1076]{2,1,0:T(8,128)(2,1)S(1)}, u32[]{:S(2)}, u32[]{:S(2)}) collective-permute-start(bf16[2,288,1076]{2,1,0:T(8,128)(2,1)S(1)} %copy-done.23), channel_id=1, source_target_pairs={{0,8},{8,0},{16,24},{24,16},{1,9},{9,1},{17,25},{25,17},{2,10},{10... | collective-permute-start | bytes 3718664 | tf_op jit(solution)/shard_map/ppermute | solution.py:31
  195.3 42.7 %collective-permute-start.17 = (bf16[2,144,1076]{2,1,0:T(8,128)(2,1)}, bf16[2,144,1076]{2,1,0:T(8,128)(2,1)}, u32[]{:S(2)}, u32[]{:S(2)}) collective-permute-start(bf16[2,144,1076]{2,1,0:T(8,128)(2,1)} %get-tuple-element.133), channel_id=1, source_target_pairs={{0,8},{8,0},{16,24},{24,16},{1,9},{9,1},{17,25},{25,17},{2,10},{10... | collective-permute-start | bytes 1859336 | tf_op jit(solution)/shard_map/ppermute | solution.py:31
  200.8 28.2 %collective-permute-start.18 = (bf16[768,640]{0,1:T(8,128)(2,1)S(1)}, bf16[768,640]{0,1:T(8,128)(2,1)}, u32[]{:S(2)}, u32[]{:S(2)}) collective-permute-start(bf16[768,640]{0,1:T(8,128)(2,1)S(1)} %slice.550), channel_id=1, source_target_pairs={{0,2},{1,3},{2,0},{3,1},{4,6},{5,7},{6,4},{7,5},{8,10},{9,11},{10,... | collective-permute-start | bytes 2949128 | tf_op jit(solution)/shard_map/ppermute | solution.py:36
  228.9 30.4 %collective-permute-start.19 = (bf16[768,640]{0,1:T(8,128)(2,1)}, bf16[768,640]{0,1:T(8,128)(2,1)}, u32[]{:S(2)}, u32[]{:S(2)}) collective-permute-start(bf16[768,640]{0,1:T(8,128)(2,1)} %collective-permute-done.18), channel_id=1, source_target_pairs={{0,1},{1,0},{2,3},{3,2},{4,5},{5,4},{6,7},{7,6},{8,9},{9,8},{10,11... | collective-permute-start | bytes 2949128 | tf_op jit(solution)/shard_map/ppermute | solution.py:36
  292.2 30.2 %collective-permute-start.51 = (bf16[2,288,1076]{2,1,0:T(8,128)(2,1)}, bf16[2,288,1076]{2,1,0:T(8,128)(2,1)}, u32[]{:S(2)}, u32[]{:S(2)}) collective-permute-start(bf16[2,288,1076]{2,1,0:T(8,128)(2,1)} %copy.123), channel_id=1, source_target_pairs={{0,16},{8,24},{16,0},{24,8},{1,17},{9,25},{17,1},{25,9},{2,18},{10... | collective-permute-start | bytes 3718664 | tf_op jit(solution)/shard_map/ppermute | solution.py:31
  299.6 29.3 %collective-permute-start.49 = (bf16[2,288,1076]{2,1,0:T(8,128)(2,1)}, bf16[2,288,1076]{2,1,0:T(8,128)(2,1)}, u32[]{:S(2)}, u32[]{:S(2)}) collective-permute-start(bf16[2,288,1076]{2,1,0:T(8,128)(2,1)} %copy.118), channel_id=1, source_target_pairs={{0,8},{8,0},{16,24},{24,16},{1,9},{9,1},{17,25},{25,17},{2,10},{10... | collective-permute-start | bytes 3718664 | tf_op jit(solution)/shard_map/ppermute | solution.py:31
  311.6 60.0 %collective-permute-start.20 = (bf16[2,768,640]{1,2,0:T(8,128)(2,1)}, bf16[2,768,640]{1,2,0:T(8,128)(2,1)}, u32[]{:S(2)}, u32[]{:S(2)}) collective-permute-start(bf16[2,768,640]{1,2,0:T(8,128)(2,1)} %slice.555), channel_id=1, source_target_pairs={{0,1},{1,0},{2,3},{3,2},{4,5},{5,4},{6,7},{7,6},{8,9},{9,8},{10,11... | collective-permute-start | bytes 5898248 | tf_op jit(solution)/shard_map/ppermute | solution.py:36
  370.9 32.2 %collective-permute-start.53 = (bf16[1,288,1076]{2,1,0:T(8,128)(2,1)S(1)}, bf16[1,288,1076]{2,1,0:T(8,128)(2,1)}, u32[]{:S(2)}, u32[]{:S(2)}) collective-permute-start(bf16[1,288,1076]{2,1,0:T(8,128)(2,1)S(1)} %copy.128), channel_id=1, source_target_pairs={{0,4},{1,5},{2,6},{3,7},{4,0},{5,1},{6,2},{7,3},{8,12},{9,13},{10,... | collective-permute-start | bytes 1859336 | tf_op jit(solution)/shard_map/ppermute | solution.py:36
  375.6 60.9 %collective-permute-start.21 = (bf16[768,640]{0,1:T(8,128)(2,1)}, bf16[768,640]{0,1:T(8,128)(2,1)}, u32[]{:S(2)}, u32[]{:S(2)}) collective-permute-start(bf16[768,640]{0,1:T(8,128)(2,1)} %slice_bitcast_fusion.8), channel_id=1, source_target_pairs={{0,2},{1,3},{2,0},{3,1},{4,6},{5,7},{6,4},{7,5},{8,10},{9,11},{10,... | collective-permute-start | bytes 2949128 | tf_op jit(solution)/shard_map/ppermute | solution.py:36
  380.8 54.1 %collective-permute-start.26 = (bf16[768,640]{0,1:T(8,128)(2,1)}, bf16[768,640]{0,1:T(8,128)(2,1)}, u32[]{:S(2)}, u32[]{:S(2)}) collective-permute-start(bf16[768,640]{0,1:T(8,128)(2,1)} %slice_bitcast_fusion.6), channel_id=1, source_target_pairs={{0,2},{1,3},{2,0},{3,1},{4,6},{5,7},{6,4},{7,5},{8,10},{9,11},{10,... | collective-permute-start | bytes 2949128 | tf_op jit(solution)/shard_map/ppermute | solution.py:36
  439.6 62.1 %collective-permute-start.22 = (bf16[144,768]{1,0:T(8,128)(2,1)}, bf16[144,768]{1,0:T(8,128)(2,1)}, u32[]{:S(2)}, u32[]{:S(2)}) collective-permute-start(bf16[144,768]{1,0:T(8,128)(2,1)} %convolution_convert_fusion.6), channel_id=1, source_target_pairs={{0,2},{1,3},{2,0},{3,1},{4,6},{5,7},{6,4},{7,5},{8,10},{9,11},{10,... | collective-permute-start | bytes 663560 | tf_op jit(solution)/shard_map/ppermute | solution.py:36
  440.8 61.5 %collective-permute-start.23 = (bf16[144,768]{1,0:T(8,128)(2,1)}, bf16[144,768]{1,0:T(8,128)(2,1)}, u32[]{:S(2)}, u32[]{:S(2)}) collective-permute-start(bf16[144,768]{1,0:T(8,128)(2,1)} %convolution_convert_fusion.5), channel_id=1, source_target_pairs={{0,4},{1,5},{2,6},{3,7},{4,0},{5,1},{6,2},{7,3},{8,12},{9,13},{10,... | collective-permute-start | bytes 663560 | tf_op jit(solution)/shard_map/ppermute | solution.py:36
  443.2 59.0 %collective-permute-start.24 = (bf16[144,768]{1,0:T(8,128)(2,1)}, bf16[144,768]{1,0:T(8,128)(2,1)}, u32[]{:S(2)}, u32[]{:S(2)}) collective-permute-start(bf16[144,768]{1,0:T(8,128)(2,1)} %convolution_convert_fusion.4), channel_id=1, source_target_pairs={{0,6},{1,7},{2,4},{3,5},{4,2},{5,3},{6,0},{7,1},{8,14},{9,15},{10,... | collective-permute-start | bytes 663560 | tf_op jit(solution)/shard_map/ppermute | solution.py:36
  496.6 47.8 %collective-permute-start.28 = (bf16[2,768,640]{1,2,0:T(8,128)(2,1)S(1)}, bf16[2,768,640]{1,2,0:T(8,128)(2,1)}, u32[]{:S(2)}, u32[]{:S(2)}) collective-permute-start(bf16[2,768,640]{1,2,0:T(8,128)(2,1)S(1)} %copy.112), channel_id=1, source_target_pairs={{0,1},{1,0},{2,3},{3,2},{4,5},{5,4},{6,7},{7,6},{8,9},{9,8},{10,11... | collective-permute-start | bytes 5898248 | tf_op jit(solution)/shard_map/ppermute | solution.py:36
  500.2 41.5 %collective-permute-start.32 = (bf16[4,288,576]{2,1,0:T(8,128)(2,1)}, bf16[4,288,576]{2,1,0:T(8,128)(2,1)S(1)}, u32[]{:S(2)}, u32[]{:S(2)}) collective-permute-start(bf16[4,288,576]{2,1,0:T(8,128)(2,1)} %pad_maximum_fusion.5), channel_id=1, source_target_pairs={{0,8},{8,0},{16,24},{24,16},{1,9},{9,1},{17,25},{25,17},{2,10},{10... | collective-permute-start | bytes 3981320 | tf_op jit(solution)/shard_map/ppermute | solution.py:31
  506.3 28.2 %collective-permute-start.41 = (f32[1,826]{1,0:T(1,128)S(1)}, f32[1,826]{1,0:T(1,128)S(1)}, u32[]{:S(2)}, u32[]{:S(2)}) collective-permute-start(f32[1,826]{1,0:T(1,128)S(1)} %broadcast_in_dim.19), channel_id=1, source_target_pairs={{0,8},{8,0},{16,24},{24,16},{1,9},{9,1},{17,25},{25,17},{2,10},{10... | collective-permute-start | bytes 9920 | tf_op jit(solution)/shard_map/ppermute | solution.py:31
  538.8 35.6 %collective-permute-start.34 = (bf16[4,288,576]{2,1,0:T(8,128)(2,1)}, bf16[4,288,576]{2,1,0:T(8,128)(2,1)}, u32[]{:S(2)}, u32[]{:S(2)}) collective-permute-start(bf16[4,288,576]{2,1,0:T(8,128)(2,1)} %concatenate.124), channel_id=1, source_target_pairs={{0,16},{8,24},{16,0},{24,8},{1,17},{9,25},{17,1},{25,9},{2,18},{10... | collective-permute-start | bytes 3981320 | tf_op jit(solution)/shard_map/ppermute | solution.py:31
  543.8 44.0 %collective-permute-start.33 = (bf16[4,144,576]{2,1,0:T(8,128)(2,1)}, bf16[4,144,576]{2,1,0:T(8,128)(2,1)}, u32[]{:S(2)}, u32[]{:S(2)}) collective-permute-start(bf16[4,144,576]{2,1,0:T(8,128)(2,1)} %add_convert_fusion.16), channel_id=1, source_target_pairs={{0,16},{8,24},{16,0},{24,8},{1,17},{9,25},{17,1},{25,9},{2,18},{10... | collective-permute-start | bytes 1990664 | tf_op jit(solution)/shard_map/ppermute | solution.py:31
  558.8 32.9 %collective-permute-start.44 = (f32[6,1280]{1,0:T(8,128)S(1)}, f32[6,1280]{1,0:T(8,128)S(1)}, u32[]{:S(2)}, u32[]{:S(2)}) collective-permute-start(f32[6,1280]{1,0:T(8,128)S(1)} %add.426), channel_id=1, source_target_pairs={{0,4},{1,5},{2,6},{3,7},{4,0},{5,1},{6,2},{7,3},{8,12},{9,13},{10,... | collective-permute-start | bytes 92168 | tf_op jit(solution)/shard_map/ppermute | solution.py:36
  611.4 31.6 %collective-permute-start.36 = (bf16[2,288,576]{2,1,0:T(8,128)(2,1)S(1)}, bf16[2,288,576]{2,1,0:T(8,128)(2,1)S(1)}, u32[]{:S(2)}, u32[]{:S(2)}) collective-permute-start(bf16[2,288,576]{2,1,0:T(8,128)(2,1)S(1)} %pad_maximum_fusion.11), channel_id=1, source_target_pairs={{0,2},{1,3},{2,0},{3,1},{4,6},{5,7},{6,4},{7,5},{8,10},{9,11},{10,... | collective-permute-start | bytes 1990664 | tf_op jit(solution)/shard_map/ppermute | solution.py:36
  616.1 26.6 %collective-permute-start.29 = (bf16[144,768]{1,0:T(8,128)(2,1)S(1)}, bf16[144,768]{1,0:T(8,128)(2,1)S(1)}, u32[]{:S(2)}, u32[]{:S(2)}) collective-permute-start(bf16[144,768]{1,0:T(8,128)(2,1)S(1)} %convolution_convert_fusion.2), channel_id=1, source_target_pairs={{0,2},{1,3},{2,0},{3,1},{4,6},{5,7},{6,4},{7,5},{8,10},{9,11},{10,... | collective-permute-start | bytes 663560 | tf_op jit(solution)/shard_map/ppermute | solution.py:36
  (71 other events, 1242.3 us)

commit v2 on v1

v2 whole, which is shorter than its diff:
```python
import functools

import jax
import jax.numpy as jnp
from jax import lax
from jax.experimental import pallas as pl
from jax.experimental.pallas import tpu as pltpu
from jax.sharding import PartitionSpec as P

HD = 72
norm_eps = 1e-06
LOG2E = 1.4426950408889634
GELU_A = 0.7978845608028654
GELU_B = 0.044715
MIB = 1024 * 1024
bf16 = jnp.bfloat16
f32 = jnp.float32


def round_up(value, unit):
    return -(-value // unit) * unit


def nn(a, b):
    return lax.dot_general(a, b, (((1,), (0,)), ((), ())), preferred_element_type=f32)


def nt(a, b):
    return lax.dot_general(a, b, (((1,), (1,)), ((), ())), preferred_element_type=f32)


def shaped(shape, dtype):
    return jax.ShapeDtypeStruct(shape, dtype)


def on_chip(kernel, out_shape, args, scratch=(), flops=0, exps=0):
    whole = pl.BlockSpec(memory_space=pltpu.VMEM)
    moved = sum(a.size * a.dtype.itemsize for a in list(args) + list(out_shape))
    return pl.pallas_call(
        kernel,
        in_specs=[whole] * len(args),
        out_specs=[whole] * len(out_shape),
        out_shape=list(out_shape),
        scratch_shapes=list(scratch),
        compiler_params=pltpu.CompilerParams(vmem_limit_bytes=60 * MIB),
        cost_estimate=pl.CostEstimate(flops=flops, bytes_accessed=moved, transcendentals=exps),
    )(*args)


def fsdp_swap(x, bit):
    size = lax.axis_size("fsdp")
    return lax.ppermute(x, "fsdp", [(i, i ^ bit) for i in range(size)])


def tensor_swap(x, bit):
    size = lax.axis_size("tensor")
    return lax.ppermute(x, "tensor", [(i, i ^ bit) for i in range(size)])


def fsdp_bits(part):
    bits = []
    bit = 1
    while bit < lax.axis_size("fsdp"):
        bits.append(bit)
        bit *= 2
    return bits if part == 0 else bits[::-1]


def gather_pieces(own):
    half = own.shape[0] // 2
    arrays = [own]
    first = {}
    for bit in fsdp_bits(0):
        first[bit] = len(arrays)
        arrays.append(fsdp_swap(own, bit))
    plan = []
    for part in (0, 1):
        have = {0: (0, part * half)}
        for bit in fsdp_bits(part):
            new = {}
            for offset, (index, row) in have.items():
                if offset == 0:
                    new[bit] = (first[bit], part * half)
                else:
                    new[offset ^ bit] = (len(arrays), 0)
                    arrays.append(fsdp_swap(arrays[index][row : row + half], bit))
            have.update(new)
        plan.append([have[o] for o in range(len(have))])
    return arrays, plan


def assemble(out, refs, plan, half, half_pad):
    for part in (0, 1):
        for offset, (index, row) in enumerate(plan[part]):
            at = part * half_pad + offset * half
            out[at : at + half, :] = refs[index][row : row + half, :]
        used = len(plan[part]) * half
        if used < half_pad:
            out[part * half_pad + used : (part + 1) * half_pad, :] = jnp.zeros(
                (half_pad - used, out.shape[1]), out.dtype
            )


def add_low(a, b):
    return (a.astype(f32) + b.astype(f32)).astype(bf16)


def split_blocks(x, axis, start, size):
    return {
        n: lax.slice_in_dim(x, start + n * size, start + (n + 1) * size, axis=axis)
        for n in range(lax.axis_size("fsdp"))
    }


def scatter_rows(grads, rows):
    done = []
    for part in (0, 1):
        held = split_blocks(grads, 0, part * (grads.shape[0] // 2), rows // 2)
        for bit in fsdp_bits(part):
            leave = [o for o in held if o & bit]
            got = fsdp_swap(jnp.concatenate([held.pop(o) for o in leave], axis=0), bit)
            for n, o in enumerate(leave):
                held[o ^ bit] = add_low(held[o ^ bit], got[n * (rows // 2) : (n + 1) * (rows // 2)])
        done.append(held[0])
    return jnp.concatenate(done, axis=0)


def attend_kernel(seq, heads, plan, count, first, *refs):
    xn_ref, bias_ref = refs[:2]
    pieces = refs[2 : 2 + count]
    rest = refs[2 + count :]
    if first:
        w_ref, qkv_ref, ctx_ref, lse_ref, part_ref = rest
    else:
        before_ref, w_ref, qkv_ref, ctx_ref, lse_ref, part_ref = rest
    rows, feats = xn_ref.shape
    half = feats // 2
    wide = heads * 3 * HD
    assemble(w_ref, pieces, plan, pieces[0].shape[0] // 2, half)
    qkv = nn(xn_ref[...], w_ref[:, :wide]) + bias_ref[...]
    qkv_t = qkv.T
    qkv_ref[...] = qkv_t.astype(bf16)
    live = lax.broadcasted_iota(jnp.int32, (rows, 1), 0) < seq
    contexts = []
    for h in range(heads):
        at = h * 3 * HD
        q_t = qkv_t[at : at + HD].astype(bf16)
        k_n = qkv[:, at + HD : at + 2 * HD].astype(bf16)
        v_t = qkv_t[at + 2 * HD : at + 3 * HD].astype(bf16)
        scores = nn(k_n, q_t) * (HD**-0.5 * LOG2E)
        scores = jnp.where(live, scores, -1e30)
        top = jnp.max(scores, axis=0, keepdims=True)
        weight = jnp.exp2(scores - top)
        total_weight = jnp.sum(weight, axis=0, keepdims=True)
        lse_ref[h : h + 1, :] = top + jnp.log2(total_weight)
        contexts.append(nn(v_t, weight.astype(bf16)) / total_weight)
    ctx = jnp.concatenate(contexts, axis=0).T.astype(bf16)
    ctx_ref[...] = ctx
    for n in (0, 1):
        add = nt(ctx, w_ref[n * half : (n + 1) * half, wide : wide + heads * HD])
        if not first:
            add = add + before_ref[n].astype(f32)
        part_ref[n] = add.astype(bf16)


def attend(xn, bias, pieces, plan, before, seq, heads):
    rows, feats = xn.shape
    wide = heads * 3 * HD
    cols = pieces[0].shape[1]
    args = [xn, bias] + pieces + ([] if before is None else [before])
    return on_chip(
        functools.partial(attend_kernel, seq, heads, plan, len(pieces), before is None),
        [
            shaped((feats, cols), bf16),
            shaped((wide, rows), bf16),
            shaped((rows, heads * HD), bf16),
            shaped((heads, rows), f32),
            shaped((2, rows, feats // 2), bf16),
        ],
        args,
        flops=2 * rows * (feats * cols + heads * 2 * rows * 256),
        exps=heads * rows * rows,
    )


def attend_back_kernel(seq, heads, first, *refs):
    xnt_ref, bg_ref, w_ref, qkv_ref, lse_ref = refs[:5]
    if first:
        dw_ref, db_ref, part_ref = refs[5:]
    else:
        before_ref, dw_ref, db_ref, part_ref = refs[5:]
    rows, feats = bg_ref.shape
    half = feats // 2
    wide = heads * 3 * HD
    d_ctx_t = nn(bg_ref[...], w_ref[:, wide : wide + heads * HD]).T
    qkv_t = qkv_ref[...].astype(f32)
    qkv = qkv_t.T
    live = lax.broadcasted_iota(jnp.int32, (rows, 1), 0) < seq
    scale = HD**-0.5
    pieces = []
    for h in range(heads):
        at = h * 3 * HD
        q_t = qkv_t[at : at + HD].astype(bf16)
        k_t = qkv_t[at + HD : at + 2 * HD].astype(bf16)
        k_n = qkv[:, at + HD : at + 2 * HD].astype(bf16)
        v_n = qkv[:, at + 2 * HD : at + 3 * HD].astype(bf16)
        d_o = d_ctx_t[h * HD : (h + 1) * HD].astype(bf16)
        scores = nn(k_n, q_t) * (scale * LOG2E)
        probs = jnp.where(live, jnp.exp2(scores - lse_ref[h : h + 1, :]), 0.0)
        d_probs = nn(v_n, d_o)
        delta = jnp.sum(d_probs * probs, axis=0, keepdims=True)
        d_scores = (probs * (d_probs - delta)).astype(bf16)
        d_v = nt(probs.astype(bf16), d_o)
        d_k = nt(d_scores, q_t) * scale
        d_q = nn(k_t, d_scores) * scale
        pieces += [d_q.T, d_k, d_v]
    d_qkv = jnp.concatenate(pieces, axis=1).astype(bf16)
    db_ref[...] = jnp.sum(d_qkv.astype(f32), axis=0, keepdims=True)
    dw_ref[...] = nn(xnt_ref[...], d_qkv).astype(bf16)
    for n in (0, 1):
        add = nt(d_qkv, w_ref[n * half : (n + 1) * half, :wide])
        if not first:
            add = add + before_ref[n].astype(f32)
        part_ref[n] = add.astype(bf16)


def attend_back(xnt, bg, weights, qkv_t, lse, before, seq, heads):
    rows, feats = bg.shape
    wide = heads * 3 * HD
    args = [xnt, bg, weights, qkv_t, lse] + ([] if before is None else [before])
    return on_chip(
        functools.partial(attend_back_kernel, seq, heads, before is None),
        [
            shaped((feats, wide), bf16),
            shaped((1, wide), f32),
            shaped((2, rows, feats // 2), bf16),
        ],
        args,
        flops=2 * rows * (2 * feats * wide + heads * 5 * rows * 256),
        exps=heads * rows * rows,
    )


def out_grad_kernel(count, bg_ref, *refs):
    ctx = jnp.concatenate([r[...].astype(f32) for r in refs[:count]], axis=1).astype(bf16)
    refs[count][...] = nn(bg_ref[...].astype(f32).T.astype(bf16), ctx).astype(bf16)


def out_grad(bg, contexts):
    rows, feats = bg.shape
    cols = sum(c.shape[1] for c in contexts)
    return on_chip(
        functools.partial(out_grad_kernel, len(contexts)),
        [shaped((feats, cols), bf16)],
        [bg] + contexts,
        flops=2 * rows * feats * cols,
    )[0]


def mlp_kernel(plan, counts, first, *refs):
    low_ref, high_ref, cot_ref, cott_ref, bias_ref = refs[:5]
    at = 5
    pieces = []
    for count in counts:
        pieces.append(refs[at : at + count])
        at += count
    before = []
    if not first:
        before = refs[at : at + len(counts)]
        at += len(counts)
    out_ref, back_ref, db_ref = refs[at : at + 3]
    dw_refs = refs[at + 3 : at + 3 + len(counts)]
    n2_ref, n2t_ref, w_ref, out_sum, back_sum = refs[at + 3 + len(counts) :]
    half = low_ref.shape[1]
    n2_ref[:, :half] = low_ref[...]
    n2_ref[:, half:] = high_ref[...]
    n2t_ref[:half, :] = low_ref[...].astype(f32).T.astype(bf16)
    n2t_ref[half:, :] = high_ref[...].astype(f32).T.astype(bf16)
    for u in range(len(counts)):
        assemble(w_ref, pieces[u], plan, pieces[u][0].shape[0] // 2, half)
        units = w_ref.shape[1] // 2
        up = w_ref[:, :units]
        down = w_ref[:, units:]
        v = nn(n2_ref[...], up) + bias_ref[u : u + 1, :]
        square = v * v
        t = jnp.tanh(GELU_A * v * (1.0 + GELU_B * square))
        hidden = (0.5 * v * (1.0 + t)).astype(bf16)
        slope = 0.5 * (1.0 + t) + (0.5 * GELU_A) * v * (1.0 - t * t) * (1.0 + 3.0 * GELU_B * square)
        pre_grad = (nn(cot_ref[...], down) * slope).astype(bf16)
        out_add = nt(hidden, down)
        back_add = nt(pre_grad, up)
        if u == 0:
            out_sum[...] = out_add
            back_sum[...] = back_add
        else:
            out_sum[...] += out_add
            back_sum[...] += back_add
        db_ref[u : u + 1, :] = jnp.sum(pre_grad.astype(f32), axis=0, keepdims=True)
        d_up = nn(n2t_ref[...], pre_grad)
        d_down = nn(cott_ref[...], hidden)
        if not first:
            d_up = d_up + before[u][:, :units].astype(f32)
            d_down = d_down + before[u][:, units:].astype(f32)
        dw_refs[u][:, :units] = d_up.astype(bf16)
        dw_refs[u][:, units:] = d_down.astype(bf16)
    for n in (0, 1):
        out_ref[n] = out_sum[:, n * half : (n + 1) * half].astype(bf16)
        back_ref[n] = back_sum[:, n * half : (n + 1) * half].astype(bf16)


def mlp(low, high, cot, cot_t, bias, gathered, before):
    rows, half = low.shape
    feats = 2 * half
    plan = gathered[0][1]
    cols = gathered[0][0][0].shape[1]
    args = [low, high, cot, cot_t, bias] + [a for g in gathered for a in g[0]] + list(before or [])
    found = on_chip(
        functools.partial(mlp_kernel, plan, [len(g[0]) for g in gathered], before is None),
        [
            shaped((2, rows, half), bf16),
            shaped((2, rows, half), bf16),
            shaped((len(gathered), cols // 2), f32),
        ]
        + [shaped((feats, cols), bf16)] * len(gathered),
        args,
        scratch=[
            pltpu.VMEM((rows, feats), bf16),
            pltpu.VMEM((feats, rows), bf16),
            pltpu.VMEM((feats, cols), bf16),
            pltpu.VMEM((rows, feats), f32),
            pltpu.VMEM((rows, feats), f32),
        ],
        flops=len(gathered) * 6 * rows * feats * cols,
        exps=len(gathered) * rows * cols // 2,
    )
    return found[0], found[1], found[2], found[3:]


def standardize(rows, width):
    mean = jnp.sum(rows, axis=-1, keepdims=True) / width
    var = jnp.sum(rows * rows, axis=-1, keepdims=True) / width - mean * mean
    rstd = lax.rsqrt(var + norm_eps)
    return (rows - mean) * rstd, rstd


def norm_back(grad, xhat, rstd, gain, width):
    a = grad * gain
    mean_a = jnp.sum(a, axis=-1, keepdims=True) / width
    mean_ax = jnp.sum(a * xhat, axis=-1, keepdims=True) / width
    return rstd * (a - mean_a - xhat * mean_ax)


def by_rows(kernel, out_shape, out_whole, args, whole, rows, tile):
    def spec(shape, uncut):
        if uncut:
            return pl.BlockSpec(shape, lambda i, n=len(shape): (0,) * n)
        if len(shape) == 3:
            return pl.BlockSpec((shape[0], tile, shape[2]), lambda i: (0, i, 0))
        return pl.BlockSpec((tile, shape[1]), lambda i: (i, 0))

    return pl.pallas_call(
        kernel,
        grid=(rows // tile,),
        in_specs=[spec(a.shape, w) for a, w in zip(args, whole)],
        out_specs=[spec(o.shape, w) for o, w in zip(out_shape, out_whole)],
        out_shape=list(out_shape),
        compiler_params=pltpu.CompilerParams(vmem_limit_bytes=40 * MIB),
        cost_estimate=pl.CostEstimate(
            flops=0,
            bytes_accessed=sum(a.size * a.dtype.itemsize for a in list(args) + list(out_shape)),
            transcendentals=0,
        ),
    )(*args)


def joined(ref):
    return jnp.concatenate([ref[0].astype(f32), ref[1].astype(f32)], axis=-1)


def crossed(ref):
    return jnp.concatenate([ref[1].astype(f32), ref[0].astype(f32)], axis=-1)


def middle_kernel(width, x_ref, own_ref, other_ref, vec_ref, middle_ref, low_ref, high_ref):
    half = low_ref.shape[1]
    middle = x_ref[...].astype(f32) + joined(own_ref) + crossed(other_ref) + vec_ref[0:1, :]
    middle_ref[...] = middle
    xhat, rstd = standardize(middle, width)
    n2 = (xhat * vec_ref[3:4, :] + vec_ref[4:5, :]).astype(bf16)
    low_ref[...] = n2[:, :half]
    high_ref[...] = n2[:, half:]


def add_sums(ref, sums):
    @pl.when(pl.program_id(0) == 0)
    def _():
        ref[...] = sums

    @pl.when(pl.program_id(0) > 0)
    def _():
        ref[...] += sums


def column_sums(parts):
    return jnp.concatenate([jnp.sum(p, axis=0, keepdims=True) for p in parts], axis=0)


def middle_back_kernel(width, low_ref, high_ref, middle_ref, cot_ref, vec_ref, grad_ref, bg_ref, sum_ref):
    half = low_ref.shape[1]
    grad = jnp.concatenate([low_ref[...].astype(f32), high_ref[...].astype(f32)], axis=-1)
    xhat, rstd = standardize(middle_ref[...], width)
    cot = cot_ref[...].astype(f32)
    back = cot + norm_back(grad, xhat, rstd, vec_ref[3:4, :], width)
    grad_ref[...] = back[:, :half]
    bg_ref[...] = back.astype(bf16)
    add_sums(
        sum_ref,
        column_sums([back[:, :half], grad[:, :half] * xhat[:, :half], grad[:, :half], cot[:, :half]]),
    )


def first_back_kernel(width, own_ref, other_ref, x_ref, grad_ref, vec_ref, pick_ref, out_ref, sum_ref):
    half = grad_ref.shape[1]
    grad = joined(own_ref) + crossed(other_ref)
    xhat, rstd = standardize(x_ref[...].astype(f32), width)
    back = norm_back(grad, xhat, rstd, vec_ref[1:2, :], width)
    result = (grad_ref[...] + back[:, :half]).astype(bf16)
    out_ref[...] = nt(pick_ref[...], result).astype(bf16)
    add_sums(sum_ref, column_sums([grad[:, :half] * xhat[:, :half], grad[:, :half]]))


def body(
    inputs, cotangent, qkv_proj, qv_bias, out_proj, out_bias, gain_one, shift_one, gain_two,
    shift_two, up_proj, up_bias, down_proj, down_bias,
):
    fsdp, tensor = lax.axis_size("fsdp"), lax.axis_size("tensor")
    images, seq, width = inputs.shape
    groups = images
    sub = tensor // groups
    heads = qkv_proj.shape[1]
    units = up_proj.shape[1]
    shard = qkv_proj.shape[0]
    share = width // tensor
    half = shard // 2
    used = half * fsdp
    half_pad = round_up(used, 128)
    feats = 2 * half_pad
    rows = round_up(seq, 128)
    tile = rows // 3 if rows % 384 == 0 else 128
    wide = heads * 3 * HD
    qv = heads * 2 * HD
    fi, ti = lax.axis_index("fsdp"), lax.axis_index("tensor")
    gi, ci = ti // sub, ti % 2
    group_bits = []
    bit = 1
    while bit < groups:
        group_bits.append(bit * sub)
        bit *= 2
    pair_bit, far_bits = group_bits[0], group_bits[1:][::-1]
    core_bits = []
    bit = 1
    while bit < sub:
        core_bits.append(bit)
        bit *= 2

    def gather_units(x, bits):
        have = [x]
        for bit in bits:
            have = have + [tensor_swap(h, bit) for h in have]
        return have

    def scatter_units(have, bits, add):
        for bit in bits[::-1]:
            keep = len(have) // 2
            have = [add(a, tensor_swap(b, bit)) for a, b in zip(have[:keep], have[keep:])]
        return have[0]

    def swap_halves(x, axis):
        low = lax.slice_in_dim(x, 0, half, axis=axis)
        high = lax.slice_in_dim(x, half, 2 * half, axis=axis)
        a = jnp.where(ci == 0, low, high)
        b = jnp.where(ci == 0, high, low)
        return jnp.concatenate([a, b], axis=axis)

    own_vectors = jnp.stack([out_bias, gain_one, shift_one, gain_two, shift_two, down_bias])
    own_vectors = swap_halves(own_vectors, 1)
    blocks = {0: own_vectors}
    for bit in fsdp_bits(0):
        blocks.update({o ^ bit: b for o, b in zip(blocks, fsdp_swap(jnp.stack(list(blocks.values())), bit))})
    spare = jnp.zeros((6, half_pad - used), bf16)
    vectors = jnp.concatenate(
        [blocks[o][:, :half] for o in range(fsdp)] + [spare]
        + [blocks[o][:, half:] for o in range(fsdp)] + [spare],
        axis=1,
    ).astype(f32)
    vectors = jnp.pad(vectors, ((0, 2), (0, 0)))
    unit_vectors = jnp.concatenate([qv_bias.reshape(-1), up_bias])[None]
    for bit in far_bits + [pair_bit]:
        unit_vectors = jnp.concatenate([unit_vectors, tensor_swap(unit_vectors, bit)])
    unit_vectors = unit_vectors.astype(f32)

    wire_a = jnp.concatenate(
        [qkv_proj.reshape(shard, wide), out_proj.reshape(heads * HD, shard).T], axis=1
    )
    wires_a = gather_units(swap_halves(wire_a, 0), far_bits + [pair_bit])
    wire_b = jnp.concatenate([up_proj, down_proj.T], axis=1)
    wires_b = gather_units(swap_halves(wire_b, 0), far_bits)
    order = sorted(range(groups), key=lambda u: (u != 0, u != groups // 2, u))
    gathered_a = {u: gather_pieces(wires_a[u]) for u in order}
    gathered_b = [gather_pieces(w) for w in wires_b]
    bias_a = unit_vectors[:, :qv].reshape(groups, heads, 2, HD)
    bias_a = jnp.concatenate(
        [bias_a[:, :, :1], jnp.zeros_like(bias_a[:, :, :1]), bias_a[:, :, 1:]], axis=2
    ).reshape(groups, 1, wide)
    bias_b = unit_vectors[: len(wires_b), qv:]

    lane = jnp.arange(feats, dtype=jnp.int32)
    part, at = lane // half_pad, lane % half_pad
    block = jnp.minimum(at // half, fsdp - 1) ^ fi
    source = jnp.where(at < used, block * shard + (part ^ ci) * half + at % half, -1)
    place = (jnp.arange(width, dtype=jnp.int32)[:, None] == source[None, :]).astype(bf16)

    def arrange(x, index):
        x = lax.dynamic_index_in_dim(x, index, 0, keepdims=False)
        x = jnp.pad(x, ((0, rows - seq), (0, 0)))
        return jnp.einsum("rd,de->re", x, place, preferred_element_type=f32).astype(bf16)

    x = arrange(inputs, gi)
    cots = [arrange(cotangent, gi), arrange(cotangent, gi ^ 1)]
    cots_t = [c.T for c in cots]
    out_share = jnp.arange(groups * share, dtype=jnp.int32)
    out_first = ((gi ^ (out_share // share)) * sub + ti % sub) * share + out_share % share
    pick = (out_first[:, None] == source[None, :half_pad]).astype(bf16)

    xhat1, _ = standardize(x.astype(f32), width)
    xn = (xhat1 * vectors[1:2] + vectors[2:3]).astype(bf16)
    xnt = xn.T
    kept = {}
    attn = None
    for u in order:
        arrays, plan = gathered_a[u]
        found = attend(xn, bias_a[u], arrays, plan, attn, seq, heads)
        kept[u] = found[:4]
        attn = found[4]

    def other_cores(parts):
        other = tensor_swap(parts, 1)
        for bit in core_bits[1:]:
            more = tensor_swap(jnp.stack([parts, other]), bit)
            parts, other = add_low(parts, more[0]), add_low(other, more[1])
        return parts, other

    attn, attn_other = other_cores(attn)
    middle, n2_low, n2_high = by_rows(
        functools.partial(middle_kernel, width),
        [shaped((rows, feats), f32), shaped((rows, half_pad), bf16), shaped((rows, half_pad), bf16)],
        [False] * 3,
        [x, attn, attn_other, vectors],
        [False, False, False, True],
        rows,
        tile,
    )
    far_low = tensor_swap(n2_low, pair_bit)
    far_high = tensor_swap(far_low, 1)

    out0, back0, up_bias0, dw0 = mlp(n2_low, n2_high, cots[0], cots_t[0], bias_b, gathered_b, None)
    out1, back1, up_bias1, dw1 = mlp(far_low, far_high, cots[1], cots_t[1], bias_b, gathered_b, dw0)
    up_bias_g = up_bias0 + up_bias1

    def sum_cores(parts):
        low = add_low(parts[0], tensor_swap(parts[1], 1))
        for bit in core_bits[1:]:
            low = add_low(low, tensor_swap(low, bit))
        return low

    back_far = tensor_swap(sum_cores(back1), pair_bit)
    back_low = add_low(sum_cores(back0), back_far)
    back_high = tensor_swap(back_low, 1)
    middle_grad, branch_grad, sums2 = by_rows(
        functools.partial(middle_back_kernel, width),
        [shaped((rows, half_pad), f32), shaped((rows, feats), bf16), shaped((4, half_pad), f32)],
        [False, False, True],
        [back_low, back_high, middle, cots[0], vectors],
        [False, False, False, False, True],
        rows,
        tile,
    )
    grad_b = scatter_units([scatter_rows(d, shard) for d in dw1], far_bits, add_low)

    def spread(blocks):
        got = [blocks[:share]]
        for i in range(1, groups):
            got.append(tensor_swap(blocks[i * share : (i + 1) * share], i * sub))
        for i in range(len(group_bits)):
            swapped = [got[n ^ (1 << i)] for n in range(groups)]
            got = [jnp.where((gi >> i) & 1 == 1, s, g) for s, g in zip(swapped, got)]
        return jnp.stack([g.T[:seq] for g in got])

    out_far = tensor_swap(sum_cores(out1), pair_bit)
    out_half = middle[:, :half_pad] + sum_cores(out0).astype(f32) + out_far.astype(f32)
    out_half = (out_half + vectors[5:6, :half_pad]).astype(bf16)
    layer_out = spread(nt(pick, out_half).astype(bf16))

    grad_o = scatter_rows(out_grad(branch_grad, [kept[u][2] for u in range(groups)]), shard)
    grad_o = [grad_o[:, u * heads * HD : (u + 1) * heads * HD] for u in range(groups)]
    grad_o = scatter_units(grad_o, far_bits + [pair_bit], add_low)
    back = None
    grads_a = [None] * groups
    biases_a = [None] * groups
    for u in range(groups)[::-1]:
        w, qkv_t, _, lse = kept[u]
        dw, biases_a[u], back = attend_back(xnt, branch_grad, w, qkv_t, lse, back, seq, heads)
        grads_a[u] = scatter_rows(dw, shard)
    grad_a = scatter_units(grads_a, far_bits + [pair_bit], add_low)
    back, back_other = other_cores(back)
    in_shares, sums1 = by_rows_turned(
        functools.partial(first_back_kernel, width), back, back_other, x, middle_grad, vectors, pick,
        rows, tile,
    )
    input_grad = spread(in_shares).astype(f32)

    vector_g = jnp.concatenate([sums2[:1], sums1, sums2[1:]])
    qv_g = jnp.concatenate(biases_a).reshape(groups, heads, 3, HD)[:, :, ::2].reshape(groups, qv)
    unit_g = jnp.concatenate([qv_g[: len(wires_b)], up_bias_g], axis=1)
    more_qv = qv_g[len(wires_b) :]
    sizes = vector_g.size
    got = tensor_swap(jnp.concatenate([vector_g.reshape(-1), more_qv.reshape(-1)]), pair_bit)
    vector_g = vector_g + got[:sizes].reshape(vector_g.shape)
    unit_g = unit_g + jnp.pad(got[sizes:].reshape(more_qv.shape), ((0, 0), (0, units)))
    for bit in far_bits[::-1]:
        keep = unit_g.shape[0] // 2
        got = tensor_swap(jnp.concatenate([vector_g.reshape(-1), unit_g[keep:].reshape(-1)]), bit)
        vector_g = vector_g + got[:sizes].reshape(vector_g.shape)
        unit_g = unit_g[:keep] + got[sizes:].reshape(unit_g[:keep].shape)
    held = split_blocks(vector_g, 1, 0, half)
    for bit in fsdp_bits(0):
        leave = [o for o in held if o & bit]
        sent = [held.pop(o).reshape(-1) for o in leave] + [unit_g.reshape(-1)]
        got = fsdp_swap(jnp.concatenate(sent), bit)
        for n, o in enumerate(leave):
            held[o ^ bit] = held[o ^ bit] + got[n * 6 * half : (n + 1) * 6 * half].reshape(6, half)
        unit_g = unit_g + got[len(leave) * 6 * half :].reshape(unit_g.shape)
    vector_g = swap_halves(jnp.concatenate([held[0], tensor_swap(held[0], 1)], axis=1), 1)
    grad_a = swap_halves(grad_a.astype(f32), 0)
    grad_o = swap_halves(grad_o.astype(f32), 0)
    grad_b = swap_halves(grad_b.astype(f32), 0)
    return (
        layer_out,
        input_grad,
        grad_a.reshape(shard, heads, 3 * HD),
        unit_g[0, :qv].reshape(heads, 2 * HD),
        grad_o.T.reshape(heads, HD, shard),
        vector_g[0],
        vector_g[1],
        vector_g[2],
        vector_g[3],
        vector_g[4],
        grad_b[:, :units],
        unit_g[0, qv:],
        grad_b[:, units:].T,
        vector_g[5],
    )


def by_rows_turned(kernel, own, other, x, grad, vectors, pick, rows, tile):
    feats = x.shape[1]
    half = grad.shape[1]
    wide = pick.shape[0]
    cut3 = pl.BlockSpec((2, tile, half), lambda i: (0, i, 0))
    whole = lambda shape: pl.BlockSpec(shape, lambda i: (0, 0))
    return pl.pallas_call(
        kernel,
        grid=(rows // tile,),
        in_specs=[
            cut3,
            cut3,
            pl.BlockSpec((tile, feats), lambda i: (i, 0)),
            pl.BlockSpec((tile, half), lambda i: (i, 0)),
            whole(vectors.shape),
            whole(pick.shape),
        ],
        out_specs=[pl.BlockSpec((wide, tile), lambda i: (0, i)), whole((2, half))],
        out_shape=[shaped((wide, rows), bf16), shaped((2, half), f32)],
        compiler_params=pltpu.CompilerParams(vmem_limit_bytes=40 * MIB),
        cost_estimate=pl.CostEstimate(
            flops=2 * rows * half * wide, bytes_accessed=rows * feats * 12, transcendentals=0
        ),
    )(own, other, x, grad, vectors, pick)


def solution(mesh):
    return jax.shard_map(
        body,
        mesh=mesh,
        in_specs=(
            P("fsdp", None, None),
            P("fsdp", None, None),
            P("fsdp", "tensor", None),
            P("tensor", None),
            P("tensor", None, "fsdp"),
            P("fsdp"),
            P("fsdp"),
            P("fsdp"),
            P("fsdp"),
            P("fsdp"),
            P("fsdp", "tensor"),
            P("tensor"),
            P("tensor", "fsdp"),
            P("fsdp"),
        ),
        out_specs=(
            P("fsdp", None, "tensor"),
            P("fsdp", None, "tensor"),
            P("fsdp", "tensor", None),
            P("tensor", None),
            P("tensor", None, "fsdp"),
            P("fsdp"),
            P("fsdp"),
            P("fsdp"),
            P("fsdp"),
            P("fsdp"),
            P("fsdp", "tensor"),
            P("tensor"),
            P("tensor", "fsdp"),
            P("fsdp"),
        ),
        check_vma=False,
    )
```

time: 667 us -> 622 us (0.933)
  Pallas kernels: 55.2 us -> 145 us
  local copies, waits for them, and re-layouts: 147 us -> 94.9 us
  matrix products: 59.5 us -> 15.5 us
  other arithmetic: 77.2 us -> 35.9 us
  starting transfers between devices: 56.7 us -> 95.7 us
  waiting for transfers between devices: 264 us -> 228 us
    pallas_call x2 -> x14, Pallas kernels: 55.2 us -> 145 us  [the longest x11 132 us: on_chip(): pl.pallas_call(kernel, in_specs=[whole] * len(args), out_specs=[whole] *...]
    dot_general x16 -> x4, matrix products: 59.5 us -> 15.5 us  [the longest x3 12.8 us: arrange(): jnp.einsum('rd,de->re', x, place, preferred_element_type=f32).astype(bf16)]
    ppermute x26 -> x56, waiting for transfers between devices: 147 us -> 111 us  [fsdp_swap(): return lax.ppermute(x, 'fsdp', [(i, i ^ bit) for i in range(size)])]
    ppermute x26 -> x56, starting transfers between devices: 28.8 us -> 60.2 us  [fsdp_swap(): return lax.ppermute(x, 'fsdp', [(i, i ^ bit) for i in range(size)])]
    unnamed x120 -> x119, local copies, waits for them, and re-layouts: 40.7 us -> 18.1 us
    concatenate x8 -> x9, local copies, waits for them, and re-layouts: 24.4 us -> 8.93 us  [the longest x7 8.76 us: scatter_rows(): got = fsdp_swap(jnp.concatenate([held.pop(o) for o in leave], axis=0), bit)]
    ppermute x6 -> x0, local copies, waits for them, and re-layouts: 12.7 us -> none  [the longest x4 8.93 us: fsdp_swap(): return lax.ppermute(x, 'fsdp', [(i, i ^ bit) for i in range(size)])]
    reduce_sum x5 -> x0, other arithmetic: 11.1 us -> none  [the longest x1 4.68 us: body(): shift1_g = jnp.sum(n1_grad, axis=0)]
  transfers between devices with their start and end apart: 54 -> 89, of which waited for: 22 -> 35; matrix products, arithmetic and copies ran while one was open for 35% -> 18% of each run, Pallas kernels for 8% -> 14%
where the time goes in v2:
time: 622 us; the launch traced here: 617 us
  waiting for transfers between devices  228 us (37%)
  Pallas kernels  145 us (23%)
  starting transfers between devices  95.7 us (15%)
  local copies, waits for them, and re-layouts  94.9 us (15%)
  other arithmetic  35.9 us (6%)
  matrix products  15.5 us (2%)
    pallas_call x11, Pallas kernels, on_chip(): pl.pallas_call(kernel, in_specs=[whole] * len(args), out_specs=[whole] *...  132 us
    ppermute x33, waiting for transfers between devices, tensor_swap(): return lax.ppermute(x, 'tensor', [(i, i ^ bit) for i in range(size)])  117 us
    ppermute x56, waiting for transfers between devices, fsdp_swap(): return lax.ppermute(x, 'fsdp', [(i, i ^ bit) for i in range(size)])  111 us
    ppermute x56, starting transfers between devices, fsdp_swap(): return lax.ppermute(x, 'fsdp', [(i, i ^ bit) for i in range(size)])  60.2 us
    ppermute x33, starting transfers between devices, tensor_swap(): return lax.ppermute(x, 'tensor', [(i, i ^ bit) for i in range(size)])  35.6 us
    convert_element_type x26, other arithmetic, add_low(): return (a.astype(f32) + b.astype(f32)).astype(bf16)  18.9 us
    unnamed x119, local copies, waits for them, and re-layouts  18.1 us
    dynamic_slice x1, local copies, waits for them, and re-layouts, arrange(): x = lax.dynamic_index_in_dim(x, index, 0, keepdims=False)  15.9 us
  transfers between devices with their start and end apart: 89, of which 35 were waited for; matrix products, arithmetic and copies ran while one was open for 18% of the time, Pallas kernels for 14%

profile of v2, /device:TPU:0, one launch (start us, length us, event | category | flops | bytes accessed | tf_op | source)
XLA Modules:
  0.0 617.0 jit_solution(3672607065189393165)
XLA Ops:
  12.3 15.9 %constant_dynamic-slice_fusion.1 = (bf16[1,729,1152]{2,0,1:T(2,128)(2,1)}, bf16[1,729,1152]{2,0,1:T(2,128)(2,1)}, bf16[1,729,1152]{2,0,1:T(2,128)(2,1)S(1)}) fusion(bf16[4,729,1152]{2,0,1:T(4,128)(2,1)} %param.15, s32[]{:T(128)S(6)} %select_n.247, s32[]{:T(128)S(6)} %select_n.257, bf16[4,729,1152]{2,0,1:T(4,128)(2,1)} %param.14), kind=kLoop, calls=%fused_computation.259 | loop fusion | bytes 10077704 | tf_op jit(solution)/shard_map/jit(dynamic_index_in_dim)/dynamic_slice | solution.py:524
  29.9 4.4 convert_reduce_fusion
  50.6 6.8 %collective-permute-done.15.refs_3_ = bf16[288,576]{1,0:T(8,128)(2,1)S(1)} collective-permute-done((bf16[288,576]{1,0:T(8,128)(2,1)}, bf16[288,576]{1,0:T(8,128)(2,1)S(1)}, u32[]{:S(2)}, u32[]{:S(2)}) %collective-permute-start.15) | collective-permute-done | bytes 331808 | tf_op jit(solution)/shard_map/ppermute | solution.py:52
  70.3 7.0 %shard_map.245 = (bf16[1280,576]{1,0:T(8,128)(2,1)}, bf16[432,768]{1,0:T(8,128)(2,1)}, bf16[768,144]{1,0:T(8,128)(2,1)}, f32[2,768]{1,0:T(2,128)}, bf16[2,768,640]{2,1,0:T(8,128)(2,1)}) custom-call(bf16[768,1280]{1,0:T(8,128)(2,1)} %fusion.6.refs_0_, f32[1,432]{1,0:T(1,128)} %squeeze.63.refs_1_, bf16[288,576]{1,0:T(8,128)(2,1)} %copy-done.22, ...), custom_call_target="tpu_custom_call" | custom-call | flops 2340421632 | bytes 7626432 | tf_op jit(solution)/shard_map/pallas_call | solution.py:39
  80.0 8.1 %shard_map.246 = (bf16[1280,576]{1,0:T(8,128)(2,1)}, bf16[432,768]{1,0:T(8,128)(2,1)}, bf16[768,144]{1,0:T(8,128)(2,1)}, f32[2,768]{1,0:T(2,128)}, bf16[2,768,640]{2,1,0:T(8,128)(2,1)}) custom-call(bf16[768,1280]{1,0:T(8,128)(2,1)} %fusion.6.refs_0_, f32[1,432]{1,0:T(1,128)} %squeeze.62.refs_1_, bf16[288,576]{1,0:T(8,128)(2,1)} %collective-permute-done.14.refs_2_, ...), custom_call_target="tpu_custom_call" | custom-call | flops 2340421632 | bytes 9592512 | tf_op jit(solution)/shard_map/pallas_call | solution.py:39
  91.5 7.6 %shard_map.247 = (bf16[1280,576]{1,0:T(8,128)(2,1)}, bf16[432,768]{1,0:T(8,128)(2,1)}, bf16[768,144]{1,0:T(8,128)(2,1)}, f32[2,768]{1,0:T(2,128)}, bf16[2,768,640]{2,1,0:T(8,128)(2,1)}) custom-call(bf16[768,1280]{1,0:T(8,128)(2,1)} %fusion.6.refs_0_, f32[1,432]{1,0:T(1,128)} %squeeze.61.refs_1_, bf16[288,576]{1,0:T(8,128)(2,1)} %collective-permute-done.4.refs_2_, ...), custom_call_target="tpu_custom_call" | custom-call | flops 2340421632 | bytes 9592512 | tf_op jit(solution)/shard_map/pallas_call | solution.py:39
  99.8 7.8 %shard_map.248 = (bf16[1280,576]{1,0:T(8,128)(2,1)}, bf16[432,768]{1,0:T(8,128)(2,1)}, bf16[768,144]{1,0:T(8,128)(2,1)}, f32[2,768]{1,0:T(2,128)}, bf16[2,768,640]{2,1,0:T(8,128)(2,1)}) custom-call(bf16[768,1280]{1,0:T(8,128)(2,1)} %fusion.6.refs_0_, f32[1,432]{1,0:T(1,128)} %squeeze.60.refs_1_, bf16[288,576]{1,0:T(8,128)(2,1)} %collective-permute-done.5.refs_2_, ...), custom_call_target="tpu_custom_call" | custom-call | flops 2340421632 | bytes 9592512 | tf_op jit(solution)/shard_map/pallas_call | solution.py:39
  119.6 20.8 %collective-permute-done.28.refs_10_ = bf16[288,1076]{1,0:T(8,128)(2,1)} collective-permute-done((bf16[288,1076]{1,0:T(8,128)(2,1)S(1)}, bf16[288,1076]{1,0:T(8,128)(2,1)}, u32[]{:S(2)}, u32[]{:S(2)}) %collective-permute-start.28) | collective-permute-done | bytes 619808 | tf_op jit(solution)/shard_map/ppermute | solution.py:57
  155.8 4.4 shard_map.249
  180.0 6.7 %collective-permute-done.34.refs_0_ = bf16[768,640]{1,0:T(8,128)(2,1)} collective-permute-done((bf16[768,640]{1,0:T(8,128)(2,1)}, bf16[768,640]{1,0:T(8,128)(2,1)}, u32[]{:S(2)}, u32[]{:S(2)}) %collective-permute-start.34) | collective-permute-done | bytes 983072 | tf_op jit(solution)/shard_map/ppermute | solution.py:57
  186.7 24.8 %shard_map.250 = (bf16[2,768,640]{2,1,0:T(8,128)(2,1)}, bf16[2,768,640]{2,1,0:T(8,128)(2,1)}, f32[2,538]{1,0:T(2,128)}, bf16[1280,1076]{1,0:T(8,128)(2,1)}, bf16[1280,1076]{1,0:T(8,128)(2,1)}) custom-call(bf16[768,640]{1,0:T(8,128)(2,1)} %get-tuple-element.69.refs_0_, bf16[768,640]{1,0:T(8,128)(2,1)} %copy-done.9, bf16[768,1280]{1,0:T(8,128)(2,1)} %fusion.9.refs_2_.cot_ref, ...), custom_call_target="tpu_custom_call" | custom-call | flops 12693012480 | bytes 20306336 | tf_op jit(solution)/shard_map/pallas_call | solution.py:39
  215.5 26.9 %shard_map.251 = (bf16[2,768,640]{2,1,0:T(8,128)(2,1)}, bf16[2,768,640]{2,1,0:T(8,128)(2,1)}, f32[2,538]{1,0:T(2,128)}, bf16[1280,1076]{1,0:T(8,128)(2,1)}, bf16[1280,1076]{1,0:T(8,128)(2,1)}) custom-call(bf16[768,640]{1,0:T(8,128)(2,1)} %collective-permute-done.34.refs_0_, bf16[768,640]{1,0:T(8,128)(2,1)} %collective-permute-done.35.refs_1_, ...), custom_call_target="tpu_custom_call" | custom-call | flops 12693012480 | bytes 25815456 | tf_op jit(solution)/shard_map/pallas_call | solution.py:39
  250.9 11.8 %collective-permute-done.84 = bf16[288,1076]{1,0:T(8,128)(2,1)S(1)} collective-permute-done((bf16[288,1076]{1,0:T(8,128)(2,1)S(1)}, bf16[288,1076]{1,0:T(8,128)(2,1)S(1)}, u32[]{:S(2)}, u32[]{:S(2)}) %collective-permute-start.84) | collective-permute-done | bytes 619808 | tf_op jit(solution)/shard_map/ppermute | solution.py:52
  264.0 12.6 %collective-permute-done.80 = bf16[288,1076]{1,0:T(8,128)(2,1)S(1)} collective-permute-done((bf16[288,1076]{1,0:T(8,128)(2,1)S(1)}, bf16[288,1076]{1,0:T(8,128)(2,1)S(1)}, u32[]{:S(2)}, u32[]{:S(2)}) %collective-permute-start.80) | collective-permute-done | bytes 619808 | tf_op jit(solution)/shard_map/ppermute | solution.py:52
  278.9 7.1 %collective-permute-done.85 = bf16[144,1076]{1,0:T(8,128)(2,1)S(1)} collective-permute-done((bf16[144,1076]{1,0:T(8,128)(2,1)S(1)}, bf16[144,1076]{1,0:T(8,128)(2,1)S(1)}, u32[]{:S(2)}, u32[]{:S(2)}) %collective-permute-start.85) | collective-permute-done | bytes 309920 | tf_op jit(solution)/shard_map/ppermute | solution.py:52
  287.4 7.1 %collective-permute-done.81 = bf16[144,1076]{1,0:T(8,128)(2,1)S(1)} collective-permute-done((bf16[144,1076]{1,0:T(8,128)(2,1)S(1)}, bf16[144,1076]{1,0:T(8,128)(2,1)S(1)}, u32[]{:S(2)}, u32[]{:S(2)}) %collective-permute-start.81) | collective-permute-done | bytes 309920 | tf_op jit(solution)/shard_map/ppermute | solution.py:52
  297.1 8.2 %collective-permute-done.87 = bf16[144,1076]{1,0:T(8,128)(2,1)S(1)} collective-permute-done((bf16[144,1076]{1,0:T(8,128)(2,1)S(1)}, bf16[144,1076]{1,0:T(8,128)(2,1)S(1)}, u32[]{:S(2)}, u32[]{:S(2)}) %collective-permute-start.87) | collective-permute-done | bytes 309920 | tf_op jit(solution)/shard_map/ppermute | solution.py:52
  309.7 32.3 %collective-permute-done.88 = bf16[288,1076]{1,0:T(8,128)(2,1)S(1)} collective-permute-done((bf16[288,1076]{1,0:T(8,128)(2,1)S(1)}, bf16[288,1076]{1,0:T(8,128)(2,1)S(1)}, u32[]{:S(2)}, u32[]{:S(2)}) %collective-permute-start.88) | collective-permute-done | bytes 619808 | tf_op jit(solution)/shard_map/ppermute | solution.py:57
  343.6 14.5 %collective-permute-done.37 = bf16[768,640]{1,0:T(8,128)(2,1)S(1)} collective-permute-done((bf16[768,640]{1,0:T(8,128)(2,1)S(1)}, bf16[768,640]{1,0:T(8,128)(2,1)S(1)}, u32[]{:S(2)}, u32[]{:S(2)}) %collective-permute-start.37) | collective-permute-done | bytes 983072 | tf_op jit(solution)/shard_map/ppermute | solution.py:57
  371.1 9.5 %collective-permute-done.39 = bf16[144,768]{1,0:T(8,128)(2,1)S(1)} collective-permute-done((bf16[144,768]{1,0:T(8,128)(2,1)S(1)}, bf16[144,768]{1,0:T(8,128)(2,1)S(1)}, u32[]{:S(2)}, u32[]{:S(2)}) %collective-permute-start.39) | collective-permute-done | bytes 221216 | tf_op jit(solution)/shard_map/ppermute | solution.py:57
  389.3 5.1 shard_map.258
  397.2 10.7 %shard_map.253 = (bf16[1280,432]{1,0:T(8,128)(2,1)}, f32[1,432]{1,0:T(1,128)}, bf16[2,768,640]{2,1,0:T(8,128)(2,1)}) custom-call(bf16[1280,768]{1,0:T(8,128)(2,1)} %copy.47.refs_0_, bf16[768,1280]{1,0:T(8,128)(2,1)} %copy-done.6, bf16[1280,576]{1,0:T(8,128)(2,1)} %get-tuple-element.87.refs_2_, bf16[432,768]{1,0:T(8,128)(2,1)} %get-tuple-element.88.refs_3_, ...), custom_call_target="tpu_custom_call" | custom-call | flops 4718592000 | bytes 9150144 | tf_op jit(solution)/shard_map/pallas_call | solution.py:39
  407.8 11.5 %shard_map.254 = (bf16[1280,432]{1,0:T(8,128)(2,1)}, f32[1,432]{1,0:T(1,128)}, bf16[2,768,640]{2,1,0:T(8,128)(2,1)}) custom-call(bf16[1280,768]{1,0:T(8,128)(2,1)} %copy.47.refs_0_, bf16[768,1280]{1,0:T(8,128)(2,1)} %copy-done.6, bf16[1280,576]{1,0:T(8,128)(2,1)} %get-tuple-element.84.refs_2_, bf16[432,768]{1,0:T(8,128)(2,1)} %get-tuple-element.85.refs_3_, ...), custom_call_target="tpu_custom_call" | custom-call | flops 4718592000 | bytes 11116224 | tf_op jit(solution)/shard_map/pallas_call | solution.py:39
  419.3 11.3 %shard_map.255 = (bf16[1280,432]{1,0:T(8,128)(2,1)}, f32[1,432]{1,0:T(1,128)}, bf16[2,768,640]{2,1,0:T(8,128)(2,1)}) custom-call(bf16[1280,768]{1,0:T(8,128)(2,1)} %copy.47.refs_0_, bf16[768,1280]{1,0:T(8,128)(2,1)} %copy-done.6, bf16[1280,576]{1,0:T(8,128)(2,1)} %get-tuple-element.81.refs_2_, bf16[432,768]{1,0:T(8,128)(2,1)} %get-tuple-element.82.refs_3_, ...), custom_call_target="tpu_custom_call" | custom-call | flops 4718592000 | bytes 11116224 | tf_op jit(solution)/shard_map/pallas_call | solution.py:39
  430.6 11.5 %shard_map.256 = (bf16[1280,432]{1,0:T(8,128)(2,1)}, f32[1,432]{1,0:T(1,128)}, bf16[2,768,640]{2,1,0:T(8,128)(2,1)}) custom-call(bf16[1280,768]{1,0:T(8,128)(2,1)} %copy.47.refs_0_, bf16[768,1280]{1,0:T(8,128)(2,1)} %copy-done.6, bf16[1280,576]{1,0:T(8,128)(2,1)} %get-tuple-element.78.refs_2_, bf16[432,768]{1,0:T(8,128)(2,1)} %get-tuple-element.79.refs_3_, ...), custom_call_target="tpu_custom_call" | custom-call | flops 4718592000 | bytes 11116224 | tf_op jit(solution)/shard_map/pallas_call | solution.py:39
  470.6 10.9 %collective-permute-done.49 = bf16[288,432]{1,0:T(8,128)(2,1)S(1)} collective-permute-done((bf16[288,432]{1,0:T(8,128)(2,1)S(1)}, bf16[288,432]{1,0:T(8,128)(2,1)S(1)}, u32[]{:S(2)}, u32[]{:S(2)}) %collective-permute-start.49) | collective-permute-done | bytes 248864 | tf_op jit(solution)/shard_map/ppermute | solution.py:52
  504.9 8.2 %collective-permute-done.50 = bf16[144,432]{1,0:T(8,128)(2,1)S(1)} collective-permute-done((bf16[144,432]{1,0:T(8,128)(2,1)S(1)}, bf16[144,432]{1,0:T(8,128)(2,1)S(1)}, u32[]{:S(2)}, u32[]{:S(2)}) %collective-permute-start.50) | collective-permute-done | bytes 124448 | tf_op jit(solution)/shard_map/ppermute | solution.py:52
  516.3 6.3 %collective-permute-done.54 = bf16[144,432]{1,0:T(8,128)(2,1)S(1)} collective-permute-done((bf16[144,432]{1,0:T(8,128)(2,1)S(1)}, bf16[144,432]{1,0:T(8,128)(2,1)S(1)}, u32[]{:S(2)}, u32[]{:S(2)}) %collective-permute-start.54) | collective-permute-done | bytes 124448 | tf_op jit(solution)/shard_map/ppermute | solution.py:52
  525.7 6.3 %collective-permute-done.59 = bf16[144,432]{1,0:T(8,128)(2,1)S(1)} collective-permute-done((bf16[144,432]{1,0:T(8,128)(2,1)S(1)}, bf16[144,432]{1,0:T(8,128)(2,1)S(1)}, u32[]{:S(2)}, u32[]{:S(2)}) %collective-permute-start.59) | collective-permute-done | bytes 124448 | tf_op jit(solution)/shard_map/ppermute | solution.py:52
  557.1 10.7 %collective-permute-done.77 = bf16[288,144]{1,0:T(8,128)(2,1)S(1)} collective-permute-done((bf16[288,144]{1,0:T(8,128)(2,1)S(1)}, bf16[288,144]{1,0:T(8,128)(2,1)S(1)}, u32[]{:S(2)}, u32[]{:S(2)}) %collective-permute-start.77) | collective-permute-done | bytes 82976 | tf_op jit(solution)/shard_map/ppermute | solution.py:57
  577.5 5.1 shard_map.257
  608.7 6.3 %collective-permute-done.47 = bf16[144,768]{1,0:T(8,128)(2,1)S(1)} collective-permute-done((bf16[144,768]{1,0:T(8,128)(2,1)S(1)}, bf16[144,768]{1,0:T(8,128)(2,1)S(1)}, u32[]{:S(2)}, u32[]{:S(2)}) %collective-permute-start.47) | collective-permute-done | bytes 221216 | tf_op jit(solution)/shard_map/ppermute | solution.py:57
  (472 shorter events, 266.6 us)
Async XLA Ops:
  3.1 44.4 %collective-permute-start.19 = (bf16[288,576]{1,0:T(8,128)(2,1)S(1)}, bf16[288,576]{1,0:T(8,128)(2,1)S(1)}, u32[]{:S(2)}, u32[]{:S(2)}) collective-permute-start(bf16[288,576]{1,0:T(8,128)(2,1)S(1)} %pad_maximum_fusion.7.refs_2_), channel_id=1, source_target_pairs={{0,8},{8,0},{16,24},{24,16},{1,9},{9,1},{17,25},{25,17},{2,10},{10... | collective-permute-start | bytes 995336 | tf_op jit(solution)/shard_map/ppermute | solution.py:52
  6.1 42.4 %collective-permute-start.20 = (bf16[288,576]{1,0:T(8,128)(2,1)S(1)}, bf16[288,576]{1,0:T(8,128)(2,1)S(1)}, u32[]{:S(2)}, u32[]{:S(2)}) collective-permute-start(bf16[288,576]{1,0:T(8,128)(2,1)S(1)} %pad_maximum_fusion.7.refs_2_), channel_id=1, source_target_pairs={{0,16},{8,24},{16,0},{24,8},{1,17},{9,25},{17,1},{25,9},{2,18},{10... | collective-permute-start | bytes 995336 | tf_op jit(solution)/shard_map/ppermute | solution.py:52
  7.6 38.0 %collective-permute-start.14 = (bf16[288,576]{1,0:T(8,128)(2,1)S(1)}, bf16[288,576]{1,0:T(8,128)(2,1)}, u32[]{:S(2)}, u32[]{:S(2)}) collective-permute-start(bf16[288,576]{1,0:T(8,128)(2,1)S(1)} %pad_maximum_fusion.7.refs_2_), channel_id=1, source_target_pairs={{0,2},{1,3},{2,0},{3,1},{4,6},{5,7},{6,4},{7,5},{8,10},{9,11},{10,... | collective-permute-start | bytes 995336 | tf_op jit(solution)/shard_map/ppermute | solution.py:57
  9.2 40.9 %collective-permute-start.4 = (bf16[288,576]{1,0:T(8,128)(2,1)S(1)}, bf16[288,576]{1,0:T(8,128)(2,1)}, u32[]{:S(2)}, u32[]{:S(2)}) collective-permute-start(bf16[288,576]{1,0:T(8,128)(2,1)S(1)} %pad_maximum_fusion.7.refs_2_), channel_id=1, source_target_pairs={{0,4},{1,5},{2,6},{3,7},{4,0},{5,1},{6,2},{7,3},{8,12},{9,13},{10,... | collective-permute-start | bytes 995336 | tf_op jit(solution)/shard_map/ppermute | solution.py:57
  11.9 22.5 %collective-permute-start.2 = (bf16[1,826]{1,0:T(2,128)(2,1)S(1)}, bf16[1,826]{1,0:T(2,128)(2,1)S(1)}, u32[]{:S(2)}, u32[]{:S(2)}) collective-permute-start(bf16[1,826]{1,0:T(2,128)(2,1)S(1)} %broadcast_in_dim.9), channel_id=1, source_target_pairs={{0,4},{1,5},{2,6},{3,7},{4,0},{5,1},{6,2},{7,3},{8,12},{9,13},{10,... | collective-permute-start | bytes 4964 | tf_op jit(solution)/shard_map/ppermute | solution.py:57
  50.1 19.1 %collective-permute-start.10 = (bf16[288,576]{1,0:T(8,128)(2,1)}, bf16[288,576]{1,0:T(8,128)(2,1)S(1)}, u32[]{:S(2)}, u32[]{:S(2)}) collective-permute-start(bf16[288,576]{1,0:T(8,128)(2,1)} %collective-permute-done.4.refs_2_), channel_id=1, source_target_pairs={{0,8},{8,0},{16,24},{24,16},{1,9},{9,1},{17,25},{25,17},{2,10},{10... | collective-permute-start | bytes 995336 | tf_op jit(solution)/shard_map/ppermute | solution.py:52
  57.3 20.0 %collective-permute-start.11 = (bf16[288,576]{1,0:T(8,128)(2,1)}, bf16[288,576]{1,0:T(8,128)(2,1)}, u32[]{:S(2)}, u32[]{:S(2)}) collective-permute-start(bf16[288,576]{1,0:T(8,128)(2,1)} %collective-permute-done.4.refs_2_), channel_id=1, source_target_pairs={{0,16},{8,24},{16,0},{24,8},{1,17},{9,25},{17,1},{25,9},{2,18},{10... | collective-permute-start | bytes 995336 | tf_op jit(solution)/shard_map/ppermute | solution.py:52
  66.3 21.8 %collective-permute-start.6 = (bf16[288,576]{1,0:T(8,128)(2,1)}, bf16[288,576]{1,0:T(8,128)(2,1)S(1)}, u32[]{:S(2)}, u32[]{:S(2)}) collective-permute-start(bf16[288,576]{1,0:T(8,128)(2,1)} %collective-permute-done.5.refs_2_), channel_id=1, source_target_pairs={{0,8},{8,0},{16,24},{24,16},{1,9},{9,1},{17,25},{25,17},{2,10},{10... | collective-permute-start | bytes 995336 | tf_op jit(solution)/shard_map/ppermute | solution.py:52
  69.2 20.1 %collective-permute-start.7 = (bf16[288,576]{1,0:T(8,128)(2,1)}, bf16[288,576]{1,0:T(8,128)(2,1)S(1)}, u32[]{:S(2)}, u32[]{:S(2)}) collective-permute-start(bf16[288,576]{1,0:T(8,128)(2,1)} %collective-permute-done.5.refs_2_), channel_id=1, source_target_pairs={{0,16},{8,24},{16,0},{24,8},{1,17},{9,25},{17,1},{25,9},{2,18},{10... | collective-permute-start | bytes 995336 | tf_op jit(solution)/shard_map/ppermute | solution.py:52
  107.6 46.6 %collective-permute-start.23 = (bf16[2,768,640]{2,1,0:T(8,128)(2,1)}, bf16[2,768,640]{2,1,0:T(8,128)(2,1)}, u32[]{:S(2)}, u32[]{:S(2)}) collective-permute-start(bf16[2,768,640]{2,1,0:T(8,128)(2,1)} %get-tuple-element.67.own_ref), channel_id=1, source_target_pairs={{0,1},{1,0},{2,3},{3,2},{4,5},{5,4},{6,7},{7,6},{8,9},{9,8},{10,11... | collective-permute-start | bytes 5898248 | tf_op jit(solution)/shard_map/ppermute | solution.py:57
  108.0 32.5 %collective-permute-start.28 = (bf16[288,1076]{1,0:T(8,128)(2,1)S(1)}, bf16[288,1076]{1,0:T(8,128)(2,1)}, u32[]{:S(2)}, u32[]{:S(2)}) collective-permute-start(bf16[288,1076]{1,0:T(8,128)(2,1)S(1)} %pad_maximum_fusion.2.refs_5_), channel_id=1, source_target_pairs={{0,4},{1,5},{2,6},{3,7},{4,0},{5,1},{6,2},{7,3},{8,12},{9,13},{10,... | collective-permute-start | bytes 1859336 | tf_op jit(solution)/shard_map/ppermute | solution.py:57
  110.6 53.5 %collective-permute-start.24 = (bf16[288,1076]{1,0:T(8,128)(2,1)S(1)}, bf16[288,1076]{1,0:T(8,128)(2,1)}, u32[]{:S(2)}, u32[]{:S(2)}) collective-permute-start(bf16[288,1076]{1,0:T(8,128)(2,1)S(1)} %pad_maximum_fusion.2.refs_5_), channel_id=1, source_target_pairs={{0,8},{8,0},{16,24},{24,16},{1,9},{9,1},{17,25},{25,17},{2,10},{10... | collective-permute-start | bytes 1859336 | tf_op jit(solution)/shard_map/ppermute | solution.py:52
  111.3 55.7 %collective-permute-start.25 = (bf16[288,1076]{1,0:T(8,128)(2,1)S(1)}, bf16[288,1076]{1,0:T(8,128)(2,1)}, u32[]{:S(2)}, u32[]{:S(2)}) collective-permute-start(bf16[288,1076]{1,0:T(8,128)(2,1)S(1)} %pad_maximum_fusion.2.refs_5_), channel_id=1, source_target_pairs={{0,16},{8,24},{16,0},{24,8},{1,17},{9,25},{17,1},{25,9},{2,18},{10... | collective-permute-start | bytes 1859336 | tf_op jit(solution)/shard_map/ppermute | solution.py:52
  140.5 28.9 %collective-permute-start.29 = (bf16[288,1076]{1,0:T(8,128)(2,1)}, bf16[288,1076]{1,0:T(8,128)(2,1)}, u32[]{:S(2)}, u32[]{:S(2)}) collective-permute-start(bf16[288,1076]{1,0:T(8,128)(2,1)} %collective-permute-done.28.refs_10_), channel_id=1, source_target_pairs={{0,8},{8,0},{16,24},{24,16},{1,9},{9,1},{17,25},{25,17},{2,10},{10... | collective-permute-start | bytes 1859336 | tf_op jit(solution)/shard_map/ppermute | solution.py:52
  141.1 30.3 %collective-permute-start.30 = (bf16[288,1076]{1,0:T(8,128)(2,1)}, bf16[288,1076]{1,0:T(8,128)(2,1)}, u32[]{:S(2)}, u32[]{:S(2)}) collective-permute-start(bf16[288,1076]{1,0:T(8,128)(2,1)} %collective-permute-done.28.refs_10_), channel_id=1, source_target_pairs={{0,16},{8,24},{16,0},{24,8},{1,17},{9,25},{17,1},{25,9},{2,18},{10... | collective-permute-start | bytes 1859336 | tf_op jit(solution)/shard_map/ppermute | solution.py:52
  163.2 23.5 %collective-permute-start.34 = (bf16[768,640]{1,0:T(8,128)(2,1)}, bf16[768,640]{1,0:T(8,128)(2,1)}, u32[]{:S(2)}, u32[]{:S(2)}) collective-permute-start(bf16[768,640]{1,0:T(8,128)(2,1)} %get-tuple-element.69.refs_0_), channel_id=1, source_target_pairs={{0,2},{1,3},{2,0},{3,1},{4,6},{5,7},{6,4},{7,5},{8,10},{9,11},{10,... | collective-permute-start | bytes 2949128 | tf_op jit(solution)/shard_map/ppermute | solution.py:57
  165.8 20.9 %collective-permute-start.26 = (bf16[144,1076]{1,0:T(8,128)(2,1)}, bf16[144,1076]{1,0:T(8,128)(2,1)}, u32[]{:S(2)}, u32[]{:S(2)}) collective-permute-start(bf16[144,1076]{1,0:T(8,128)(2,1)} %slice.746), channel_id=1, source_target_pairs={{0,16},{8,24},{16,0},{24,8},{1,17},{9,25},{17,1},{25,9},{2,18},{10... | collective-permute-start | bytes 929672 | tf_op jit(solution)/shard_map/ppermute | solution.py:52
  186.7 28.8 %collective-permute-start.35 = (bf16[768,640]{1,0:T(8,128)(2,1)}, bf16[768,640]{1,0:T(8,128)(2,1)}, u32[]{:S(2)}, u32[]{:S(2)}) collective-permute-start(bf16[768,640]{1,0:T(8,128)(2,1)} %collective-permute-done.34.refs_0_), channel_id=1, source_target_pairs={{0,1},{1,0},{2,3},{3,2},{4,5},{5,4},{6,7},{7,6},{8,9},{9,8},{10,11... | collective-permute-start | bytes 2949128 | tf_op jit(solution)/shard_map/ppermute | solution.py:57
  213.9 151.4 %collective-permute-start.41 = (bf16[768,640]{1,0:T(8,128)(2,1)}, bf16[768,640]{1,0:T(8,128)(2,1)}, u32[]{:S(2)}, u32[]{:S(2)}) collective-permute-start(bf16[768,640]{1,0:T(8,128)(2,1)} %slice_bitcast_fusion.1), channel_id=1, source_target_pairs={{0,1},{1,0},{2,3},{3,2},{4,5},{5,4},{6,7},{7,6},{8,9},{9,8},{10,11... | collective-permute-start | bytes 2949128 | tf_op jit(solution)/shard_map/ppermute | solution.py:57
  215.4 128.1 %collective-permute-start.33 = (bf16[768,640]{1,0:T(8,128)(2,1)}, bf16[768,640]{1,0:T(8,128)(2,1)}, u32[]{:S(2)}, u32[]{:S(2)}) collective-permute-start(bf16[768,640]{1,0:T(8,128)(2,1)} %slice_bitcast_fusion.3), channel_id=1, source_target_pairs={{0,1},{1,0},{2,3},{3,2},{4,5},{5,4},{6,7},{7,6},{8,9},{9,8},{10,11... | collective-permute-start | bytes 2949128 | tf_op jit(solution)/shard_map/ppermute | solution.py:57
  246.6 30.0 %collective-permute-start.80 = (bf16[288,1076]{1,0:T(8,128)(2,1)S(1)}, bf16[288,1076]{1,0:T(8,128)(2,1)S(1)}, u32[]{:S(2)}, u32[]{:S(2)}) collective-permute-start(bf16[288,1076]{1,0:T(8,128)(2,1)S(1)} %pad_maximum_fusion.3), channel_id=1, source_target_pairs={{0,8},{8,0},{16,24},{24,16},{1,9},{9,1},{17,25},{25,17},{2,10},{10... | collective-permute-start | bytes 1859336 | tf_op jit(solution)/shard_map/ppermute | solution.py:52
  247.3 40.0 %collective-permute-start.82 = (bf16[288,1076]{1,0:T(8,128)(2,1)S(1)}, bf16[288,1076]{1,0:T(8,128)(2,1)S(1)}, u32[]{:S(2)}, u32[]{:S(2)}) collective-permute-start(bf16[288,1076]{1,0:T(8,128)(2,1)S(1)} %concatenate.163), channel_id=1, source_target_pairs={{0,16},{8,24},{16,0},{24,8},{1,17},{9,25},{17,1},{25,9},{2,18},{10... | collective-permute-start | bytes 1859336 | tf_op jit(solution)/shard_map/ppermute | solution.py:52
  305.3 60.0 %collective-permute-start.43 = (bf16[768,640]{1,0:T(8,128)(2,1)S(1)}, bf16[768,640]{1,0:T(8,128)(2,1)S(1)}, u32[]{:S(2)}, u32[]{:S(2)}) collective-permute-start(bf16[768,640]{1,0:T(8,128)(2,1)S(1)} %fusion.14), channel_id=1, source_target_pairs={{0,2},{1,3},{2,0},{3,1},{4,6},{5,7},{6,4},{7,5},{8,10},{9,11},{10,... | collective-permute-start | bytes 2949128 | tf_op jit(solution)/shard_map/ppermute | solution.py:57
  305.7 36.2 %collective-permute-start.88 = (bf16[288,1076]{1,0:T(8,128)(2,1)S(1)}, bf16[288,1076]{1,0:T(8,128)(2,1)S(1)}, u32[]{:S(2)}, u32[]{:S(2)}) collective-permute-start(bf16[288,1076]{1,0:T(8,128)(2,1)S(1)} %pad_maximum_fusion.5), channel_id=1, source_target_pairs={{0,4},{1,5},{2,6},{3,7},{4,0},{5,1},{6,2},{7,3},{8,12},{9,13},{10,... | collective-permute-start | bytes 1859336 | tf_op jit(solution)/shard_map/ppermute | solution.py:57
  309.3 48.8 %collective-permute-start.37 = (bf16[768,640]{1,0:T(8,128)(2,1)S(1)}, bf16[768,640]{1,0:T(8,128)(2,1)S(1)}, u32[]{:S(2)}, u32[]{:S(2)}) collective-permute-start(bf16[768,640]{1,0:T(8,128)(2,1)S(1)} %fusion.16), channel_id=1, source_target_pairs={{0,2},{1,3},{2,0},{3,1},{4,6},{5,7},{6,4},{7,5},{8,10},{9,11},{10,... | collective-permute-start | bytes 2949128 | tf_op jit(solution)/shard_map/ppermute | solution.py:57
  455.1 120.9 %collective-permute-start.45 = (bf16[2,768,640]{2,1,0:T(8,128)(2,1)}, bf16[2,768,640]{2,1,0:T(8,128)(2,1)}, u32[]{:S(2)}, u32[]{:S(2)}) collective-permute-start(bf16[2,768,640]{2,1,0:T(8,128)(2,1)} %get-tuple-element.93.own_ref), channel_id=1, source_target_pairs={{0,1},{1,0},{2,3},{3,2},{4,5},{5,4},{6,7},{7,6},{8,9},{9,8},{10,11... | collective-permute-start | bytes 5898248 | tf_op jit(solution)/shard_map/ppermute | solution.py:57
  463.7 38.1 %collective-permute-start.72 = (bf16[288,576]{1,0:T(8,128)(2,1)S(1)}, bf16[288,576]{1,0:T(8,128)(2,1)S(1)}, u32[]{:S(2)}, u32[]{:S(2)}) collective-permute-start(bf16[288,576]{1,0:T(8,128)(2,1)S(1)} %pad_maximum_fusion.8), channel_id=1, source_target_pairs={{0,8},{8,0},{16,24},{24,16},{1,9},{9,1},{17,25},{25,17},{2,10},{10... | collective-permute-start | bytes 995336 | tf_op jit(solution)/shard_map/ppermute | solution.py:52
  464.8 72.5 %collective-permute-start.74 = (bf16[288,576]{1,0:T(8,128)(2,1)}, bf16[288,576]{1,0:T(8,128)(2,1)S(1)}, u32[]{:S(2)}, u32[]{:S(2)}) collective-permute-start(bf16[288,576]{1,0:T(8,128)(2,1)} %concatenate.169), channel_id=1, source_target_pairs={{0,16},{8,24},{16,0},{24,8},{1,17},{9,25},{17,1},{25,9},{2,18},{10... | collective-permute-start | bytes 995336 | tf_op jit(solution)/shard_map/ppermute | solution.py:52
  468.7 19.1 %collective-permute-start.53 = (bf16[288,432]{1,0:T(8,128)(2,1)S(1)}, bf16[288,432]{1,0:T(8,128)(2,1)S(1)}, u32[]{:S(2)}, u32[]{:S(2)}) collective-permute-start(bf16[288,432]{1,0:T(8,128)(2,1)S(1)} %pad_maximum_fusion.11), channel_id=1, source_target_pairs={{0,8},{8,0},{16,24},{24,16},{1,9},{9,1},{17,25},{25,17},{2,10},{10... | collective-permute-start | bytes 746504 | tf_op jit(solution)/shard_map/ppermute | solution.py:52
  504.1 20.4 %collective-permute-start.60 = (bf16[288,432]{1,0:T(8,128)(2,1)S(1)}, bf16[288,432]{1,0:T(8,128)(2,1)S(1)}, u32[]{:S(2)}, u32[]{:S(2)}) collective-permute-start(bf16[288,432]{1,0:T(8,128)(2,1)S(1)} %copy-done.24), channel_id=1, source_target_pairs={{0,16},{8,24},{16,0},{24,8},{1,17},{9,25},{17,1},{25,9},{2,18},{10... | collective-permute-start | bytes 746504 | tf_op jit(solution)/shard_map/ppermute | solution.py:52
  548.7 38.3 %collective-permute-start.57 = (bf16[288,432]{1,0:T(8,128)(2,1)}, bf16[288,432]{1,0:T(8,128)(2,1)}, u32[]{:S(2)}, u32[]{:S(2)}) collective-permute-start(bf16[288,432]{1,0:T(8,128)(2,1)} %pad_maximum_fusion.12), channel_id=1, source_target_pairs={{0,2},{1,3},{2,0},{3,1},{4,6},{5,7},{6,4},{7,5},{8,10},{9,11},{10,... | collective-permute-start | bytes 746504 | tf_op jit(solution)/shard_map/ppermute | solution.py:57
  549.8 19.7 %collective-permute-start.66 = (bf16[288,432]{1,0:T(8,128)(2,1)S(1)}, bf16[288,432]{1,0:T(8,128)(2,1)S(1)}, u32[]{:S(2)}, u32[]{:S(2)}) collective-permute-start(bf16[288,432]{1,0:T(8,128)(2,1)S(1)} %pad_maximum_fusion.15), channel_id=1, source_target_pairs={{0,2},{1,3},{2,0},{3,1},{4,6},{5,7},{6,4},{7,5},{8,10},{9,11},{10,... | collective-permute-start | bytes 746504 | tf_op jit(solution)/shard_map/ppermute | solution.py:57
  (115 other events, 1147.8 us)

commit v3 on v2

v3 whole, which is shorter than its diff:
```python
import functools

import jax
import jax.numpy as jnp
from jax import lax
from jax.experimental import pallas as pl
from jax.experimental.pallas import tpu as pltpu
from jax.sharding import PartitionSpec as P

HD = 72
norm_eps = 1e-06
LOG2E = 1.4426950408889634
GELU_A = 0.7978845608028654
GELU_B = 0.044715
MIB = 1024 * 1024
bf16 = jnp.bfloat16
f32 = jnp.float32


def round_up(value, unit):
    return -(-value // unit) * unit


def nn(a, b):
    return lax.dot_general(a, b, (((1,), (0,)), ((), ())), preferred_element_type=f32)


def nt(a, b):
    return lax.dot_general(a, b, (((1,), (1,)), ((), ())), preferred_element_type=f32)


def shaped(shape, dtype):
    return jax.ShapeDtypeStruct(shape, dtype)


def on_chip(kernel, out_shape, args, scratch=(), flops=0, exps=0, after=()):
    whole = pl.BlockSpec(memory_space=pltpu.VMEM)
    count, extra = len(args), len(after)

    def run(*refs):
        kernel(*refs[:count], *refs[count + extra :])

    moved = sum(a.size * a.dtype.itemsize for a in list(args) + list(out_shape))
    return pl.pallas_call(
        run,
        in_specs=[whole] * count + [pl.BlockSpec(memory_space=pl.ANY)] * extra,
        out_specs=[whole] * len(out_shape),
        out_shape=list(out_shape),
        scratch_shapes=list(scratch),
        compiler_params=pltpu.CompilerParams(vmem_limit_bytes=60 * MIB),
        cost_estimate=pl.CostEstimate(flops=flops, bytes_accessed=moved, transcendentals=exps),
    )(*args, *after)


def fsdp_swap(x, bit):
    size = lax.axis_size("fsdp")
    return lax.ppermute(x, "fsdp", [(i, i ^ bit) for i in range(size)])


def tensor_swap(x, bit):
    size = lax.axis_size("tensor")
    return lax.ppermute(x, "tensor", [(i, i ^ bit) for i in range(size)])


def fsdp_bits(part):
    bits = []
    bit = 1
    while bit < lax.axis_size("fsdp"):
        bits.append(bit)
        bit *= 2
    return bits if part == 0 else bits[::-1]


def gather_pieces(own):
    half = own.shape[1] // 2
    arrays = [own]
    first = {}
    for bit in fsdp_bits(0):
        first[bit] = len(arrays)
        arrays.append(fsdp_swap(own, bit))
    plan = []
    for part in (0, 1):
        have = {0: (0, part * half)}
        for bit in fsdp_bits(part):
            new = {}
            for offset, (index, row) in have.items():
                if offset == 0:
                    new[bit] = (first[bit], part * half)
                else:
                    new[offset ^ bit] = (len(arrays), 0)
                    arrays.append(fsdp_swap(arrays[index][:, row : row + half], bit))
            have.update(new)
        plan.append([have[o] for o in range(len(have))])
    return arrays, plan


def assemble(out, refs, unit, plan, half, half_pad, start=0):
    for part in (0, 1):
        for offset, (index, row) in enumerate(plan[part]):
            at = part * half_pad + offset * half
            out[at : at + half, :] = refs[index][unit, row : row + half, start : start + out.shape[1]]
        used = len(plan[part]) * half
        if used < half_pad:
            out[part * half_pad + used : (part + 1) * half_pad, :] = jnp.zeros(
                (half_pad - used, out.shape[1]), out.dtype
            )


def add_low(a, b):
    return (a.astype(f32) + b.astype(f32)).astype(bf16)


def split_blocks(x, axis, start, size):
    return {
        n: lax.slice_in_dim(x, start + n * size, start + (n + 1) * size, axis=axis)
        for n in range(lax.axis_size("fsdp"))
    }


def payload_shapes(units, half, cols):
    held = lax.axis_size("fsdp") // 2 * half
    return [shaped((units, held, cols), bf16)] * 4


def emit(refs, unit, grad, half, at):
    count = lax.axis_size("fsdp")
    cols = grad.shape[1]
    for part in (0, 1):
        bit = fsdp_bits(part)[0]
        places = [0, 0]
        for offset in range(count):
            kept = 0 if offset & bit else 1
            row = part * (grad.shape[0] // 2) + offset * half
            to = places[kept] * half
            places[kept] += 1
            refs[2 * part + kept][unit, to : to + half, at : at + cols] = grad[row : row + half].astype(bf16)


def fold_kernel(stage, half, *refs):
    keeps, gots, outs = refs[:2], refs[2:4], refs[4:]
    for part in (0, 1):
        bits = fsdp_bits(part)
        offsets = [o for o in range(lax.axis_size("fsdp")) if not any(o & b for b in bits[: stage + 1])]
        places = [0, 0]
        for n, offset in enumerate(offsets):
            rows = slice(n * half, (n + 1) * half)
            total = add_low(keeps[part][:, rows, :], gots[part][:, rows, :])
            if stage + 1 == len(bits):
                outs[0][:, part * half : (part + 1) * half, :] = total
            else:
                kept = 0 if offset & bits[stage + 1] else 1
                to = places[kept] * half
                places[kept] += 1
                outs[2 * part + kept][:, to : to + half, :] = total


def send(payload, stage):
    return [fsdp_swap(payload[2 * part], fsdp_bits(part)[stage]) for part in (0, 1)]


def fold(payload, got, stage, after=()):
    keeps = [payload[1], payload[3]]
    units, held, cols = keeps[0].shape
    half = held // (lax.axis_size("fsdp") >> (stage + 1))
    if stage + 1 == len(fsdp_bits(0)):
        outs = [shaped((units, 2 * half, cols), bf16)]
    else:
        outs = [shaped((units, held // 2, cols), bf16)] * 4
    return on_chip(functools.partial(fold_kernel, stage, half), outs, keeps + got, after=after)


def finish(payload, after=()):
    stages = len(fsdp_bits(0))
    for stage in range(stages):
        payload = fold(payload, send(payload, stage), stage, after if stage == 0 else ())
    return payload[0]


def row_of(ref, unit, start, count, size):
    table = ref[unit, :, start : start + count].astype(f32).T
    return jnp.concatenate([table[n : n + 1] for n in range(count)], axis=1)[:, :size]


def attend_kernel(seq, heads, plan, count, chosen, first, *refs):
    xn_ref = refs[0]
    pieces = refs[1 : 1 + count]
    rest = refs[1 + count :]
    if not first:
        before_ref, rest = rest[0], rest[1:]
    part_ref = rest[4 * len(chosen)]
    rows, feats = xn_ref.shape
    half = feats // 2
    wide = heads * 3 * HD
    shard = pieces[0].shape[1]
    live = lax.broadcasted_iota(jnp.int32, (rows, 1), 0) < seq
    for place, unit in enumerate(chosen):
        w_ref, qkv_ref, ctx_ref, lse_ref = rest[4 * place : 4 * place + 4]
        assemble(w_ref, pieces, unit, plan, shard // 2, half)
        qv = row_of(pieces[0], unit, wide + heads * HD + 6, -(-heads * 2 * HD // shard), heads * 2 * HD)
        bias = []
        for h in range(heads):
            at = h * 2 * HD
            bias += [qv[:, at : at + HD], jnp.zeros((1, HD), f32), qv[:, at + HD : at + 2 * HD]]
        qkv = nn(xn_ref[...], w_ref[:, :wide]) + jnp.concatenate(bias, axis=1)
        qkv_t = qkv.T
        qkv_ref[...] = qkv_t.astype(bf16)
        contexts = []
        for h in range(heads):
            at = h * 3 * HD
            q_t = qkv_t[at : at + HD].astype(bf16)
            k_n = qkv[:, at + HD : at + 2 * HD].astype(bf16)
            v_t = qkv_t[at + 2 * HD : at + 3 * HD].astype(bf16)
            scores = nn(k_n, q_t) * (HD**-0.5 * LOG2E)
            scores = jnp.where(live, scores, -1e30)
            top = jnp.max(scores, axis=0, keepdims=True)
            weight = jnp.exp2(scores - top)
            total_weight = jnp.sum(weight, axis=0, keepdims=True)
            lse_ref[h : h + 1, :] = top + jnp.log2(total_weight)
            contexts.append(nn(v_t, weight.astype(bf16)) / total_weight)
        ctx = jnp.concatenate(contexts, axis=0).T.astype(bf16)
        ctx_ref[...] = ctx
        for n in (0, 1):
            add = nt(ctx, w_ref[n * half : (n + 1) * half, wide : wide + heads * HD])
            if place > 0:
                add = add + part_ref[n].astype(f32)
            elif not first:
                add = add + before_ref[n].astype(f32)
            part_ref[n] = add.astype(bf16)


def attend(xn, pieces, plan, chosen, before, seq, heads, after):
    rows, feats = xn.shape
    wide = heads * 3 * HD
    cols = wide + heads * HD
    units = len(chosen)
    args = [xn] + pieces + ([] if before is None else [before])
    found = on_chip(
        functools.partial(attend_kernel, seq, heads, plan, len(pieces), chosen, before is None),
        [
            shaped((feats, cols), bf16),
            shaped((wide, rows), bf16),
            shaped((rows, heads * HD), bf16),
            shaped((heads, rows), f32),
        ]
        * units
        + [shaped((2, rows, feats // 2), bf16)],
        args,
        flops=units * 2 * rows * (feats * cols + heads * 2 * rows * 256),
        exps=units * heads * rows * rows,
        after=after,
    )
    return [found[4 * u : 4 * u + 4] for u in range(units)], found[4 * units]


def attend_back_kernel(seq, heads, count, first, half, extra, *refs):
    xnt_ref, bg_ref = refs[:2]
    w_refs, qkv_refs, lse_refs = [refs[2 + n * count : 2 + (n + 1) * count] for n in range(3)]
    rest = refs[2 + 3 * count :]
    ctx_refs, rest = rest[: count * extra], rest[count * extra :]
    if not first:
        before_ref, rest = rest[0], rest[1:]
    payload, db_ref, part_ref = rest[:4], rest[4], rest[5]
    rows, feats = bg_ref.shape
    half_pad = feats // 2
    wide = heads * 3 * HD
    live = lax.broadcasted_iota(jnp.int32, (rows, 1), 0) < seq
    scale = HD**-0.5
    if extra:
        bg_t = bg_ref[...].astype(f32).T.astype(bf16)
        for unit in range(count):
            ctx = [r[...].astype(f32) for r in ctx_refs[unit * extra : (unit + 1) * extra]]
            emit(payload, unit, nn(bg_t, jnp.concatenate(ctx, axis=1).astype(bf16)), half, wide)
    for unit in range(count):
        w_ref = w_refs[unit]
        d_ctx_t = nn(bg_ref[...], w_ref[:, wide : wide + heads * HD]).T
        qkv_t = qkv_refs[unit][...].astype(f32)
        qkv = qkv_t.T
        pieces = []
        for h in range(heads):
            at = h * 3 * HD
            q_t = qkv_t[at : at + HD].astype(bf16)
            k_t = qkv_t[at + HD : at + 2 * HD].astype(bf16)
            k_n = qkv[:, at + HD : at + 2 * HD].astype(bf16)
            v_n = qkv[:, at + 2 * HD : at + 3 * HD].astype(bf16)
            d_o = d_ctx_t[h * HD : (h + 1) * HD].astype(bf16)
            scores = nn(k_n, q_t) * (scale * LOG2E)
            probs = jnp.where(live, jnp.exp2(scores - lse_refs[unit][h : h + 1, :]), 0.0)
            d_probs = nn(v_n, d_o)
            delta = jnp.sum(d_probs * probs, axis=0, keepdims=True)
            d_scores = (probs * (d_probs - delta)).astype(bf16)
            d_v = nt(probs.astype(bf16), d_o)
            d_k = nt(d_scores, q_t) * scale
            d_q = nn(k_t, d_scores) * scale
            pieces += [d_q.T, d_k, d_v]
        d_qkv = jnp.concatenate(pieces, axis=1).astype(bf16)
        db_ref[unit : unit + 1, :] = jnp.sum(d_qkv.astype(f32), axis=0, keepdims=True)
        emit(payload, unit, nn(xnt_ref[...], d_qkv), half, 0)
        for n in (0, 1):
            add = nt(d_qkv, w_ref[n * half_pad : (n + 1) * half_pad, :wide])
            if unit > 0:
                add = add + part_ref[n].astype(f32)
            elif not first:
                add = add + before_ref[n].astype(f32)
            part_ref[n] = add.astype(bf16)


def attend_back(xnt, bg, kept, contexts, before, seq, heads, half, after):
    rows, feats = bg.shape
    wide = heads * 3 * HD
    count = len(kept)
    extra = len(contexts) // count
    args = [xnt, bg] + [k[0] for k in kept] + [k[1] for k in kept] + [k[3] for k in kept] + contexts
    found = on_chip(
        functools.partial(attend_back_kernel, seq, heads, count, before is None, half, extra),
        payload_shapes(count, half, wide + extra * heads * HD)
        + [shaped((count, wide), f32), shaped((2, rows, feats // 2), bf16)],
        args + ([] if before is None else [before]),
        flops=count * 2 * rows * (2 * feats * wide + heads * 5 * rows * 256),
        exps=count * heads * rows * rows,
        after=after,
    )
    return found[:4], found[4], found[5]


def mlp_kernel(plan, counts, units, first, half, *refs):
    low_ref, high_ref, cot_ref, cott_ref = refs[:4]
    at = 4
    pieces = []
    for count in counts:
        pieces.append(refs[at : at + count])
        at += count
    if not first:
        before_refs, before_db = refs[at : at + len(counts)], refs[at + len(counts)]
        at += len(counts) + 1
    out_refs, back_refs, db_ref = refs[at : at + 2], refs[at + 2 : at + 4], refs[at + 4]
    at += 5
    dw_refs = refs[at : at + (len(counts) if first else 4)]
    n2_ref, n2t_ref, w_ref, out_sum, back_sum = refs[at + len(dw_refs) :]
    half_pad = low_ref.shape[1]
    n2_ref[:, :half_pad] = low_ref[...]
    n2_ref[:, half_pad:] = high_ref[...]
    n2t_ref[:half_pad, :] = low_ref[...].astype(f32).T.astype(bf16)
    n2t_ref[half_pad:, :] = high_ref[...].astype(f32).T.astype(bf16)
    for u in range(len(counts)):
        shard = pieces[u][0].shape[1]
        assemble(w_ref, pieces[u], 0, plan, shard // 2, half_pad)
        bias = row_of(pieces[u][0], 0, 2 * units, -(-units // shard), units)
        up = w_ref[:, :units]
        down = w_ref[:, units:]
        v = nn(n2_ref[...], up) + bias
        square = v * v
        t = jnp.tanh(GELU_A * v * (1.0 + GELU_B * square))
        hidden = (0.5 * v * (1.0 + t)).astype(bf16)
        slope = 0.5 * (1.0 + t) + (0.5 * GELU_A) * v * (1.0 - t * t) * (1.0 + 3.0 * GELU_B * square)
        pre_grad = (nn(cot_ref[...], down) * slope).astype(bf16)
        out_add = nt(hidden, down)
        back_add = nt(pre_grad, up)
        if u == 0:
            out_sum[...] = out_add
            back_sum[...] = back_add
        else:
            out_sum[...] += out_add
            back_sum[...] += back_add
        db = jnp.sum(pre_grad.astype(f32), axis=0, keepdims=True)
        db_ref[u : u + 1, :] = db if first else db + before_db[u : u + 1, :]
        d_up = nn(n2t_ref[...], pre_grad)
        d_down = nn(cott_ref[...], hidden)
        if first:
            dw_refs[u][:, :units] = d_up.astype(bf16)
            dw_refs[u][:, units:] = d_down.astype(bf16)
        else:
            emit(dw_refs, u, d_up + before_refs[u][:, :units].astype(f32), half, 0)
            emit(dw_refs, u, d_down + before_refs[u][:, units:].astype(f32), half, units)
    for n in (0, 1):
        out_refs[n][...] = out_sum[:, n * half_pad : (n + 1) * half_pad].astype(bf16)
        back_refs[n][...] = back_sum[:, n * half_pad : (n + 1) * half_pad].astype(bf16)


def mlp(low, high, cot, cot_t, gathered, units, before):
    rows, half_pad = low.shape
    feats = 2 * half_pad
    plan = gathered[0][1]
    half = gathered[0][0][0].shape[1] // 2
    count = len(gathered)
    args = [low, high, cot, cot_t] + [a for g in gathered for a in g[0]] + list(before or [])
    grads = [shaped((feats, 2 * units), bf16)] * count if before is None else payload_shapes(count, half, 2 * units)
    found = on_chip(
        functools.partial(mlp_kernel, plan, [len(g[0]) for g in gathered], units, before is None, half),
        [
            shaped((rows, half_pad), bf16),
            shaped((rows, half_pad), bf16),
            shaped((rows, half_pad), bf16),
            shaped((rows, half_pad), bf16),
            shaped((count, units), f32),
        ]
        + grads,
        args,
        scratch=[
            pltpu.VMEM((rows, feats), bf16),
            pltpu.VMEM((feats, rows), bf16),
            pltpu.VMEM((feats, 2 * units), bf16),
            pltpu.VMEM((rows, feats), f32),
            pltpu.VMEM((rows, feats), f32),
        ],
        flops=count * 12 * rows * feats * units,
        exps=count * rows * units,
    )
    return found[:2], found[2:4], found[4], found[5:]


def standardize(rows, width):
    mean = jnp.sum(rows, axis=-1, keepdims=True) / width
    var = jnp.sum(rows * rows, axis=-1, keepdims=True) / width - mean * mean
    rstd = lax.rsqrt(var + norm_eps)
    return (rows - mean) * rstd, rstd


def norm_back(grad, xhat, rstd, gain, width):
    a = grad * gain
    mean_a = jnp.sum(a, axis=-1, keepdims=True) / width
    mean_ax = jnp.sum(a * xhat, axis=-1, keepdims=True) / width
    return rstd * (a - mean_a - xhat * mean_ax)


def by_rows(kernel, out_shape, out_whole, args, whole, rows, tile, after=()):
    def spec(shape, uncut):
        if uncut:
            return pl.BlockSpec(shape, lambda i, n=len(shape): (0,) * n)
        if len(shape) == 3:
            return pl.BlockSpec((shape[0], tile, shape[2]), lambda i: (0, i, 0))
        return pl.BlockSpec((tile, shape[1]), lambda i: (i, 0))

    count, extra = len(args), len(after)

    def run(*refs):
        kernel(*refs[:count], *refs[count + extra :])

    return pl.pallas_call(
        run,
        grid=(rows // tile,),
        in_specs=[spec(a.shape, w) for a, w in zip(args, whole)]
        + [pl.BlockSpec(memory_space=pl.ANY)] * extra,
        out_specs=[spec(o.shape, w) for o, w in zip(out_shape, out_whole)],
        out_shape=list(out_shape),
        compiler_params=pltpu.CompilerParams(vmem_limit_bytes=40 * MIB),
        cost_estimate=pl.CostEstimate(
            flops=0,
            bytes_accessed=sum(a.size * a.dtype.itemsize for a in list(args) + list(out_shape)),
            transcendentals=0,
        ),
    )(*args, *after)


def joined(ref):
    return jnp.concatenate([ref[0].astype(f32), ref[1].astype(f32)], axis=-1)


def crossed(ref):
    return jnp.concatenate([ref[1].astype(f32), ref[0].astype(f32)], axis=-1)


def middle_kernel(width, x_ref, own_ref, other_ref, vec_ref, middle_ref, low_ref, high_ref):
    half = low_ref.shape[1]
    middle = x_ref[...].astype(f32) + joined(own_ref) + crossed(other_ref) + vec_ref[0:1, :]
    middle_ref[...] = middle
    xhat, rstd = standardize(middle, width)
    n2 = (xhat * vec_ref[3:4, :] + vec_ref[4:5, :]).astype(bf16)
    low_ref[...] = n2[:, :half]
    high_ref[...] = n2[:, half:]


def add_sums(ref, sums):
    @pl.when(pl.program_id(0) == 0)
    def _():
        ref[...] = sums

    @pl.when(pl.program_id(0) > 0)
    def _():
        ref[...] += sums


def column_sums(parts):
    return jnp.concatenate([jnp.sum(p, axis=0, keepdims=True) for p in parts], axis=0)


def middle_back_kernel(
    width, low_ref, high_ref, middle_ref, cot_ref, out_ref, more_ref, vec_ref,
    grad_ref, bg_ref, out_sum_ref, sum_ref,
):
    out_sum_ref[...] = add_low(out_ref[...], more_ref[...])
    half = low_ref.shape[1]
    grad = jnp.concatenate([low_ref[...].astype(f32), high_ref[...].astype(f32)], axis=-1)
    xhat, rstd = standardize(middle_ref[...], width)
    cot = cot_ref[...].astype(f32)
    back = cot + norm_back(grad, xhat, rstd, vec_ref[3:4, :], width)
    grad_ref[...] = back[:, :half]
    bg_ref[...] = back.astype(bf16)
    add_sums(
        sum_ref,
        column_sums([back[:, :half], grad[:, :half] * xhat[:, :half], grad[:, :half], cot[:, :half]]),
    )


def out_kernel(own_ref, other_ref, far_ref, middle_ref, _, vec_ref, pick_ref, out_ref):
    half = own_ref.shape[1]
    result = middle_ref[:, :half] + own_ref[...].astype(f32) + other_ref[...].astype(f32)
    result = result + far_ref[...].astype(f32) + vec_ref[5:6, :half]
    out_ref[...] = nt(pick_ref[...], result.astype(bf16)).astype(bf16)


def first_back_kernel(width, own_ref, other_ref, x_ref, grad_ref, _, vec_ref, pick_ref, out_ref, sum_ref):
    half = grad_ref.shape[1]
    grad = joined(own_ref) + crossed(other_ref)
    xhat, rstd = standardize(x_ref[...].astype(f32), width)
    back = norm_back(grad, xhat, rstd, vec_ref[1:2, :], width)
    result = (grad_ref[...] + back[:, :half]).astype(bf16)
    out_ref[...] = nt(pick_ref[...], result).astype(bf16)
    add_sums(sum_ref, column_sums([grad[:, :half] * xhat[:, :half], grad[:, :half]]))


def start_kernel(seq, turned, pick_ref, source_ref, *refs):
    count = (len(refs) - 1) // (2 + turned)
    ins, outs = refs[:count], refs[len(refs) - count * (1 + turned) :]
    width = ins[0].shape[2]
    place = lax.broadcasted_iota(jnp.int32, (width, source_ref.shape[1]), 0) == source_ref[...]
    place = jnp.where(place, 1.0, 0.0).astype(bf16)
    for n in range(count):
        outs[n][...] = jnp.zeros(outs[n].shape, bf16)
        outs[n][:seq, :] = nn(ins[n][0], place).astype(bf16)
        if turned:
            outs[count + n][...] = outs[n][...].astype(f32).T.astype(bf16)


def start(array, index, source, rows, turned, after):
    _, seq, width = array.shape
    feats = source.shape[0]
    count = index.shape[0]
    image = lambda n: pl.BlockSpec((1, seq, width), lambda i, pick: (pick[n], 0, 0))
    flat = lambda *shape: pl.BlockSpec(shape, lambda i, pick: (0, 0))
    return pl.pallas_call(
        functools.partial(start_kernel, seq, turned),
        grid_spec=pltpu.PrefetchScalarGridSpec(
            num_scalar_prefetch=1,
            grid=(1,),
            in_specs=[flat(1, feats)] + [image(n) for n in range(count)] + [pl.BlockSpec(memory_space=pl.ANY)],
            out_specs=[flat(rows, feats)] * count + [flat(feats, rows)] * (count * turned),
        ),
        out_shape=[shaped((rows, feats), bf16)] * count + [shaped((feats, rows), bf16)] * (count * turned),
        compiler_params=pltpu.CompilerParams(vmem_limit_bytes=60 * MIB),
        cost_estimate=pl.CostEstimate(
            flops=2 * count * rows * width * feats, bytes_accessed=6 * count * rows * feats, transcendentals=0
        ),
    )(index, source[None, :], *([array] * count), after)


def stack_kernel(*refs):
    for n, ref in enumerate(refs[:-1]):
        refs[-1][n] = ref[0]


def turn_kernel(vectors_ref, bias_ref, out_ref):
    spare = out_ref.shape[1] - vectors_ref.shape[0] - bias_ref.shape[0]
    rows = [vectors_ref[...].astype(f32), bias_ref[...].astype(f32)]
    if spare:
        rows.append(jnp.zeros((spare, out_ref.shape[0]), f32))
    out_ref[...] = jnp.concatenate(rows, axis=0).T.astype(bf16)


def pack_kernel(heads, calls, sums1_ref, sums2_ref, up_ref, *refs):
    out_ref = refs[-1]
    lanes = out_ref.shape[1]
    out_ref[...] = jnp.zeros(out_ref.shape, f32)
    out_ref[0:1, : sums2_ref.shape[1]] = sums2_ref[0:1, :]
    out_ref[1:3, : sums1_ref.shape[1]] = sums1_ref[...]
    out_ref[3:6, : sums2_ref.shape[1]] = sums2_ref[1:4, :]
    groups = sum(len(c) for c in calls)
    for call, ref in zip(calls, refs[:-1]):
        for n, unit in enumerate(call):
            for h in range(heads):
                at, to = h * 3 * HD, h * 2 * HD
                out_ref[6 + unit : 7 + unit, to : to + HD] = ref[n : n + 1, at : at + HD]
                out_ref[6 + unit : 7 + unit, to + HD : to + 2 * HD] = ref[n : n + 1, at + 2 * HD : at + 3 * HD]
    out_ref[6 + groups : 6 + groups + up_ref.shape[0], : up_ref.shape[1]] = up_ref[...]


def group_sum_kernel(groups, rows_q, rows_b, cut_b, own_ref, got_ref, out_ref):
    out_ref[...] = own_ref[...]
    out_ref[0:6, :] = own_ref[0:6, :] + got_ref[0:6, :]
    keep = rows_q // 2
    out_ref[6 : 6 + keep, :] = own_ref[6 : 6 + keep, :] + got_ref[6 + keep : 6 + rows_q, :]
    if cut_b:
        base, keep = 6 + groups, rows_b // 2
        out_ref[base : base + keep, :] = own_ref[base : base + keep, :] + got_ref[base + keep : base + rows_b, :]


def block_sum_kernel(bits, half, own_ref, got_ref, out_ref):
    out_ref[...] = own_ref[...] + got_ref[...]
    for offset in range(lax.axis_size("fsdp")):
        if not any(offset & b for b in bits):
            at, other = offset * half, (offset ^ bits[-1]) * half
            out_ref[0:6, at : at + half] = own_ref[0:6, at : at + half] + got_ref[0:6, other : other + half]


def add_kernel(*refs):
    total = refs[0][...].astype(f32)
    for ref in refs[1:-1]:
        total = total + ref[...].astype(f32)
    refs[-1][...] = total.astype(bf16)


def add_after(parts, after):
    return on_chip(add_kernel, [shaped(parts[0].shape, bf16)], parts, after=after)[0]


def first_kernel(width, plan, at, count, *refs):
    x_ref, pieces = refs[0], refs[1 : 1 + count]
    xn_ref, xnt_ref, vec_ref, table = refs[1 + count :]
    assemble(table, pieces, 0, plan, pieces[0].shape[1] // 2, x_ref.shape[1] // 2, at)
    vectors = table[...].astype(f32).T
    vec_ref[...] = vectors
    xhat, _ = standardize(x_ref[...].astype(f32), width)
    xn = xhat * vectors[1:2] + vectors[2:3]
    xn_ref[...] = xn.astype(bf16)
    xnt_ref[...] = xn.T.astype(bf16)


def first(x, pieces, plan, width, at, after):
    rows, feats = x.shape
    return on_chip(
        functools.partial(first_kernel, width, plan, at, len(pieces)),
        [shaped((rows, feats), bf16), shaped((feats, rows), bf16), shaped((8, feats), f32)],
        [x] + pieces,
        scratch=[pltpu.VMEM((feats, 8), bf16)],
        after=after,
    )


def body(
    inputs, cotangent, qkv_proj, qv_bias, out_proj, out_bias, gain_one, shift_one, gain_two,
    shift_two, up_proj, up_bias, down_proj, down_bias,
):
    fsdp, tensor = lax.axis_size("fsdp"), lax.axis_size("tensor")
    images, seq, width = inputs.shape
    groups = images
    sub = tensor // groups
    heads = qkv_proj.shape[1]
    units = up_proj.shape[1]
    shard = qkv_proj.shape[0]
    share = width // tensor
    half = shard // 2
    used = half * fsdp
    half_pad = round_up(used, 128)
    feats = 2 * half_pad
    rows = round_up(seq, 128)
    tile = rows // 3 if rows % 384 == 0 else 128
    wide = heads * 3 * HD
    qv = heads * 2 * HD
    fi, ti = lax.axis_index("fsdp"), lax.axis_index("tensor")
    gi, ci = ti // sub, ti % 2
    group_bits = []
    bit = 1
    while bit < groups:
        group_bits.append(bit * sub)
        bit *= 2
    pair_bit, far_bits = group_bits[0], group_bits[1:][::-1]
    core_bits = []
    bit = 1
    while bit < sub:
        core_bits.append(bit)
        bit *= 2

    def gather_units(x, bits):
        have = [x]
        for bit in bits:
            have = have + [tensor_swap(h, bit) for h in have]
        return have

    def scatter_units(have, bits, add):
        for bit in bits[::-1]:
            keep = len(have) // 2
            have = [add(a, tensor_swap(b, bit)) for a, b in zip(have[:keep], have[keep:])]
        return have[0]

    def swap_halves(x, axis):
        low = lax.slice_in_dim(x, 0, half, axis=axis)
        high = lax.slice_in_dim(x, half, 2 * half, axis=axis)
        a = jnp.where(ci == 0, low, high)
        b = jnp.where(ci == 0, high, low)
        return jnp.concatenate([a, b], axis=axis)

    def columns(vector):
        count = -(-vector.size // shard)
        return jnp.pad(vector, (0, count * shard - vector.size)).reshape(count, shard).T

    own_vectors = swap_halves(
        jnp.stack([out_bias, gain_one, shift_one, gain_two, shift_two, down_bias]), 1
    )
    qv_rows = -(-qv // shard)
    own_bias = jnp.pad(qv_bias.reshape(1, qv), ((0, 0), (0, qv_rows * shard - qv))).reshape(qv_rows, shard)
    own_columns = on_chip(
        turn_kernel, [shaped((shard, round_up(6 + qv_rows, 8)), bf16)], [own_vectors, own_bias]
    )[0]
    wire_a = jnp.concatenate(
        [qkv_proj.reshape(shard, wide), out_proj.reshape(heads * HD, shard).T], axis=1
    )
    wire_a = jnp.concatenate([swap_halves(wire_a, 0), own_columns], axis=1)
    wires_a = gather_units(wire_a[None], far_bits)
    wire_b = swap_halves(jnp.concatenate([up_proj, down_proj.T], axis=1), 0)
    wire_b = jnp.concatenate([wire_b, columns(up_bias)], axis=1)
    near = len(fsdp_bits(0)) + 1
    gathered_a = gather_pieces(wires_a[0])

    lane = jnp.arange(feats, dtype=jnp.int32)
    part, at = lane // half_pad, lane % half_pad
    block = jnp.minimum(at // half, fsdp - 1) ^ fi
    source = jnp.where(at < used, block * shard + (part ^ ci) * half + at % half, -1)
    wire_b = add_after([wire_b[None]], gathered_a[0][near:])
    x = start(inputs, gi[None], source, rows, 0, wire_b)[0]
    wires_a += [tensor_swap(wires_a[0], pair_bit)]
    wires_a += [tensor_swap(add_after([w], [x]), pair_bit) for w in wires_a[1:-1]]
    wires_b = gather_units(wire_b, far_bits)
    gathered_b = [gather_pieces(wires_b[0])]
    found = start(cotangent, jnp.stack([gi, gi ^ 1]), source, rows, 1, gathered_b[0][0][1])
    cots, cots_t = found[:2], found[2:]
    out_share = jnp.arange(groups * share, dtype=jnp.int32)
    out_first = ((gi ^ (out_share // share)) * sub + ti % sub) * share + out_share % share
    pick = (out_first[:, None] == source[None, :half_pad]).astype(bf16)

    xn, xnt, vectors = first(x, *gathered_a, width, wide + heads * HD, [])
    kept, attn = attend(xn, *gathered_a, (0,), None, seq, heads, [cots[0]])
    later = on_chip(
        stack_kernel, [shaped((groups - 1,) + wire_a.shape, bf16)], wires_a[1:], after=gathered_b[0][0][near:]
    )[0]
    later = gather_pieces(later)
    held = [add_after([w], later[0][1:near]) for w in wires_b[1:]]
    gathered_b += [gather_pieces(w) for w in held]
    more, attn = attend(xn, *later, tuple(range(groups - 2)), attn, seq, heads, held)
    kept += more
    early = [a for g in gathered_b[1:] for a in g[0][1:near]]
    more, attn = attend(xn, *later, (groups - 2,), attn, seq, heads, early)
    kept += more

    def other_cores(parts):
        other = tensor_swap(parts, 1)
        for bit in core_bits[1:]:
            more = tensor_swap(jnp.stack([parts, other]), bit)
            parts, other = add_low(parts, more[0]), add_low(other, more[1])
        return parts, other

    attn, attn_other = other_cores(attn)
    middle, n2_low, n2_high = by_rows(
        functools.partial(middle_kernel, width),
        [shaped((rows, feats), f32), shaped((rows, half_pad), bf16), shaped((rows, half_pad), bf16)],
        [False] * 3,
        [x, attn, attn_other, vectors],
        [False, False, False, True],
        rows,
        tile,
        after=[a for g in gathered_b[1:] for a in g[0][1:near]],
    )
    far_low = tensor_swap(n2_low, pair_bit)

    out0, back0, up_bias0, dw0 = mlp(n2_low, n2_high, cots[0], cots_t[0], gathered_b, units, None)
    far_low = add_after([far_low], [up_bias0])
    far_high = tensor_swap(far_low, 1)
    out1, back1, up_bias_g, payload_b = mlp(
        far_low, far_high, cots[1], cots_t[1], gathered_b, units, list(dw0) + [up_bias0]
    )
    got_b = send(payload_b, 0)

    def other_half(parts):
        other = tensor_swap(parts[1], 1)
        for bit in core_bits[1:]:
            other = add_low(other, tensor_swap(add_low(parts[0], other), bit))
        return other

    def sum_cores(parts):
        return add_after([parts[0], other_half(parts)], [])

    back_far = tensor_swap(sum_cores(back1), pair_bit)
    back_low = add_low(sum_cores(back0), back_far)
    back_high = tensor_swap(back_low, 1)
    middle_grad, branch_grad, out_sum, sums2 = by_rows(
        functools.partial(middle_back_kernel, width),
        [
            shaped((rows, half_pad), f32),
            shaped((rows, feats), bf16),
            shaped((rows, half_pad), bf16),
            shaped((4, half_pad), f32),
        ],
        [False, False, False, True],
        [back_low, back_high, middle, cots[0], out1[0], other_half(out1), vectors],
        [False] * 6 + [True],
        rows,
        tile,
    )
    def spread(blocks):
        got = [blocks[:share]]
        for i in range(1, groups):
            got.append(tensor_swap(blocks[i * share : (i + 1) * share], i * sub))
        return got

    def collect(got):
        for i in range(len(group_bits)):
            swapped = [got[n ^ (1 << i)] for n in range(groups)]
            got = [jnp.where((gi >> i) & 1 == 1, s, g) for s, g in zip(swapped, got)]
        return jnp.stack([g.T[:seq] for g in got])

    stages = len(fsdp_bits(0))

    def rest_of(waiting, after):
        for stage in range(1, stages):
            waiting = fold(waiting, send(waiting, stage), stage, after)
        return waiting[0]

    middle_unit = groups // 2
    calls = [list(range(middle_unit, groups))[::-1]] + [[u] for u in range(middle_unit)[::-1]]
    back = None
    bias_calls = []
    payloads = []
    out_far = tensor_swap(out_sum, pair_bit)
    waiting_b = fold(payload_b, got_b, 0, [branch_grad])
    needed = [waiting_b[0]]
    for n, call in enumerate(calls):
        contexts = [kept[v][2] for u in call for v in (u, u - middle_unit)] if n == 0 else []
        payload, bias_g, back = attend_back(
            xnt, branch_grad, [kept[u] for u in call], contexts, back, seq, heads, half, needed
        )
        payloads.append(payload)
        bias_calls.append(bias_g)
        needed = []
        if n == 0:
            out_shares = by_rows_turned(
                out_kernel, [out0[0], other_half(out0), out_far, middle, back, vectors, pick], rows, tile, []
            )[0]
            out_got = spread(out_shares)
            layer_out = collect(out_got)
            grad_b = rest_of(waiting_b, [back])
            needed = [grad_b]
        elif n == 1:
            waiting = fold(payloads[0], send(payloads[0], 0), 0, [back])
            needed = [waiting[0]]
    back_done = back
    back, back_other = other_cores(back)
    grad_b = scatter_units([grad_b[u] for u in range(len(wires_b))], far_bits, add_low)
    far = rest_of(waiting, [back_done] + out_got)
    near_sums = [fold(p, send(p, 0), 0, [back_done]) for p in payloads[1:-1]]
    in_shares, sums1 = by_rows_turned(
        functools.partial(first_back_kernel, width),
        [back, back_other, x, middle_grad, far, vectors, pick],
        rows,
        tile,
        [(2, half_pad)],
    )
    in_got = spread(in_shares)
    own = [rest_of(p, [in_shares])[0] for p in near_sums] + [finish(payloads[-1], in_got)[0]]
    own = own[::-1]
    both = wide + heads * HD
    got = tensor_swap(far[..., :both], pair_bit)
    grads_a = []
    for u in range(middle_unit):
        n = calls[0].index(u + middle_unit)
        grads_a.append(add_low(jnp.concatenate([own[u], far[n, :, both:]], axis=1), got[n]))
    grad_a = scatter_units(grads_a, far_bits, add_low)
    grad_a, grad_o = grad_a[:, :wide], grad_a[:, wide:]
    input_grad = collect(in_got).astype(f32)

    small = on_chip(
        functools.partial(pack_kernel, heads, calls),
        [shaped((16, round_up(max(half_pad, qv, units), 128)), f32)],
        [sums1, sums2, up_bias_g] + bias_calls,
    )[0]
    rows_q, rows_b = groups, len(wires_b)
    for bit in (far_bits + [pair_bit])[::-1]:
        cut_b = bit != pair_bit
        small = on_chip(
            functools.partial(group_sum_kernel, groups, rows_q, rows_b, cut_b),
            [shaped(small.shape, f32)],
            [small, tensor_swap(small, bit)],
        )[0]
        rows_q //= 2
        rows_b = rows_b // 2 if cut_b else rows_b
    done_bits = []
    for bit in fsdp_bits(0):
        done_bits.append(bit)
        small = on_chip(
            functools.partial(block_sum_kernel, tuple(done_bits), half),
            [shaped(small.shape, f32)],
            [small, fsdp_swap(small, bit)],
        )[0]
    own_vector_g = small[:6, :half]
    vector_g = swap_halves(jnp.concatenate([own_vector_g, tensor_swap(own_vector_g, 1)], axis=1), 1)
    qvbias_g = small[6, :qv].reshape(heads, 2 * HD)
    upbias_g = small[6 + groups, :units]
    grad_a = swap_halves(grad_a.astype(f32), 0)
    grad_o = swap_halves(grad_o.astype(f32), 0)
    grad_b = swap_halves(grad_b.astype(f32), 0)
    return (
        layer_out,
        input_grad,
        grad_a.reshape(shard, heads, 3 * HD),
        qvbias_g,
        grad_o.T.reshape(heads, HD, shard),
        vector_g[0],
        vector_g[1],
        vector_g[2],
        vector_g[3],
        vector_g[4],
        grad_b[:, :units],
        upbias_g,
        grad_b[:, units:].T,
        vector_g[5],
    )


def by_rows_turned(kernel, args, rows, tile, sums):
    wide = args[-1].shape[0]

    def spec(shape):
        if len(shape) == 3:
            return pl.BlockSpec((shape[0], tile, shape[2]), lambda i: (0, i, 0))
        return pl.BlockSpec((tile, shape[1]), lambda i: (i, 0))

    whole = lambda shape: pl.BlockSpec(shape, lambda i: (0, 0))
    return pl.pallas_call(
        kernel,
        grid=(rows // tile,),
        in_specs=[spec(a.shape) for a in args[:-3]]
        + [pl.BlockSpec(memory_space=pl.ANY)]
        + [whole(a.shape) for a in args[-2:]],
        out_specs=[pl.BlockSpec((wide, tile), lambda i: (0, i))] + [whole(shape) for shape in sums],
        out_shape=[shaped((wide, rows), bf16)] + [shaped(shape, f32) for shape in sums],
        compiler_params=pltpu.CompilerParams(vmem_limit_bytes=40 * MIB),
        cost_estimate=pl.CostEstimate(
            flops=2 * rows * args[-1].size, bytes_accessed=12 * rows * args[0].shape[-1], transcendentals=0
        ),
    )(*args)


def solution(mesh):
    return jax.shard_map(
        body,
        mesh=mesh,
        in_specs=(
            P("fsdp", None, None),
            P("fsdp", None, None),
            P("fsdp", "tensor", None),
            P("tensor", None),
            P("tensor", None, "fsdp"),
            P("fsdp"),
            P("fsdp"),
            P("fsdp"),
            P("fsdp"),
            P("fsdp"),
            P("fsdp", "tensor"),
            P("tensor"),
            P("tensor", "fsdp"),
            P("fsdp"),
        ),
        out_specs=(
            P("fsdp", None, "tensor"),
            P("fsdp", None, "tensor"),
            P("fsdp", "tensor", None),
            P("tensor", None),
            P("tensor", None, "fsdp"),
            P("fsdp"),
            P("fsdp"),
            P("fsdp"),
            P("fsdp"),
            P("fsdp"),
            P("fsdp", "tensor"),
            P("tensor"),
            P("tensor", "fsdp"),
            P("fsdp"),
        ),
        check_vma=False,
    )
```

time: 622 us -> 471 us (0.76)
  waiting for transfers between devices: 228 us -> 92.5 us
  Pallas kernels: 145 us -> 218 us
  starting transfers between devices: 95.7 us -> 65.5 us
  local copies, waits for them, and re-layouts: 94.9 us -> 67.8 us
  matrix products: 15.5 us -> 0 us
  other arithmetic: 35.9 us -> 21.2 us
    ppermute x56 -> x34, waiting for transfers between devices: 111 us -> 29.5 us  [fsdp_swap(): return lax.ppermute(x, 'fsdp', [(i, i ^ bit) for i in range(size)])]
    pallas_call x14 -> x36, Pallas kernels: 145 us -> 218 us  [the longest x30 186 us: on_chip(): pl.pallas_call(run, in_specs=[whole] * count + [pl.BlockSpec(memory_space...]
    ppermute x33 -> x27, waiting for transfers between devices: 117 us -> 63 us  [tensor_swap(): return lax.ppermute(x, 'tensor', [(i, i ^ bit) for i in range(size)])]
    unnamed x119 -> x142, local copies, waits for them, and re-layouts: 18.1 us -> 45.8 us
    ppermute x56 -> x34, starting transfers between devices: 60.2 us -> 38.6 us  [fsdp_swap(): return lax.ppermute(x, 'fsdp', [(i, i ^ bit) for i in range(size)])]
    dynamic_slice x1 -> x0, local copies, waits for them, and re-layouts: 15.9 us -> none  [arrange(): x = lax.dynamic_index_in_dim(x, index, 0, keepdims=False)]
    slice x42 -> x12, local copies, waits for them, and re-layouts: 24.7 us -> 8.89 us  [the longest x8 4.01 us: gather_pieces(): arrays.append(fsdp_swap(arrays[index][:, row:row + half], bit))]
    dot_general x4 -> x0, matrix products: 15.5 us -> none  [the longest x3 12.8 us: arrange(): jnp.einsum('rd,de->re', x, place, preferred_element_type=f32).astype(bf16)]
  transfers between devices with their start and end apart: 89 -> 61, of which waited for: 35 -> 21; matrix products, arithmetic and copies ran while one was open for 18% -> 9% of each run, Pallas kernels for 14% -> 35%
where the time goes in v3:
time: 471 us; the launch traced here: 466 us
  Pallas kernels  218 us (46%)
  waiting for transfers between devices  92.5 us (20%)
  local copies, waits for them, and re-layouts  67.8 us (14%)
  starting transfers between devices  65.5 us (14%)
  other arithmetic  21.2 us (5%)
    pallas_call x30, Pallas kernels, on_chip(): pl.pallas_call(run, in_specs=[whole] * count + [pl.BlockSpec(memory_space...  186 us
    ppermute x27, waiting for transfers between devices, tensor_swap(): return lax.ppermute(x, 'tensor', [(i, i ^ bit) for i in range(size)])  63 us
    unnamed x142, local copies, waits for them, and re-layouts  45.8 us
    ppermute x34, starting transfers between devices, fsdp_swap(): return lax.ppermute(x, 'fsdp', [(i, i ^ bit) for i in range(size)])  38.6 us
    ppermute x34, waiting for transfers between devices, fsdp_swap(): return lax.ppermute(x, 'fsdp', [(i, i ^ bit) for i in range(size)])  29.5 us
    ppermute x27, starting transfers between devices, tensor_swap(): return lax.ppermute(x, 'tensor', [(i, i ^ bit) for i in range(size)])  26.9 us
    pallas_call x2, Pallas kernels, start(): pl.pallas_call(functools.partial(start_kernel, seq, turned), grid_spec=pl...  15.9 us
  transfers between devices with their start and end apart: 61, of which 21 were waited for; matrix products, arithmetic and copies ran while one was open for 9% of the time, Pallas kernels for 35%

profile of v3, /device:TPU:0, one launch (start us, length us, event | category | flops | bytes accessed | tf_op | source)
XLA Modules:
  0.0 466.2 jit_solution(14214638047164835356)
XLA Ops:
  11.7 3.0 collective-permute-start
  16.8 6.5 %collective-permute-done.refs_2_ = bf16[1,288,584]{2,1,0:T(8,128)(2,1)S(1)} collective-permute-done((bf16[1,288,584]{2,1,0:T(8,128)(2,1)S(1)}, bf16[1,288,584]{2,1,0:T(8,128)(2,1)S(1)}, u32[]{:S(2)}, u32[]{:S(2)}) %collective-permute-start) | collective-permute-done | bytes 336416 | tf_op jit(solution)/shard_map/ppermute | solution.py:57
  39.7 6.6 %copy.35.refs_0_ = bf16[4,729,1152]{2,1,0:T(8,128)(2,1)} copy(bf16[4,729,1152]{2,0,1:T(4,128)(2,1)} %param.14) | data formatting | bytes 13436928 | tf_op args[0]
  46.9 5.4 %shard_map.247.refs_0_.refs_1_.x_ref = bf16[768,1280]{1,0:T(8,128)(2,1)} custom-call(s32[1]{0:T(128)} %bitcast.pick_ref, s32[1,1280]{1,0:T(1,128)} %compare_select_fusion.source_ref, bf16[4,729,1152]{2,1,0:T(8,128)(2,1)} %copy.35.refs_0_, bf16[1,288,1078]{2,1,0:T(8,128)(2,1)} %shard_map.246.refs_1_.refs_4_), custom_call_target="tpu_custom_call" | custom-call | flops 2264924160 | bytes 5898240 | tf_op jit(solution)/shard_map/pallas_call | solution.py:540
  59.2 5.1 %collective-permute-done.6.refs_2_ = bf16[1,288,584]{2,1,0:T(8,128)(2,1)S(1)} collective-permute-done((bf16[1,288,584]{2,1,0:T(8,128)(2,1)}, bf16[1,288,584]{2,1,0:T(8,128)(2,1)S(1)}, u32[]{:S(2)}, u32[]{:S(2)}) %collective-permute-start.6) | collective-permute-done | bytes 336416 | tf_op jit(solution)/shard_map/ppermute | solution.py:62
  72.9 3.4 collective-permute-start.15
  76.3 6.6 %copy.36.refs_0_.refs_1_ = bf16[4,729,1152]{2,1,0:T(8,128)(2,1)} copy(bf16[4,729,1152]{2,0,1:T(4,128)(2,1)} %param.15) | data formatting | bytes 13436928 | tf_op args[1]
  83.4 5.6 %shard_map.248 = (bf16[768,1280]{1,0:T(8,128)(2,1)}, bf16[1280,768]{1,0:T(8,128)(2,1)}, f32[8,1280]{1,0:T(8,128)}) custom-call(bf16[768,1280]{1,0:T(8,128)(2,1)} %shard_map.247.refs_0_.refs_1_.x_ref, bf16[1,288,584]{2,1,0:T(8,128)(2,1)} %copy-done.32, bf16[1,288,584]{2,1,0:T(8,128)(2,1)} %copy-done.41, bf16[1,288,584]{2,1,0:T(8,128)(2,1)} %copy-done.42, ...), custom_call_target="tpu_custom_call" | custom-call | bytes 7284736 | tf_op jit(solution)/shard_map/pallas_call | solution.py:44
  89.0 6.4 %collective-permute-done.11.refs_1_.refs_2_ = bf16[3,288,584]{2,1,0:T(8,128)(2,1)S(1)} collective-permute-done((bf16[3,288,584]{2,1,0:T(8,128)(2,1)}, bf16[3,288,584]{2,1,0:T(8,128)(2,1)S(1)}, u32[]{:S(2)}, u32[]{:S(2)}) %collective-permute-start.11) | collective-permute-done | bytes 1009184 | tf_op jit(solution)/shard_map/ppermute | solution.py:57
  99.7 10.6 %shard_map.251 = (bf16[768,1280]{1,0:T(8,128)(2,1)}, bf16[768,1280]{1,0:T(8,128)(2,1)}, bf16[1280,768]{1,0:T(8,128)(2,1)}, bf16[1280,768]{1,0:T(8,128)(2,1)}) custom-call(s32[2]{0:T(128)} %pad_add_fusion.pick_ref, s32[1,1280]{1,0:T(1,128)} %compare_select_fusion.source_ref, bf16[4,729,1152]{2,1,0:T(8,128)(2,1)} %copy.36.refs_0_.refs_1_, ...), custom_call_target="tpu_custom_call" | custom-call | flops 4529848320 | bytes 11796480 | tf_op jit(solution)/shard_map/pallas_call | solution.py:540
  114.8 7.0 %shard_map.252 = (bf16[1280,576]{1,0:T(8,128)(2,1)}, bf16[432,768]{1,0:T(8,128)(2,1)}, bf16[768,144]{1,0:T(8,128)(2,1)}, f32[2,768]{1,0:T(2,128)}, bf16[2,768,640]{2,1,0:T(8,128)(2,1)}) custom-call(bf16[768,1280]{1,0:T(8,128)(2,1)} %get-tuple-element.99.refs_0_, bf16[1,288,584]{2,1,0:T(8,128)(2,1)} %copy-done.32, bf16[1,288,584]{2,1,0:T(8,128)(2,1)} %copy-done.41, ...), custom_call_target="tpu_custom_call" | custom-call | flops 2340421632 | bytes 7643136 | tf_op jit(solution)/shard_map/pallas_call | solution.py:44
  122.6 12.3 %shard_map.254 = (bf16[1280,576]{1,0:T(8,128)(2,1)}, bf16[432,768]{1,0:T(8,128)(2,1)}, bf16[768,144]{1,0:T(8,128)(2,1)}, f32[2,768]{1,0:T(2,128)}, bf16[1280,576...) custom-call(bf16[768,1280]{1,0:T(8,128)(2,1)} %get-tuple-element.99., ...), custom_call_target="tpu_custom_call" | custom-call | flops 4680843264 | bytes 14665728 | tf_op jit(solution)/shard_map/pallas_call | solution.py:44
  135.9 19.9 %shard_map.255 = (bf16[1280,576]{1,0:T(8,128)(2,1)}, bf16[432,768]{1,0:T(8,128)(2,1)}, bf16[768,144]{1,0:T(8,128)(2,1)}, f32[2,768]{1,0:T(2,128)}, bf16[2,768,640]{2,1,0:T(8,128)(2,1)}) custom-call(bf16[768,1280]{1,0:T(8,128)(2,1)} %get-tuple-element.99.refs_0_, bf16[3,288,584]{2,1,0:T(8,128)(2,1)} %shard_map.250.refs_1_, bf16[3,288,584]{2,1,0:T(8,128)(2,1)} %copy-done.28, ...), custom_call_target="tpu_custom_call" | custom-call | flops 2340421632 | bytes 12300288 | tf_op jit(solution)/shard_map/pallas_call | solution.py:44
  169.6 25.0 %shard_map.257 = (bf16[768,640]{1,0:T(8,128)(2,1)}, bf16[768,640]{1,0:T(8,128)(2,1)}, bf16[768,640]{1,0:T(8,128)(2,1)}, bf16[768,640]{1,0:T(8,128)(2,1)}, f32[2,...) custom-call(bf16[768,640]{1,0:T(8,128)(2,1)} %copy-done.27, bf16[768,640]{1,0:T(8,128)(2,1)} %copy-done.26, ...), custom_call_target="tpu_custom_call" | custom-call | flops 12693012480 | bytes 20311248 | tf_op jit(solution)/shard_map/pallas_call | solution.py:44
  196.9 2.8 collective-permute-done.24.refs_1_
  200.6 27.1 %shard_map.260 = (bf16[768,640]{1,0:T(8,128)(2,1)}, bf16[768,640]{1,0:T(8,128)(2,1)}, bf16[768,640]{1,0:T(8,128)(2,1)}, bf16[768,640]{1,0:T(8,128)(2,1)}, f32[2,...) custom-call(bf16[768,640]{1,0:T(8,128)(2,1)} %shard_map.259.refs_0_,, ...), custom_call_target="tpu_custom_call" | custom-call | flops 12693012480 | bytes 25273760 | tf_op jit(solution)/shard_map/pallas_call | solution.py:44
  239.5 18.7 %collective-permute-done.26 = bf16[768,640]{1,0:T(8,128)(2,1)S(1)} collective-permute-done((bf16[768,640]{1,0:T(8,128)(2,1)}, bf16[768,640]{1,0:T(8,128)(2,1)S(1)}, u32[]{:S(2)}, u32[]{:S(2)}) %collective-permute-start.26) | collective-permute-done | bytes 983072 | tf_op jit(solution)/shard_map/ppermute | solution.py:62
  262.3 5.0 %shard_map.262 = (f32[768,640]{1,0:T(8,128)S(1)}, bf16[768,1280]{1,0:T(8,128)(2,1)S(1)}, bf16[768,640]{1,0:T(8,128)(2,1)S(1)}, f32[4,640]{1,0:T(4,128)S(1)}) custom-call(bf16[768,640]{1,0:T(8,128)(2,1)S(1)} %add_convert_fusion.refs_0_, bf16[768,640]{1,0:T(8,128)(2,1)S(1)} %collective-permute-done.27.refs_1_, f32[768,1280]{1,0:T(8,128)} %copy-done.2, ...), custom_call_target="tpu_custom_call" | custom-call | bytes 14796800 | tf_op jit(solution)/shard_map/pallas_call | solution.py:438
  271.5 4.2 shard_map.263
  278.3 20.9 %shard_map.264 = (bf16[2,288,720]{2,1,0:T(8,128)(2,1)}, bf16[2,288,720]{2,1,0:T(8,128)(2,1)}, bf16[2,288,720]{2,1,0:T(8,128)(2,1)}, bf16[2,288,720]{2,1,0:T(8,12...) custom-call(bf16[1280,768]{1,0:T(8,128)(2,1)} %get-tuple-element.123.refs_0_, bf16[768,1280]{1,0:T(8,128)(2,1)} %copy-done.15, ...), custom_call_target="tpu_custom_call" | custom-call | flops 9437184000 | bytes 14392704 | tf_op jit(solution)/shard_map/pallas_call | solution.py:44
  301.4 3.1 shard_map.266.refs_6_
  304.4 11.2 %shard_map.267 = (bf16[1,288,432]{2,1,0:T(8,128)(2,1)}, bf16[1,288,432]{2,1,0:T(8,128)(2,1)}, bf16[1,288,432]{2,1,0:T(8,128)(2,1)}, bf16[1,288,432]{2,1,0:T(8,12...) custom-call(bf16[1280,768]{1,0:T(8,128)(2,1)} %get-tuple-element.123.refs_0_, bf16[768,1280]{1,0:T(8,128)(2,1)} %copy-done.15, ...), custom_call_target="tpu_custom_call" | custom-call | flops 4718592000 | bytes 11005632 | tf_op jit(solution)/shard_map/pallas_call | solution.py:44
  318.7 3.4 collective-permute-done.37.refs_2_
  323.3 3.3 shard_map.268
  331.5 3.3 shard_map.265
  335.8 4.6 collective-permute-start.32
  341.1 11.2 %shard_map.269 = (bf16[1,288,432]{2,1,0:T(8,128)(2,1)}, bf16[1,288,432]{2,1,0:T(8,128)(2,1)}, bf16[1,288,432]{2,1,0:T(8,128)(2,1)}, bf16[1,288,432]{2,1,0:T(8,12...) custom-call(bf16[1280,768]{1,0:T(8,128)(2,1)} %get-tuple-element.123.refs_0_, bf16[768,1280]{1,0:T(8,128)(2,1)} %copy-done.15, ...), custom_call_target="tpu_custom_call" | custom-call | flops 4718592000 | bytes 11005632 | tf_op jit(solution)/shard_map/pallas_call | solution.py:44
  357.6 13.4 %collective-permute-done.33.refs_7_ = bf16[144,768]{1,0:T(8,128)(2,1)S(1)} collective-permute-done((bf16[144,768]{1,0:T(8,128)(2,1)S(1)}, bf16[144,768]{1,0:T(8,128)(2,1)S(1)}, u32[]{:S(2)}, u32[]{:S(2)}) %collective-permute-start.33) | collective-permute-done | bytes 221216 | tf_op jit(solution)/shard_map/ppermute | solution.py:62
  375.9 8.4 %collective-permute-done.60 = bf16[288,1076]{1,0:T(8,128)(2,1)} collective-permute-done((bf16[288,1076]{1,0:T(8,128)(2,1)}, bf16[288,1076]{1,0:T(8,128)(2,1)}, u32[]{:S(2)}, u32[]{:S(2)}) %collective-permute-start.60) | collective-permute-done | bytes 619808 | tf_op jit(solution)/shard_map/ppermute | solution.py:62
  397.3 5.1 %shard_map.271 = (bf16[576,768]{1,0:T(8,128)(2,1)S(1)}, f32[2,640]{1,0:T(2,128)S(1)}) custom-call(bf16[2,768,640]{2,1,0:T(8,128)(2,1)S(1)} %copy-done.1, bf16[2,768,640]{2,1,0:T(8,128)(2,1)} %collective-permute-done.39.other_ref, bf16[768,1280]{1,0:T(8,128)(2,1)S(1)} %copy-done, f32[768,640]{1,0:T(8,128)S(1)} %copy-done.17, ...), custom_call_target="tpu_custom_call" | custom-call | flops 566231040 | bytes 5898240 | tf_op jit(solution)/shard_map/pallas_call | solution.py:925
  415.0 3.7 collective-permute-done.56.refs_1_
  442.8 6.1 %collective-permute-done.44.refs_5_ = bf16[144,768]{1,0:T(8,128)(2,1)S(1)} collective-permute-done((bf16[144,768]{1,0:T(8,128)(2,1)S(1)}, bf16[144,768]{1,0:T(8,128)(2,1)S(1)}, u32[]{:S(2)}, u32[]{:S(2)}) %collective-permute-start.44) | collective-permute-done | bytes 221216 | tf_op jit(solution)/shard_map/ppermute | solution.py:62
  (341 shorter events, 185.7 us)
Async XLA Ops:
  33.5 21.8 %collective-permute-start.9 = (bf16[1,288,1078]{2,1,0:T(8,128)(2,1)}, bf16[1,288,1078]{2,1,0:T(8,128)(2,1)S(1)}, u32[]{:S(2)}, u32[]{:S(2)}) collective-permute-start(bf16[1,288,1078]{2,1,0:T(8,128)(2,1)} %shard_map.246.refs_1_.refs_4_), channel_id=1, source_target_pairs={{0,16},{8,24},{16,0},{24,8},{1,17},{9,25},{17,1},{25,9},{2,18},{10... | collective-permute-start | bytes 1862792 | tf_op jit(solution)/shard_map/ppermute | solution.py:57
  34.6 22.8 %collective-permute-start.7 = (bf16[1,288,1078]{2,1,0:T(8,128)(2,1)}, bf16[1,288,1078]{2,1,0:T(8,128)(2,1)S(1)}, u32[]{:S(2)}, u32[]{:S(2)}) collective-permute-start(bf16[1,288,1078]{2,1,0:T(8,128)(2,1)} %shard_map.246.refs_1_.refs_4_), channel_id=1, source_target_pairs={{0,8},{8,0},{16,24},{24,16},{1,9},{9,1},{17,25},{25,17},{2,10},{10... | collective-permute-start | bytes 1862792 | tf_op jit(solution)/shard_map/ppermute | solution.py:57
  70.4 25.0 %collective-permute-start.11 = (bf16[3,288,584]{2,1,0:T(8,128)(2,1)}, bf16[3,288,584]{2,1,0:T(8,128)(2,1)S(1)}, u32[]{:S(2)}, u32[]{:S(2)}) collective-permute-start(bf16[3,288,584]{2,1,0:T(8,128)(2,1)} %shard_map.250.refs_1_), channel_id=1, source_target_pairs={{0,8},{8,0},{16,24},{24,16},{1,9},{9,1},{17,25},{25,17},{2,10},{10... | collective-permute-start | bytes 3027464 | tf_op jit(solution)/shard_map/ppermute | solution.py:57
  71.4 25.9 %collective-permute-start.12 = (bf16[3,288,584]{2,1,0:T(8,128)(2,1)}, bf16[3,288,584]{2,1,0:T(8,128)(2,1)S(1)}, u32[]{:S(2)}, u32[]{:S(2)}) collective-permute-start(bf16[3,288,584]{2,1,0:T(8,128)(2,1)} %shard_map.250.refs_1_), channel_id=1, source_target_pairs={{0,16},{8,24},{16,0},{24,8},{1,17},{9,25},{17,1},{25,9},{2,18},{10... | collective-permute-start | bytes 3027464 | tf_op jit(solution)/shard_map/ppermute | solution.py:57
  72.9 37.4 %collective-permute-start.15 = (bf16[1,288,1078]{2,1,0:T(8,128)(2,1)S(1)}, bf16[1,288,1078]{2,1,0:T(8,128)(2,1)S(1)}, u32[]{:S(2)}, u32[]{:S(2)}) collective-permute-start(bf16[1,288,1078]{2,1,0:T(8,128)(2,1)S(1)} %copy-done.31), channel_id=1, source_target_pairs={{0,4},{1,5},{2,6},{3,7},{4,0},{5,1},{6,2},{7,3},{8,12},{9,13},{10,... | collective-permute-start | bytes 1862792 | tf_op jit(solution)/shard_map/ppermute | solution.py:62
  96.4 25.4 %collective-permute-start.13 = (bf16[3,144,584]{2,1,0:T(8,128)(2,1)}, bf16[3,144,584]{2,1,0:T(8,128)(2,1)S(1)}, u32[]{:S(2)}, u32[]{:S(2)}) collective-permute-start(bf16[3,144,584]{2,1,0:T(8,128)(2,1)} %slice.238), channel_id=1, source_target_pairs={{0,16},{8,24},{16,0},{24,8},{1,17},{9,25},{17,1},{25,9},{2,18},{10... | collective-permute-start | bytes 1513736 | tf_op jit(solution)/shard_map/ppermute | solution.py:57
  98.3 23.5 %collective-permute-start.14 = (bf16[3,144,584]{2,1,0:T(8,128)(2,1)}, bf16[3,144,584]{2,1,0:T(8,128)(2,1)}, u32[]{:S(2)}, u32[]{:S(2)}) collective-permute-start(bf16[3,144,584]{2,1,0:T(8,128)(2,1)} %slice.239), channel_id=1, source_target_pairs={{0,8},{8,0},{16,24},{24,16},{1,9},{9,1},{17,25},{25,17},{2,10},{10... | collective-permute-start | bytes 1513736 | tf_op jit(solution)/shard_map/ppermute | solution.py:57
  113.2 21.7 %collective-permute-start.16 = (bf16[1,288,1078]{2,1,0:T(8,128)(2,1)}, bf16[1,288,1078]{2,1,0:T(8,128)(2,1)S(1)}, u32[]{:S(2)}, u32[]{:S(2)}) collective-permute-start(bf16[1,288,1078]{2,1,0:T(8,128)(2,1)} %shard_map.253.refs_7_.refs_9_), channel_id=1, source_target_pairs={{0,8},{8,0},{16,24},{24,16},{1,9},{9,1},{17,25},{25,17},{2,10},{10... | collective-permute-start | bytes 1862792 | tf_op jit(solution)/shard_map/ppermute | solution.py:57
  167.5 27.2 %collective-permute-start.23 = (bf16[768,640]{1,0:T(8,128)(2,1)S(1)}, bf16[768,640]{1,0:T(8,128)(2,1)}, u32[]{:S(2)}, u32[]{:S(2)}) collective-permute-start(bf16[768,640]{1,0:T(8,128)(2,1)S(1)} %get-tuple-element.105.refs_0_), channel_id=1, source_target_pairs={{0,2},{1,3},{2,0},{3,1},{4,6},{5,7},{6,4},{7,5},{8,10},{9,11},{10,... | collective-permute-start | bytes 2949128 | tf_op jit(solution)/shard_map/ppermute | solution.py:62
  234.2 24.0 %collective-permute-start.26 = (bf16[768,640]{1,0:T(8,128)(2,1)}, bf16[768,640]{1,0:T(8,128)(2,1)S(1)}, u32[]{:S(2)}, u32[]{:S(2)}) collective-permute-start(bf16[768,640]{1,0:T(8,128)(2,1)} %shard_map.261), channel_id=1, source_target_pairs={{0,2},{1,3},{2,0},{3,1},{4,6},{5,7},{6,4},{7,5},{8,10},{9,11},{10,... | collective-permute-start | bytes 2949128 | tf_op jit(solution)/shard_map/ppermute | solution.py:62
  237.6 23.0 %collective-permute-start.28 = (bf16[768,640]{1,0:T(8,128)(2,1)}, bf16[768,640]{1,0:T(8,128)(2,1)S(1)}, u32[]{:S(2)}, u32[]{:S(2)}) collective-permute-start(bf16[768,640]{1,0:T(8,128)(2,1)} %get-tuple-element.121), channel_id=1, source_target_pairs={{0,1},{1,0},{2,3},{3,2},{4,5},{5,4},{6,7},{7,6},{8,9},{9,8},{10,11... | collective-permute-start | bytes 2949128 | tf_op jit(solution)/shard_map/ppermute | solution.py:62
  237.6 33.9 %collective-permute-start.30 = (bf16[2,288,1076]{2,1,0:T(8,128)(2,1)}, bf16[2,288,1076]{2,1,0:T(8,128)(2,1)}, u32[]{:S(2)}, u32[]{:S(2)}) collective-permute-start(bf16[2,288,1076]{2,1,0:T(8,128)(2,1)} %get-tuple-element.137), channel_id=1, source_target_pairs={{0,8},{8,0},{16,24},{24,16},{1,9},{9,1},{17,25},{25,17},{2,10},{10... | collective-permute-start | bytes 3718664 | tf_op jit(solution)/shard_map/ppermute | solution.py:57
  238.5 32.9 %collective-permute-start.31 = (bf16[2,288,1076]{2,1,0:T(8,128)(2,1)}, bf16[2,288,1076]{2,1,0:T(8,128)(2,1)}, u32[]{:S(2)}, u32[]{:S(2)}) collective-permute-start(bf16[2,288,1076]{2,1,0:T(8,128)(2,1)} %get-tuple-element.138), channel_id=1, source_target_pairs={{0,16},{8,24},{16,0},{24,8},{1,17},{9,25},{17,1},{25,9},{2,18},{10... | collective-permute-start | bytes 3718664 | tf_op jit(solution)/shard_map/ppermute | solution.py:57
  260.1 66.6 %collective-permute-start.21 = (bf16[768,640]{1,0:T(8,128)(2,1)}, bf16[768,640]{1,0:T(8,128)(2,1)}, u32[]{:S(2)}, u32[]{:S(2)}) collective-permute-start(bf16[768,640]{1,0:T(8,128)(2,1)} %get-tuple-element.109), channel_id=1, source_target_pairs={{0,1},{1,0},{2,3},{3,2},{4,5},{5,4},{6,7},{7,6},{8,9},{9,8},{10,11... | collective-permute-start | bytes 2949128 | tf_op jit(solution)/shard_map/ppermute | solution.py:62
  275.7 24.3 %collective-permute-start.35 = (bf16[2,144,1076]{2,1,0:T(8,128)(2,1)}, bf16[2,144,1076]{2,1,0:T(8,128)(2,1)}, u32[]{:S(2)}, u32[]{:S(2)}) collective-permute-start(bf16[2,144,1076]{2,1,0:T(8,128)(2,1)} %get-tuple-element.139.refs_12_), channel_id=1, source_target_pairs={{0,16},{8,24},{16,0},{24,8},{1,17},{9,25},{17,1},{25,9},{2,18},{10... | collective-permute-start | bytes 1859336 | tf_op jit(solution)/shard_map/ppermute | solution.py:57
  276.7 24.7 %collective-permute-start.36 = (bf16[2,144,1076]{2,1,0:T(8,128)(2,1)}, bf16[2,144,1076]{2,1,0:T(8,128)(2,1)}, u32[]{:S(2)}, u32[]{:S(2)}) collective-permute-start(bf16[2,144,1076]{2,1,0:T(8,128)(2,1)} %get-tuple-element.149), channel_id=1, source_target_pairs={{0,8},{8,0},{16,24},{24,16},{1,9},{9,1},{17,25},{25,17},{2,10},{10... | collective-permute-start | bytes 1859336 | tf_op jit(solution)/shard_map/ppermute | solution.py:57
  277.7 48.9 %collective-permute-start.29 = (bf16[768,640]{1,0:T(8,128)(2,1)}, bf16[768,640]{1,0:T(8,128)(2,1)}, u32[]{:S(2)}, u32[]{:S(2)}) collective-permute-start(bf16[768,640]{1,0:T(8,128)(2,1)} %copy-done.25), channel_id=1, source_target_pairs={{0,2},{1,3},{2,0},{3,1},{4,6},{5,7},{6,4},{7,5},{8,10},{9,11},{10,... | collective-permute-start | bytes 2949128 | tf_op jit(solution)/shard_map/ppermute | solution.py:62
  299.2 22.9 %collective-permute-start.37 = (bf16[2,288,720]{2,1,0:T(8,128)(2,1)}, bf16[2,288,720]{2,1,0:T(8,128)(2,1)}, u32[]{:S(2)}, u32[]{:S(2)}) collective-permute-start(bf16[2,288,720]{2,1,0:T(8,128)(2,1)} %get-tuple-element.153), channel_id=1, source_target_pairs={{0,8},{8,0},{16,24},{24,16},{1,9},{9,1},{17,25},{25,17},{2,10},{10... | collective-permute-start | bytes 2488328 | tf_op jit(solution)/shard_map/ppermute | solution.py:57
  300.0 23.4 %collective-permute-start.38 = (bf16[2,288,720]{2,1,0:T(8,128)(2,1)}, bf16[2,288,720]{2,1,0:T(8,128)(2,1)}, u32[]{:S(2)}, u32[]{:S(2)}) collective-permute-start(bf16[2,288,720]{2,1,0:T(8,128)(2,1)} %get-tuple-element.154), channel_id=1, source_target_pairs={{0,16},{8,24},{16,0},{24,8},{1,17},{9,25},{17,1},{25,9},{2,18},{10... | collective-permute-start | bytes 2488328 | tf_op jit(solution)/shard_map/ppermute | solution.py:57
  315.7 36.6 %collective-permute-start.50 = (bf16[1,288,432]{2,1,0:T(8,128)(2,1)}, bf16[1,288,432]{2,1,0:T(8,128)(2,1)S(1)}, u32[]{:S(2)}, u32[]{:S(2)}) collective-permute-start(bf16[1,288,432]{2,1,0:T(8,128)(2,1)} %get-tuple-element.172), channel_id=1, source_target_pairs={{0,8},{8,0},{16,24},{24,16},{1,9},{9,1},{17,25},{25,17},{2,10},{10... | collective-permute-start | bytes 746504 | tf_op jit(solution)/shard_map/ppermute | solution.py:57
  322.2 32.5 %collective-permute-start.51 = (bf16[1,288,432]{2,1,0:T(8,128)(2,1)}, bf16[1,288,432]{2,1,0:T(8,128)(2,1)S(1)}, u32[]{:S(2)}, u32[]{:S(2)}) collective-permute-start(bf16[1,288,432]{2,1,0:T(8,128)(2,1)} %get-tuple-element.173), channel_id=1, source_target_pairs={{0,16},{8,24},{16,0},{24,8},{1,17},{9,25},{17,1},{25,9},{2,18},{10... | collective-permute-start | bytes 746504 | tf_op jit(solution)/shard_map/ppermute | solution.py:57
  335.8 21.7 %collective-permute-start.32 = (bf16[144,768]{1,0:T(8,128)(2,1)S(1)}, bf16[144,768]{1,0:T(8,128)(2,1)S(1)}, u32[]{:S(2)}, u32[]{:S(2)}) collective-permute-start(bf16[144,768]{1,0:T(8,128)(2,1)S(1)} %get-tuple-element.225), channel_id=1, source_target_pairs={{0,6},{1,7},{2,4},{3,5},{4,2},{5,3},{6,0},{7,1},{8,14},{9,15},{10,... | collective-permute-start | bytes 663560 | tf_op jit(solution)/shard_map/ppermute | solution.py:62
  340.4 30.6 %collective-permute-start.33 = (bf16[144,768]{1,0:T(8,128)(2,1)S(1)}, bf16[144,768]{1,0:T(8,128)(2,1)S(1)}, u32[]{:S(2)}, u32[]{:S(2)}) collective-permute-start(bf16[144,768]{1,0:T(8,128)(2,1)S(1)} %get-tuple-element.224), channel_id=1, source_target_pairs={{0,4},{1,5},{2,6},{3,7},{4,0},{5,1},{6,2},{7,3},{8,12},{9,13},{10,... | collective-permute-start | bytes 663560 | tf_op jit(solution)/shard_map/ppermute | solution.py:62
  340.4 31.1 %collective-permute-start.34 = (bf16[144,768]{1,0:T(8,128)(2,1)S(1)}, bf16[144,768]{1,0:T(8,128)(2,1)S(1)}, u32[]{:S(2)}, u32[]{:S(2)}) collective-permute-start(bf16[144,768]{1,0:T(8,128)(2,1)S(1)} %get-tuple-element.223), channel_id=1, source_target_pairs={{0,2},{1,3},{2,0},{3,1},{4,6},{5,7},{6,4},{7,5},{8,10},{9,11},{10,... | collective-permute-start | bytes 663560 | tf_op jit(solution)/shard_map/ppermute | solution.py:62
  352.3 32.0 %collective-permute-start.60 = (bf16[288,1076]{1,0:T(8,128)(2,1)}, bf16[288,1076]{1,0:T(8,128)(2,1)}, u32[]{:S(2)}, u32[]{:S(2)}) collective-permute-start(bf16[288,1076]{1,0:T(8,128)(2,1)} %slice_bitcast_fusion), channel_id=1, source_target_pairs={{0,4},{1,5},{2,6},{3,7},{4,0},{5,1},{6,2},{7,3},{8,12},{9,13},{10,... | collective-permute-start | bytes 1859336 | tf_op jit(solution)/shard_map/ppermute | solution.py:62
  354.7 32.6 %collective-permute-start.40 = (bf16[2,144,720]{2,1,0:T(8,128)(2,1)}, bf16[2,144,720]{2,1,0:T(8,128)(2,1)}, u32[]{:S(2)}, u32[]{:S(2)}) collective-permute-start(bf16[2,144,720]{2,1,0:T(8,128)(2,1)} %get-tuple-element.155.refs_6_), channel_id=1, source_target_pairs={{0,16},{8,24},{16,0},{24,8},{1,17},{9,25},{17,1},{25,9},{2,18},{10... | collective-permute-start | bytes 1244168 | tf_op jit(solution)/shard_map/ppermute | solution.py:57
  357.5 35.6 %collective-permute-start.39 = (bf16[2,768,640]{2,1,0:T(8,128)(2,1)}, bf16[2,768,640]{2,1,0:T(8,128)(2,1)}, u32[]{:S(2)}, u32[]{:S(2)}) collective-permute-start(bf16[2,768,640]{2,1,0:T(8,128)(2,1)} %get-tuple-element.156.refs_4_.own_ref), channel_id=1, source_target_pairs={{0,1},{1,0},{2,3},{3,2},{4,5},{5,4},{6,7},{7,6},{8,9},{9,8},{10,11... | collective-permute-start | bytes 5898248 | tf_op jit(solution)/shard_map/ppermute | solution.py:62
  371.5 79.1 %collective-permute-start.45 = (bf16[1,288,432]{2,1,0:T(8,128)(2,1)}, bf16[1,288,432]{2,1,0:T(8,128)(2,1)}, u32[]{:S(2)}, u32[]{:S(2)}) collective-permute-start(bf16[1,288,432]{2,1,0:T(8,128)(2,1)} %get-tuple-element.164), channel_id=1, source_target_pairs={{0,8},{8,0},{16,24},{24,16},{1,9},{9,1},{17,25},{25,17},{2,10},{10... | collective-permute-start | bytes 746504 | tf_op jit(solution)/shard_map/ppermute | solution.py:57
  384.3 37.4 %collective-permute-start.52 = (bf16[1,144,432]{2,1,0:T(8,128)(2,1)}, bf16[1,144,432]{2,1,0:T(8,128)(2,1)S(1)}, u32[]{:S(2)}, u32[]{:S(2)}) collective-permute-start(bf16[1,144,432]{2,1,0:T(8,128)(2,1)} %get-tuple-element.176), channel_id=1, source_target_pairs={{0,16},{8,24},{16,0},{24,8},{1,17},{9,25},{17,1},{25,9},{2,18},{10... | collective-permute-start | bytes 373256 | tf_op jit(solution)/shard_map/ppermute | solution.py:57
  387.3 35.9 %collective-permute-start.53 = (bf16[1,144,432]{2,1,0:T(8,128)(2,1)}, bf16[1,144,432]{2,1,0:T(8,128)(2,1)S(1)}, u32[]{:S(2)}, u32[]{:S(2)}) collective-permute-start(bf16[1,144,432]{2,1,0:T(8,128)(2,1)} %get-tuple-element.177), channel_id=1, source_target_pairs={{0,8},{8,0},{16,24},{24,16},{1,9},{9,1},{17,25},{25,17},{2,10},{10... | collective-permute-start | bytes 373256 | tf_op jit(solution)/shard_map/ppermute | solution.py:57
  393.1 35.4 %collective-permute-start.49 = (bf16[2,288,576]{2,1,0:T(8,128)(2,1)}, bf16[2,288,576]{2,1,0:T(8,128)(2,1)}, u32[]{:S(2)}, u32[]{:S(2)}) collective-permute-start(bf16[2,288,576]{2,1,0:T(8,128)(2,1)} %slice.262), channel_id=1, source_target_pairs={{0,2},{1,3},{2,0},{3,1},{4,6},{5,7},{6,4},{7,5},{8,10},{9,11},{10,... | collective-permute-start | bytes 1990664 | tf_op jit(solution)/shard_map/ppermute | solution.py:62
  421.7 29.0 %collective-permute-start.46 = (bf16[1,288,432]{2,1,0:T(8,128)(2,1)}, bf16[1,288,432]{2,1,0:T(8,128)(2,1)S(1)}, u32[]{:S(2)}, u32[]{:S(2)}) collective-permute-start(bf16[1,288,432]{2,1,0:T(8,128)(2,1)} %get-tuple-element.165), channel_id=1, source_target_pairs={{0,16},{8,24},{16,0},{24,8},{1,17},{9,25},{17,1},{25,9},{2,18},{10... | collective-permute-start | bytes 746504 | tf_op jit(solution)/shard_map/ppermute | solution.py:57
  (99 other events, 718.6 us)
